TPU v7x, 32 devices: a whole 2x2x4 slice. The times are simulated.
32 devices in a mesh: pts: 4 (over y, core), cen: 8 (over z, x).
Axes of the slice: x: 2, y: 2, z: 4, core: 2. Of those that a mesh axis runs over, the one named last changes fastest.
Arguments:
- points: bfloat16 [16384, 1024], P('pts'), may hold values from -128 to 128
- centroids: float32 [8192, 1024], P('cen'), may hold values from -10 to 10
Outputs:
- centroid_means: float32 [8192, 1024], P('cen', 'pts')
- log_norms: float32 [16384], P('pts')
All inputs are finite; a program needn't handle non-finite values.
Results may differ from a plain program's by a relative error of at most 0.0015.
The roundings to bfloat16 on the way count: a program that leaves them out, or rounds other values in their place, can miss the bound.
Values may be sent and summed in bfloat16 or wider, within the bound.
No kernel may reach another device: no remote copies, remote signals or barrier semaphores. Data moves between devices by JAX's collectives and lax.ppermute only.
A program may use at most 64 MiB of HBM per device.

v0:
```python
import functools

import jax
import jax.numpy as jnp
from jax import lax
from jax.experimental import pallas as pl
from jax.experimental.pallas import tpu as pltpu
from jax.sharding import PartitionSpec as P

ITERS = 2
F32 = jnp.float32
BF16 = jnp.bfloat16
SCORE_VMEM = 34
WEIGH_VMEM = 34
KEPT_VMEM = 20
CHUNK_LINES = 2
WEIGH_SLOTS = 2
LEVELS = 30000.0
LOWEST = -117.0


def divisor(total, wanted):
    size = min(total, wanted)
    while total % size:
        size -= 1
    return size


def round_up(value, unit):
    return -(-value // unit) * unit


def normalize_rows(rows):
    return rows * lax.rsqrt(jnp.sum(rows * rows, axis=1, keepdims=True) + 1e-06)


CORES = 2


def place():
    me = lax.axis_index("pts")
    return lax.div(me, CORES), lax.rem(me, CORES)


def params(mebibytes):
    return pltpu.CompilerParams(vmem_limit_bytes=mebibytes * 2**20)


VMEM = pl.BlockSpec(memory_space=pltpu.VMEM)
ANY = pl.BlockSpec(memory_space=pl.ANY)


def merge(sets):
    top = functools.reduce(jnp.maximum, [stats[0] for stats in sets])
    return top, functools.reduce(jnp.add, [stats[1] * jnp.exp(stats[0] - top) for stats in sets])


def to_column(row, height):
    return jnp.broadcast_to(row, (128, height)).T


def encode(values, scale):
    steps = jnp.floor(jnp.abs(values) * (LEVELS / scale) + 0.5)
    power = jnp.floor(steps * (1.0 / 128.0))
    size = (1.0 + (steps * (1.0 / 128.0) - power)) * jnp.exp2(power + LOWEST)
    return jnp.where(values < 0.0, -size, size).astype(BF16)


def decode(codes, scale):
    wide = codes.astype(F32)
    size = jnp.abs(wide)
    power = jnp.floor(jnp.log2(size))
    steps = 128.0 * (power - LOWEST + (size * jnp.exp2(-power) - 1.0))
    return jnp.where(wide < 0.0, -steps, steps) * (scale * (1.0 / LEVELS))


def score_points(raw, units, x_ref, e_parts, stat_ref, stage, semaphores):
    line = stat_ref.shape[2]
    lines = stage.shape[0]
    sub = divisor(line, 256)

    def copies(number, slot):
        columns = pl.ds(pl.multiple_of(number * line, line), line)
        return [
            pltpu.make_async_copy(stage.at[slot, rows, :], target(columns), semaphores.at[slot, part])
            for part, (rows, target) in enumerate(e_parts)
        ]

    def visit(step, carry):
        for slot in range(lines):
            number = step * lines + slot

            @pl.when(step > 0)
            def _():
                for copy in copies(number - lines, slot):
                    copy.wait()

            tops, totals = [], []
            for offset in range(0, line, sub):
                logits = lax.dot_general(
                    units[...],
                    x_ref[pl.ds(pl.multiple_of(number * line + offset, sub), sub), :],
                    (((1,), (1,)), ((), ())),
                    preferred_element_type=F32,
                )
                top = jnp.max(logits, axis=0, keepdims=True)
                shifted = jnp.exp(logits - top)
                stage[slot, :, offset : offset + sub] = logits if raw else shifted
                tops.append(top)
                totals.append(jnp.sum(shifted, axis=0, keepdims=True))
            stat_ref[0, pl.ds(number, 1), :] = jnp.concatenate(tops, axis=1)
            stat_ref[1, pl.ds(number, 1), :] = jnp.concatenate(totals, axis=1)
            for copy in copies(number, slot):
                copy.start()
        return carry

    steps = stat_ref.shape[1] // lines
    lax.fori_loop(0, steps, visit, 0)
    for slot in range(lines):
        for copy in copies((steps - 1) * lines + slot, slot):
            copy.wait()


def stat_shape(total):
    line = divisor(total, 512)
    return (2, total // line, line)


def first_scores_body(raw, units, x_ref, _, e_hbm, stat_ref, stage, semaphores):
    target = [(slice(None), lambda columns: e_hbm.at[:, columns])]
    score_points(raw, units, x_ref, target, stat_ref, stage, semaphores)


def next_scores_body(raw, count, away, *refs):
    unit_refs = refs[:count]
    x_ref = refs[count]
    e_hbm, stat_ref, units, stage, semaphores = refs[-5:]
    rows = unit_refs[0].shape[0]
    pair = CORES * rows
    chip, core = place()
    chips = e_hbm.shape[0] // pair
    for number, ref in enumerate(unit_refs):
        of_pair = core if number % CORES == 0 else 1 - core
        start = pl.multiple_of((number - number % CORES + of_pair) * rows, rows)
        units[pl.ds(start, rows), :] = ref[...]

    def target_of(number):
        start = pl.multiple_of(lax.rem(chip + away + number, chips) * pair, pair)
        return lambda columns: e_hbm.at[pl.ds(start, pair), columns]

    targets = [
        (slice(number * pair, (number + 1) * pair), target_of(number)) for number in range(count // CORES)
    ]
    score_points(raw, units, x_ref, targets, stat_ref, stage, semaphores)


def scores(raw, blocks, points, away=None, shifted=None):
    total, width = points.shape
    count = len(blocks)
    rows = sum(block.shape[0] for block in blocks)
    all_rows = rows if shifted is None else shifted.shape[0]
    stat = stat_shape(total)
    parts = 1 if away is None else count // CORES
    more = [] if shifted is None or away == 0 else [shifted]
    scratch = [
        pltpu.VMEM((divisor(stat[1], 2), rows, stat[2]), F32),
        pltpu.SemaphoreType.DMA((divisor(stat[1], 2), parts)),
    ]
    if away is not None:
        scratch = [pltpu.VMEM((rows, width), BF16)] + scratch
    if away is None:
        body = functools.partial(first_scores_body, raw)
    else:
        body = functools.partial(next_scores_body, raw, count, away)
    return pl.pallas_call(
        body,
        in_specs=[VMEM] * (count + 1) + [ANY] * len(more),
        out_specs=[VMEM, ANY, VMEM],
        out_shape=[
            jax.ShapeDtypeStruct(points.shape, BF16),
            jax.ShapeDtypeStruct((all_rows, total), F32),
            jax.ShapeDtypeStruct(stat, F32),
        ],
        input_output_aliases={count + number: number for number in range(1 + len(more))},
        scratch_shapes=scratch,
        compiler_params=params(SCORE_VMEM),
        cost_estimate=pl.CostEstimate(
            flops=2 * rows * total * width,
            bytes_accessed=2 * total * width + 4 * rows * total,
            transcendentals=rows * total,
        ),
    )(*blocks, points, *more)


FAR, THEIRS, OWN = range(3)


def weigh_body(by_rows, n_sets, n_tops, kind, others, extra, pair, *refs):
    parts = CORES if kind == FAR else 1
    stat_refs, refs = refs[:n_sets], refs[n_sets:]
    top_refs, (e_hbm, x_ref, _), refs = refs[:n_tops], refs[n_tops : n_tops + 3], refs[n_tops + 3 :]
    out_refs, refs = refs[:parts], refs[parts + 1 :]
    if not by_rows:
        (kept_ref, kept_mass_ref), refs = refs[:2], refs[2:]
    scale_refs, refs = refs[:2], refs[2:]
    n_weights = 2 if by_rows else 0
    weights_refs, (stage, mass_ref, sum_ref, semaphores) = refs[:n_weights], refs[n_weights:]
    chip, core = place()
    line = stat_refs[0].shape[2]
    total = x_ref.shape[0]
    height, span = sum_ref.shape
    slots, _, chunk = stage.shape
    steps = total // chunk
    lanes = min(line, 128)

    def block_of(other):
        if kind == FAR:
            return lax.rem(chip + 1 + other, others + 1)
        return chip * CORES + (core if kind == OWN else 1 - core)

    def copy_of(number):
        other, step = divmod(number, steps)
        rows = pl.ds(pl.multiple_of(block_of(other) * height, height), height) if by_rows else slice(None)
        columns = slice(step * chunk, (step + 1) * chunk)
        slot = number % slots
        return pltpu.make_async_copy(e_hbm.at[rows, columns], stage.at[slot], semaphores.at[slot])

    for number in range(min(slots, others * steps)):
        copy_of(number).start()
    top, all_total = merge(stat_refs)
    if by_rows:
        scale_refs[0][...] = top
        scale_refs[1][...] = 1.0 / all_total
    else:
        for ref, scale_ref in zip((top_refs[0], top_refs[-1]), scale_refs):
            scale_ref[...] = jnp.exp(ref[0] - top) / all_total

    def weights_of(values, group, number):
        one, two = (ref[number : number + 1, :] for ref in scale_refs)
        if by_rows:
            return jnp.exp(values - one) * two
        return values * jnp.where(chip == group, one, two)

    group_rows = height if by_rows else pair
    kept = not by_rows

    def weights_part(step):
        columns = slice(step * chunk, (step + 1) * chunk)
        return kept_ref.at[:, columns] if kept else weights_refs[step % 2]

    def weigh_step(number):
        step = number % steps
        weights_ref = weights_part(step)
        for group in range(height // group_rows):
            rows = slice(group * group_rows, (group + 1) * group_rows)
            mass = None
            for offset in range(0, chunk, line):
                values = stage[number % slots, rows, offset : offset + line]
                weights = weights_of(values, group, (step * chunk + offset) // line).astype(BF16)
                weights_ref[rows, offset : offset + line] = weights
                wide = weights.astype(F32)
                for lane in range(0, line, lanes):
                    piece = wide[:, lane : lane + lanes]
                    mass = piece if mass is None else mass + piece
            mass_ref[rows, :] = mass if step == 0 else mass_ref[rows, :] + mass

    weighed = steps if kept else others * steps
    for number in range(others * steps):
        other, step = divmod(number, steps)
        if number < weighed:
            copy_of(number).wait()
            weigh_step(number)
        if number + slots < weighed:
            copy_of(number + slots).start()
        columns = slice(None)
        if not by_rows:
            columns = pl.ds(pl.multiple_of(block_of(other) * span, span), span)
        product = jnp.dot(
            weights_part(step)[...],
            x_ref[step * chunk : (step + 1) * chunk, columns],
            preferred_element_type=F32,
        )
        sum_ref[...] = product if step == 0 else sum_ref[...] + product
        if step == steps - 1:
            mass = jnp.sum(mass_ref[...].T, axis=0, keepdims=True)
            if kept:
                kept_mass_ref[...] = mass
            write_sums(by_rows, other, core, out_refs, sum_ref, mass, extra)


def write_sums(by_rows, other, core, out_refs, sum_ref, mass, extra):
    parts = len(out_refs)
    rows = out_refs[0].shape[1] - extra
    width = out_refs[0].shape[2]
    for part, ref in enumerate(out_refs):
        side = lax.rem(core + part, parts)
        ref[other, rows:, :] = jnp.zeros((extra, width), F32)
        if by_rows:
            found = mass
            if parts > 1:
                found = jnp.where(side == 0, mass[:, :rows], mass[:, rows:])
                ref[other, :rows, :] = sum_ref[pl.ds(pl.multiple_of(side * rows, rows), rows), :]
            else:
                ref[other, :rows, :] = sum_ref[...]
            ref[other, rows : rows + 1, :rows] = found
        else:
            sums = sum_ref[...]
            if parts > 1:
                sums = jnp.where(side == 0, sums[:, :width], sums[:, width:])
            ref[other, :rows, :] = sums
            for number in range(rows // width):
                ref[other, rows + number : rows + number + 1, :] = mass[
                    :, number * width : (number + 1) * width
                ]


def weigh_kept_body(kind, extra, kept_ref, mass_ref, x_ref, _, out_ref, kept_out, x_out, sum_ref):
    chip, core = place()
    span = sum_ref.shape[1]
    total = x_ref.shape[0]
    block = chip * CORES + (core if kind == OWN else 1 - core)
    columns = pl.ds(pl.multiple_of(block * span, span), span)
    sum_ref[...] = jnp.dot(kept_ref[...], x_ref[:, columns], preferred_element_type=F32)
    write_sums(False, 0, core, [out_ref], sum_ref, mass_ref[...], extra)


def weigh_kept(kind, n_pts, kept, mass, points, after):
    total, width = points.shape
    rows, cols = kept.shape[0], width // n_pts
    extra = round_up(-(-rows // cols), 8)
    return pl.pallas_call(
        functools.partial(weigh_kept_body, kind, extra),
        in_specs=[VMEM] * 3 + [ANY],
        out_specs=[VMEM] * 3,
        input_output_aliases={0: 1, 2: 2},
        scratch_shapes=[pltpu.VMEM((rows, cols), F32)],
        out_shape=[
            jax.ShapeDtypeStruct((1, rows + extra, cols), F32),
            jax.ShapeDtypeStruct(kept.shape, BF16),
            jax.ShapeDtypeStruct(points.shape, BF16),
        ],
        compiler_params=params(KEPT_VMEM),
        cost_estimate=pl.CostEstimate(
            flops=2 * rows * cols * total, bytes_accessed=2 * total * (rows + cols), transcendentals=0
        ),
    )(kept, mass, points, after)


def weigh(by_rows, kind, chips, stats, tops, shifted, points, after):
    total, width = points.shape
    pair = shifted.shape[0] // chips
    parts, others = (CORES, chips - 1) if kind == FAR else (1, 1)
    line = stats[0].shape[2]
    chunk = line * divisor(total // line, CHUNK_LINES)
    slots = min(WEIGH_SLOTS, total // chunk)
    kept = []
    if not by_rows:
        kept = [
            jax.ShapeDtypeStruct((shifted.shape[0], total), BF16),
            jax.ShapeDtypeStruct((1, shifted.shape[0]), F32),
        ]
    if by_rows:
        rows, cols = pair // CORES, width
        sums = (rows * parts, width)
    else:
        rows, cols = shifted.shape[0], width // (CORES * chips)
        sums = (rows, cols * parts)
    n_tops = len(tops)
    extra = round_up(-(-rows // cols), 8)
    return pl.pallas_call(
        functools.partial(weigh_body, by_rows, len(stats), n_tops, kind, others, extra, pair),
        in_specs=[VMEM] * (len(stats) + n_tops) + [ANY, VMEM, ANY],
        out_specs=[VMEM] * (parts + (1 if by_rows else 3)),
        input_output_aliases={len(stats) + n_tops + 1: parts},
        scratch_shapes=[pltpu.VMEM(stats[0].shape[1:], F32)] * 2
        + [pltpu.VMEM((sums[0], chunk), BF16)] * (2 if by_rows else 0)
        + [
            pltpu.VMEM((slots, sums[0], chunk), F32),
            pltpu.VMEM((sums[0], 128), F32),
            pltpu.VMEM(sums, F32),
            pltpu.SemaphoreType.DMA((slots,)),
        ],
        out_shape=[jax.ShapeDtypeStruct((others, rows + extra, cols), F32)] * parts
        + [jax.ShapeDtypeStruct(points.shape, BF16)]
        + kept,
        compiler_params=params(WEIGH_VMEM),
        cost_estimate=pl.CostEstimate(
            flops=2 * others * sums[0] * sums[1] * total,
            bytes_accessed=2 * others * total * (sums[1] + 2 * sums[0]),
            transcendentals=0,
        ),
    )(*stats, *tops, shifted, points, after)


def fold_body(rows, lines, mine_ref, theirs_ref, after_ref, out_ref):
    width = out_ref.shape[1]
    step = divisor(rows, 128) if lines == 1 else width
    out_ref[rows:, :] = jnp.zeros((out_ref.shape[0] - rows, width), BF16)
    scales = []
    for start in range(0, rows, step):
        part = slice(start, start + step)
        total = mine_ref[part, :] + theirs_ref[part, :]
        top = jnp.max(jnp.abs(total), axis=1, keepdims=True)
        scale = jnp.maximum(top * 1.01, 1e-30).astype(BF16)
        out_ref[part, :] = encode(total, scale.astype(F32))
        scales.append(jnp.broadcast_to(scale.astype(F32), (step, 128)).T[0:1, :])
    mass = mine_ref[rows : rows + lines, :] + theirs_ref[rows : rows + lines, :]
    if lines == 1:
        out_ref[rows : rows + 1, :rows] = jnp.concatenate(scales, axis=1).astype(BF16)
    else:
        out_ref[rows : rows + lines, :] = jnp.concatenate(scales, axis=0).astype(BF16)
    for number in range(1, 4):
        rounded = mass.astype(BF16)
        out_ref[rows + number * lines : rows + (number + 1) * lines, :] = rounded
        mass = mass - rounded.astype(F32)


def fold(mine, theirs, after):
    others, height, width = mine.shape
    out_height = coded_height(height, width)
    return pl.pallas_call(
        functools.partial(fold_body, *shape_of(height, width)),
        grid=(others,),
        in_specs=[pl.BlockSpec((None, height, width), lambda d: (d, 0, 0))] * 2 + [ANY],
        out_specs=pl.BlockSpec((None, out_height, width), lambda d: (d, 0, 0)),
        out_shape=jax.ShapeDtypeStruct((others, out_height, width), BF16),
        compiler_params=params(10),
        cost_estimate=pl.CostEstimate(
            flops=20 * others * height * width,
            bytes_accessed=10 * others * height * width,
            transcendentals=others * height * width,
        ),
    )(mine, theirs, after)


def shape_of(height, width):
    rows = height - 8
    while rows + round_up(-(-rows // width), 8) != height:
        rows -= 8
    return rows, -(-rows // width)


def coded_height(height, width):
    rows, lines = shape_of(height, width)
    return rows + round_up(4 * lines, 16)


def finish_body(rows, lines, as_units, mine_ref, theirs_ref, *refs):
    code_refs, out_ref = refs[:-1], refs[-1]
    width = out_ref.shape[1]
    step = divisor(rows, 128) if lines == 1 else width
    mass = mine_ref[rows : rows + lines, :] + theirs_ref[rows : rows + lines, :]
    for ref in code_refs:
        for number in range(1, 4):
            start = rows + number * lines
            mass = mass + ref[start : start + lines, :].astype(F32)

    def column(values, number):
        if lines == 1:
            line = values[:, number * step : (number + 1) * step]
        else:
            line = values[number : number + 1, :]
        return to_column(line, step)[:, 0:1]

    scales = [ref[rows : rows + lines, :].astype(F32) for ref in code_refs]
    for number in range(rows // step):
        part = slice(number * step, (number + 1) * step)
        total = mine_ref[part, :] + theirs_ref[part, :]
        for ref, scale in zip(code_refs, scales):
            total = total + decode(ref[part, :], column(scale, number))
        means = total / jnp.maximum(column(mass, number), 1.0)
        out_ref[part, :] = normalize_rows(means).astype(BF16) if as_units else means


def finish(as_units, mine, theirs, codes):
    height, width = mine.shape
    rows, lines = shape_of(height, width)
    out_type = BF16 if as_units else F32
    return pl.pallas_call(
        functools.partial(finish_body, rows, lines, as_units),
        out_shape=jax.ShapeDtypeStruct((rows, width), out_type),
        compiler_params=params(10),
        cost_estimate=pl.CostEstimate(
            flops=30 * rows * width,
            bytes_accessed=(12 + 2 * len(codes)) * rows * width,
            transcendentals=2 * rows * width,
        ),
    )(mine, theirs, *codes)


def keep_body(value_ref, after_ref, out_ref):
    pass


def keep_until(value, after):
    return pl.pallas_call(
        keep_body,
        in_specs=[VMEM, ANY],
        out_specs=VMEM,
        out_shape=jax.ShapeDtypeStruct(value.shape, value.dtype),
        input_output_aliases={0: 0},
        compiler_params=params(10),
    )(value, after)


def merge_body(*refs):
    refs[-1][0], refs[-1][1] = merge(refs[:-1])


def merged(sets):
    return pl.pallas_call(
        merge_body, out_shape=jax.ShapeDtypeStruct(sets[0].shape, F32), compiler_params=params(10)
    )(*sets)


def log_body(*refs):
    top, total = merge(refs[:-1])
    refs[-1][...] = top + jnp.log(total)


def log_norms(sets):
    return pl.pallas_call(
        log_body, out_shape=jax.ShapeDtypeStruct(sets[0].shape[1:], F32), compiler_params=params(10)
    )(*sets).reshape(-1)


def on_device(n_pts, n_cen, points, centroids):
    chips = n_pts // CORES

    def to_partner(value):
        return lax.ppermute(value, "pts", [(i, i ^ 1) for i in range(n_pts)])

    def to_chip(value, away):
        moves = [(i, (i + CORES * away) % n_pts) for i in range(n_pts)]
        return lax.ppermute(value, "pts", moves)

    def over_centroids(stats):
        if n_cen & (n_cen - 1):
            moves = [[(i, (i + away) % n_cen) for i in range(n_cen)] for away in range(1, n_cen)]
            return [stats] + [lax.ppermute(stats, "cen", move) for move in moves]
        done, sets = 1, [stats]
        while done < n_cen:
            if done > 1:
                sets = [merged(sets)]
            ways = 4 if (n_cen // done).bit_length() % 2 else 2
            for way in range(1, ways):
                moves = [(i, i ^ (way * done)) for i in range(n_cen)]
                sets.append(lax.ppermute(sets[0], "cen", moves))
            done *= ways
        return sets

    def sums_over_pts(by_rows, stats, tops, shifted, points):
        kept = mass = None

        def weighted(kind, after):
            nonlocal points, kept, mass
            if by_rows:
                *found, points = weigh(by_rows, kind, chips, stats, tops, shifted, points, after)
                return found
            if kind == FAR:
                *found, points, kept, mass = weigh(by_rows, kind, chips, stats, tops, shifted, points, after)
                return found
            *found, kept, points = weigh_kept(kind, n_pts, kept, mass, points, after)
            return found

        far_mine, far_theirs = weighted(FAR, stats[0])
        far_found = to_partner(far_theirs)
        (near_theirs,) = weighted(THEIRS, far_theirs)
        near_found = to_partner(near_theirs)
        coded = fold(far_mine, far_found, near_theirs)
        codes = [to_chip(coded[away - 1], away) for away in range(1, chips)]
        (near_mine,) = weighted(OWN, coded)
        return finish(by_rows, near_mine[0], near_found[0], codes), points

    square_sums = jnp.sum(centroids * centroids, axis=1)
    units = (centroids * lax.rsqrt(square_sums + 1e-06)[:, None]).astype(BF16)
    points, shifted, own = scores(ITERS > 1, [units], points)
    stats = over_centroids(own)
    tops = [own]
    for iteration in range(1, ITERS):
        raw = iteration + 1 < ITERS
        mine, points = sums_over_pts(True, stats, tops, shifted, points)
        away_units = [to_chip(mine, -away) for away in range(1, chips)]
        points, shifted, near_own = scores(raw, [mine, to_partner(mine)], points, 0, shifted)
        away_units = [keep_until(unit, near_own) for unit in away_units]
        blocks = [unit for mine in away_units for unit in (mine, to_partner(mine))]
        points, shifted, far_own = scores(raw, blocks, points, 1, shifted)
        tops = [near_own, far_own]
        stats = over_centroids(merged([near_own, far_own]))
    means, _ = sums_over_pts(False, stats, tops, shifted, points)
    return (means, log_norms(stats))


def solution(mesh):
    placed = (P("pts", None), P("cen", None))
    return jax.shard_map(
        functools.partial(on_device, mesh.shape["pts"], mesh.shape["cen"]),
        mesh=mesh,
        in_specs=placed,
        out_specs=(P("cen", "pts"), P("pts")),
        check_vma=False,
    )
```

profile of v0, /device:TPU:0, one launch (start us, length us, event | category | flops | bytes accessed | tf_op | source)
XLA Modules:
  0.0 135.1 jit_solution(10069748603330312558)
XLA Ops:
  0.6 7.6 %copy.32.x_ref = bf16[4096,1024]{1,0:T(8,128)(2,1)} copy(bf16[4096,1024]{1,0:T(8,128)(2,1)} %param.2) | data formatting | bytes 16777216
  8.2 2.7 %multiply_reduce_fusion = f32[1024]{0:T(1024)S(1)} fusion(f32[1024,1024]{1,0:T(8,128)} %param.3), kind=kLoop, calls=%fused_computation.1 | loop fusion | flops 2096128 | bytes 4198400 | tf_op jit(solution)/shard_map/reduce_sum | solution.py:575
  10.9 2.9 %multiply_convert_fusion.units = bf16[1024,1024]{1,0:T(8,128)(2,1)S(1)} fusion(f32[1024,1024]{1,0:T(8,128)} %param.3, f32[1024]{0:T(1024)S(1)} %add_rsqrt_fusion), kind=kLoop, calls=%fused_computation | loop fusion | flops 2097152 | bytes 6295552 | tf_op jit(solution)/shard_map/convert_element_type | solution.py:576
  13.8 0.3 copy-done
  14.1 14.4 %shard_map.41 = (bf16[4096,1024]{1,0:T(8,128)(2,1)S(1)}, f32[1024,4096]{1,0:T(8,128)}, f32[2,8,512]{2,1,0:T(8,128)S(1)}) custom-call(bf16[1024,1024]{1,0:T(8,128)(2,1)S(1)} %multiply_convert_fusion.units, bf16[4096,1024]{1,0:T(8,128)(2,1)S(1)} %copy-done), custom_call_target="tpu_custom_call", output_to_operand_aliasing={{0}: (1, {})} | custom-call | flops 8589934592 | bytes 25165824 | tf_op jit(solution)/shard_map/pallas_call | solution.py:175
  28.6 3.0 %collective-permute-start = (f32[2,8,512]{2,1,0:T(8,128)S(1)}, f32[2,8,512]{2,1,0:T(8,128)S(1)}, u32[]{:S(2)}, u32[]{:S(2)}) collective-permute-start(f32[2,8,512]{2,1,0:T(8,128)S(1)} %get-tuple-element.27.refs_0_.refs_4_), channel_id=1, source_target_pairs={{0,1},{1,0},{2,3},{3,2},{4,5},{5,4},{6,7},{7,6},{8,9},{9,8},{10,11... | collective-permute-start | bytes 98312 | tf_op jit(solution)/shard_map/ppermute | solution.py:548
  31.6 1.9 %collective-permute-done.refs_1_ = f32[2,8,512]{2,1,0:T(8,128)S(1)} collective-permute-done((f32[2,8,512]{2,1,0:T(8,128)S(1)}, f32[2,8,512]{2,1,0:T(8,128)S(1)}, u32[]{:S(2)}, u32[]{:S(2)}) %collective-permute-start) | collective-permute-done | bytes 32800 | tf_op jit(solution)/shard_map/ppermute | solution.py:548
  33.5 4.2 %collective-permute-start.3 = (f32[2,8,512]{2,1,0:T(8,128)S(1)}, f32[2,8,512]{2,1,0:T(8,128)S(1)}, u32[]{:S(2)}, u32[]{:S(2)}) collective-permute-start(f32[2,8,512]{2,1,0:T(8,128)S(1)} %shard_map.42.refs_0_.refs_7_), channel_id=1, source_target_pairs={{0,6},{1,7},{2,4},{3,5},{4,2},{5,3},{6,0},{7,1},{8,14},{9,15},{10,... | collective-permute-start | bytes 98312 | tf_op jit(solution)/shard_map/ppermute | solution.py:548
  37.7 0.0 collective-permute-start.2
  37.7 0.6 collective-permute-start.1
  38.3 1.3 collective-permute-done.3.refs_3_
  39.6 2.9 %collective-permute-done.2.refs_2_ = f32[2,8,512]{2,1,0:T(8,128)S(1)} collective-permute-done((f32[2,8,512]{2,1,0:T(8,128)S(1)}, f32[2,8,512]{2,1,0:T(8,128)S(1)}, u32[]{:S(2)}, u32[]{:S(2)}) %collective-permute-start.2) | collective-permute-done | bytes 32800 | tf_op jit(solution)/shard_map/ppermute | solution.py:548
  42.5 6.9 %shard_map.43 = (f32[1,264,1024]{2,1,0:T(8,128)S(1)}, f32[1,264,1024]{2,1,0:T(8,128)S(1)}, bf16[4096,1024]{1,0:T(8,128)(2,1)S(1)}) custom-call(f32[2,8,512]{2,1,0:T(8,128)S(1)} %shard_map.42.refs_0_.refs_7_, f32[2,8,512]{2,1,0:T(8,128)S(1)} %collective-permute-done.1.refs_1_, ...), custom_call_target="tpu_custom_call", output_to_operand_aliasing={{2}: (6, {})} | custom-call | flops 4294967296 | bytes 16777216 | tf_op jit(solution)/shard_map/pallas_call | solution.py:370
  49.4 0.1 collective-permute-start.4
  49.5 4.4 %shard_map.44 = (f32[1,264,1024]{2,1,0:T(8,128)S(1)}, bf16[4096,1024]{1,0:T(8,128)(2,1)S(1)}) custom-call(f32[2,8,512]{2,1,0:T(8,128)S(1)} %shard_map.42.refs_0_.refs_7_, f32[2,8,512]{2,1,0:T(8,128)S(1)} %collective-permute-done.1.refs_1_, f32[2,8,512]{2,1,0:T(8,128)S(1)} %collective-permute-done.2.refs_2_, ...), custom_call_target="tpu_custom_call", output_to_operand_aliasing={{1}: (6, {})} | custom-call | flops 2147483648 | bytes 12582912 | tf_op jit(solution)/shard_map/pallas_call | solution.py:370
  53.9 0.6 collective-permute-start.5
  54.4 0.0 collective-permute-done.4.theirs_ref
  54.4 0.7 shard_map.45.refs_7_
  55.1 1.6 %collective-permute-start.6 = (bf16[272,1024]{1,0:T(8,128)(2,1)S(1)}, bf16[272,1024]{1,0:T(8,128)(2,1)S(1)}, u32[]{:S(2)}, u32[]{:S(2)}) collective-permute-start(bf16[272,1024]{1,0:T(8,128)(2,1)S(1)} %bitcast.8), channel_id=1, source_target_pairs={{0,16},{8,24},{16,0},{24,8},{1,17},{9,25},{17,1},{25,9},{2,18},{10... | collective-permute-start | bytes 1671176 | tf_op jit(solution)/shard_map/ppermute | solution.py:535
  56.7 4.4 %shard_map.46 = (f32[1,264,1024]{2,1,0:T(8,128)S(1)}, bf16[4096,1024]{1,0:T(8,128)(2,1)S(1)}) custom-call(f32[2,8,512]{2,1,0:T(8,128)S(1)} %shard_map.42.refs_0_.refs_7_, f32[2,8,512]{2,1,0:T(8,128)S(1)} %collective-permute-done.1.refs_1_, f32[2,8,512]{2,1,0:T(8,128)S(1)} %collective-permute-done.2.refs_2_, ...), custom_call_target="tpu_custom_call", output_to_operand_aliasing={{1}: (6, {})} | custom-call | flops 2147483648 | bytes 12582912 | tf_op jit(solution)/shard_map/pallas_call | solution.py:370
  61.1 0.0 collective-permute-done.5
  61.1 8.6 %collective-permute-done.6.refs_0_ = bf16[272,1024]{1,0:T(8,128)(2,1)S(1)} collective-permute-done((bf16[272,1024]{1,0:T(8,128)(2,1)S(1)}, bf16[272,1024]{1,0:T(8,128)(2,1)S(1)}, u32[]{:S(2)}, u32[]{:S(2)}) %collective-permute-start.6) | collective-permute-done | bytes 557088 | tf_op jit(solution)/shard_map/ppermute | solution.py:535
  69.7 0.9 shard_map.47.refs_0_
  70.7 0.1 collective-permute-start.7
  70.8 1.6 %collective-permute-start.8 = (bf16[256,1024]{1,0:T(8,128)(2,1)S(1)}, bf16[256,1024]{1,0:T(8,128)(2,1)S(1)}, u32[]{:S(2)}, u32[]{:S(2)}) collective-permute-start(bf16[256,1024]{1,0:T(8,128)(2,1)S(1)} %shard_map.47.refs_0_), channel_id=1, source_target_pairs={{0,16},{8,24},{16,0},{24,8},{1,17},{9,25},{17,1},{25,9},{2,18},{10... | collective-permute-start | bytes 1572872 | tf_op jit(solution)/shard_map/ppermute | solution.py:535
  72.4 0.3 collective-permute-done.7.refs_1_
  72.7 9.2 %shard_map.48 = (bf16[4096,1024]{1,0:T(8,128)(2,1)S(1)}, f32[1024,4096]{1,0:T(8,128)}, f32[2,8,512]{2,1,0:T(8,128)S(1)}) custom-call(bf16[256,1024]{1,0:T(8,128)(2,1)S(1)} %shard_map.47.refs_0_, bf16[256,1024]{1,0:T(8,128)(2,1)S(1)} %collective-permute-done.7.refs_1_, bf16[4096,1024]{1,0:T(8,128)(2,1)S(1)} %get-tuple-element.36.refs_2_), custom_call_target="tpu_custom_call", output_to_operand_aliasing={{0}: (2, {})} | custom-call | flops 4294967296 | bytes 16777216 | tf_op jit(solution)/shard_map/pallas_call | solution.py:175
  81.9 3.2 %collective-permute-done.8.value_ref = bf16[256,1024]{1,0:T(8,128)(2,1)S(1)} collective-permute-done((bf16[256,1024]{1,0:T(8,128)(2,1)S(1)}, bf16[256,1024]{1,0:T(8,128)(2,1)S(1)}, u32[]{:S(2)}, u32[]{:S(2)}) %collective-permute-start.8) | collective-permute-done | bytes 524320 | tf_op jit(solution)/shard_map/ppermute | solution.py:535
  85.1 1.9 %collective-permute-done.9.refs_1_ = bf16[256,1024]{1,0:T(8,128)(2,1)S(1)} collective-permute-done((bf16[256,1024]{1,0:T(8,128)(2,1)S(1)}, bf16[256,1024]{1,0:T(8,128)(2,1)S(1)}, u32[]{:S(2)}, u32[]{:S(2)}) %collective-permute-start.9) | collective-permute-done | bytes 524320 | tf_op jit(solution)/shard_map/ppermute | solution.py:531
  87.0 9.0 %shard_map.50 = (bf16[4096,1024]{1,0:T(8,128)(2,1)S(1)}, f32[1024,4096]{1,0:T(8,128)}, f32[2,8,512]{2,1,0:T(8,128)S(1)}) custom-call(bf16[256,1024]{1,0:T(8,128)(2,1)S(1)} %shard_map.49.refs_0_, bf16[256,1024]{1,0:T(8,128)(2,1)S(1)} %collective-permute-done.9.refs_1_, ...), custom_call_target="tpu_custom_call", output_to_operand_aliasing={{0}: (2, {}), {1}: (3, {})} | custom-call | flops 4294967296 | bytes 16777216 | tf_op jit(solution)/shard_map/pallas_call | solution.py:175
  96.0 1.6 %collective-permute-start.10 = (f32[2,8,512]{2,1,0:T(8,128)S(1)}, f32[2,8,512]{2,1,0:T(8,128)S(1)}, u32[]{:S(2)}, u32[]{:S(2)}) collective-permute-start(f32[2,8,512]{2,1,0:T(8,128)S(1)} %shard_map.51.refs_0_), channel_id=1, source_target_pairs={{0,1},{1,0},{2,3},{3,2},{4,5},{5,4},{6,7},{7,6},{8,9},{9,8},{10,11... | collective-permute-start | bytes 98312 | tf_op jit(solution)/shard_map/ppermute | solution.py:548
  97.6 2.4 %collective-permute-done.10.refs_1_ = f32[2,8,512]{2,1,0:T(8,128)S(1)} collective-permute-done((f32[2,8,512]{2,1,0:T(8,128)S(1)}, f32[2,8,512]{2,1,0:T(8,128)S(1)}, u32[]{:S(2)}, u32[]{:S(2)}) %collective-permute-start.10) | collective-permute-done | bytes 32800 | tf_op jit(solution)/shard_map/ppermute | solution.py:548
  100.0 1.5 %collective-permute-start.13 = (f32[2,8,512]{2,1,0:T(8,128)S(1)}, f32[2,8,512]{2,1,0:T(8,128)S(1)}, u32[]{:S(2)}, u32[]{:S(2)}) collective-permute-start(f32[2,8,512]{2,1,0:T(8,128)S(1)} %shard_map.52.refs_0_.refs_8_), channel_id=1, source_target_pairs={{0,6},{1,7},{2,4},{3,5},{4,2},{5,3},{6,0},{7,1},{8,14},{9,15},{10,... | collective-permute-start | bytes 98312 | tf_op jit(solution)/shard_map/ppermute | solution.py:548
  101.5 0.6 collective-permute-start.12
  102.2 2.3 %collective-permute-start.11 = (f32[2,8,512]{2,1,0:T(8,128)S(1)}, f32[2,8,512]{2,1,0:T(8,128)S(1)}, u32[]{:S(2)}, u32[]{:S(2)}) collective-permute-start(f32[2,8,512]{2,1,0:T(8,128)S(1)} %shard_map.52.refs_0_.refs_8_), channel_id=1, source_target_pairs={{0,2},{1,3},{2,0},{3,1},{4,6},{5,7},{6,4},{7,5},{8,10},{9,11},{10,... | collective-permute-start | bytes 98312 | tf_op jit(solution)/shard_map/ppermute | solution.py:548
  104.5 1.3 collective-permute-done.13.refs_3_
  105.8 0.6 collective-permute-done.12.refs_2_
  106.4 0.3 collective-permute-done.11.refs_1_
  106.7 8.5 %shard_map.53 = (f32[1,1032,256]{2,1,0:T(8,128)S(1)}, f32[1,1032,256]{2,1,0:T(8,128)S(1)}, bf16[4096,1024]{1,0:T(8,128)(2,1)S(1)}, bf16[1024,4096]{1,0:T(8,128)(2,1)S(1)}, f32[1,1024]{1,0:T(1,128)S(1)}) custom-call(f32[2,8,512]{2,1,0:T(8,128)S(1)} %shard_map.52.refs_0_.refs_8_, ...), custom_call_target="tpu_custom_call", output_to_operand_aliasing={{2}: (7, {})} | custom-call | flops 4294967296 | bytes 20971520 | tf_op jit(solution)/shard_map/pallas_call | solution.py:370
  115.2 0.1 collective-permute-start.14
  115.3 2.4 %shard_map.54 = (f32[1,1032,256]{2,1,0:T(8,128)S(1)}, bf16[1024,4096]{1,0:T(8,128)(2,1)S(1)}, bf16[4096,1024]{1,0:T(8,128)(2,1)S(1)}) custom-call(bf16[1024,4096]{1,0:T(8,128)(2,1)S(1)} %get-tuple-element.43.kept_ref, f32[1,1024]{1,0:T(1,128)S(1)} %get-tuple-element.44.mass_ref, ...), custom_call_target="tpu_custom_call", output_to_operand_aliasing={{1}: (0, {}), {2}: (2, {})} | custom-call | flops 2147483648 | bytes 10485760 | tf_op jit(solution)/shard_map/pallas_call | solution.py:331
  117.7 0.5 collective-permute-start.15
  118.2 0.8 shard_map.55._
  119.0 1.6 %collective-permute-start.16 = (bf16[1040,256]{1,0:T(8,128)(2,1)S(1)}, bf16[1040,256]{1,0:T(8,128)(2,1)S(1)}, u32[]{:S(2)}, u32[]{:S(2)}) collective-permute-start(bf16[1040,256]{1,0:T(8,128)(2,1)S(1)} %bitcast.9), channel_id=1, source_target_pairs={{0,16},{8,24},{16,0},{24,8},{1,17},{9,25},{17,1},{25,9},{2,18},{10... | collective-permute-start | bytes 1597448 | tf_op jit(solution)/shard_map/ppermute | solution.py:535
  120.6 0.6 copy.17
  121.2 2.4 %shard_map.56 = (f32[1,1032,256]{2,1,0:T(8,128)S(1)}, bf16[1024,4096]{1,0:T(8,128)(2,1)S(1)}, bf16[4096,1024]{1,0:T(8,128)(2,1)S(1)}) custom-call(bf16[1024,4096]{1,0:T(8,128)(2,1)S(1)} %get-tuple-element.47.kept_ref, f32[1,1024]{1,0:T(1,128)S(1)} %get-tuple-element.44.mass_ref, ...), custom_call_target="tpu_custom_call", output_to_operand_aliasing={{1}: (0, {}), {2}: (2, {})} | custom-call | flops 2147483648 | bytes 10485760 | tf_op jit(solution)/shard_map/pallas_call | solution.py:331
  123.6 9.5 %collective-permute-done.16.refs_0_ = bf16[1040,256]{1,0:T(8,128)(2,1)S(1)} collective-permute-done((bf16[1040,256]{1,0:T(8,128)(2,1)S(1)}, bf16[1040,256]{1,0:T(8,128)(2,1)S(1)}, u32[]{:S(2)}, u32[]{:S(2)}) %collective-permute-start.16) | collective-permute-done | bytes 532512 | tf_op jit(solution)/shard_map/ppermute | solution.py:535
  133.1 2.0 %shard_map.57 = f32[1024,256]{1,0:T(8,128)} custom-call(f32[1032,256]{1,0:T(8,128)S(1)} %bitcast.13, f32[1032,256]{1,0:T(8,128)S(1)} %bitcast.12, bf16[1040,256]{1,0:T(8,128)(2,1)S(1)} %collective-permute-done.16.refs_0_), custom_call_target="tpu_custom_call" | custom-call | flops 7864320 | bytes 3670016 | tf_op jit(solution)/shard_map/pallas_call | solution.py:479
  (11 shorter events, 0.1 us)
Async XLA Ops:
  8.2 5.9 %copy-start = (bf16[4096,1024]{1,0:T(8,128)(2,1)S(1)}, bf16[4096,1024]{1,0:T(8,128)(2,1)}, u32[]{:S(2)}) copy-start(bf16[4096,1024]{1,0:T(8,128)(2,1)} %copy.32.x_ref) | copy-start | bytes 25165828
  28.6 4.9 %collective-permute-start = (f32[2,8,512]{2,1,0:T(8,128)S(1)}, f32[2,8,512]{2,1,0:T(8,128)S(1)}, u32[]{:S(2)}, u32[]{:S(2)}) collective-permute-start(f32[2,8,512]{2,1,0:T(8,128)S(1)} %get-tuple-element.27.refs_0_.refs_4_), channel_id=1, source_target_pairs={{0,1},{1,0},{2,3},{3,2},{4,5},{5,4},{6,7},{7,6},{8,9},{9,8},{10,11... | collective-permute-start | bytes 98312 | tf_op jit(solution)/shard_map/ppermute | solution.py:548
  33.5 6.1 %collective-permute-start.3 = (f32[2,8,512]{2,1,0:T(8,128)S(1)}, f32[2,8,512]{2,1,0:T(8,128)S(1)}, u32[]{:S(2)}, u32[]{:S(2)}) collective-permute-start(f32[2,8,512]{2,1,0:T(8,128)S(1)} %shard_map.42.refs_0_.refs_7_), channel_id=1, source_target_pairs={{0,6},{1,7},{2,4},{3,5},{4,2},{5,3},{6,0},{7,1},{8,14},{9,15},{10,... | collective-permute-start | bytes 98312 | tf_op jit(solution)/shard_map/ppermute | solution.py:548
  37.7 4.8 %collective-permute-start.2 = (f32[2,8,512]{2,1,0:T(8,128)S(1)}, f32[2,8,512]{2,1,0:T(8,128)S(1)}, u32[]{:S(2)}, u32[]{:S(2)}) collective-permute-start(f32[2,8,512]{2,1,0:T(8,128)S(1)} %shard_map.42.refs_0_.refs_7_), channel_id=1, source_target_pairs={{0,4},{1,5},{2,6},{3,7},{4,0},{5,1},{6,2},{7,3},{8,12},{9,13},{10,... | collective-permute-start | bytes 98312 | tf_op jit(solution)/shard_map/ppermute | solution.py:548
  37.7 4.8 %collective-permute-start.1 = (f32[2,8,512]{2,1,0:T(8,128)S(1)}, f32[2,8,512]{2,1,0:T(8,128)S(1)}, u32[]{:S(2)}, u32[]{:S(2)}) collective-permute-start(f32[2,8,512]{2,1,0:T(8,128)S(1)} %shard_map.42.refs_0_.refs_7_), channel_id=1, source_target_pairs={{0,2},{1,3},{2,0},{3,1},{4,6},{5,7},{6,4},{7,5},{8,10},{9,11},{10,... | collective-permute-start | bytes 98312 | tf_op jit(solution)/shard_map/ppermute | solution.py:548
  49.4 5.0 %collective-permute-start.4 = (f32[1,264,1024]{2,1,0:T(8,128)S(1)}, f32[1,264,1024]{2,1,0:T(8,128)S(1)}, u32[]{:S(2)}, u32[]{:S(2)}) collective-permute-start(f32[1,264,1024]{2,1,0:T(8,128)S(1)} %get-tuple-element.31.refs_7_), channel_id=1, source_target_pairs={{0,8},{8,0},{16,24},{24,16},{1,9},{9,1},{17,25},{25,17},{2,10},{10... | collective-permute-start | bytes 3244040 | tf_op jit(solution)/shard_map/ppermute | solution.py:531
  53.9 7.2 %collective-permute-start.5 = (f32[1,264,1024]{2,1,0:T(8,128)S(1)}, f32[1,264,1024]{2,1,0:T(8,128)S(1)}, u32[]{:S(2)}, u32[]{:S(2)}) collective-permute-start(f32[1,264,1024]{2,1,0:T(8,128)S(1)} %get-tuple-element.34.after_ref), channel_id=1, source_target_pairs={{0,8},{8,0},{16,24},{24,16},{1,9},{9,1},{17,25},{25,17},{2,10},{10... | collective-permute-start | bytes 3244040 | tf_op jit(solution)/shard_map/ppermute | solution.py:531
  55.1 14.6 %collective-permute-start.6 = (bf16[272,1024]{1,0:T(8,128)(2,1)S(1)}, bf16[272,1024]{1,0:T(8,128)(2,1)S(1)}, u32[]{:S(2)}, u32[]{:S(2)}) collective-permute-start(bf16[272,1024]{1,0:T(8,128)(2,1)S(1)} %bitcast.8), channel_id=1, source_target_pairs={{0,16},{8,24},{16,0},{24,8},{1,17},{9,25},{17,1},{25,9},{2,18},{10... | collective-permute-start | bytes 1671176 | tf_op jit(solution)/shard_map/ppermute | solution.py:535
  70.7 2.0 %collective-permute-start.7 = (bf16[256,1024]{1,0:T(8,128)(2,1)S(1)}, bf16[256,1024]{1,0:T(8,128)(2,1)S(1)}, u32[]{:S(2)}, u32[]{:S(2)}) collective-permute-start(bf16[256,1024]{1,0:T(8,128)(2,1)S(1)} %shard_map.47.refs_0_), channel_id=1, source_target_pairs={{0,8},{8,0},{16,24},{24,16},{1,9},{9,1},{17,25},{25,17},{2,10},{10... | collective-permute-start | bytes 1572872 | tf_op jit(solution)/shard_map/ppermute | solution.py:531
  70.8 14.3 %collective-permute-start.8 = (bf16[256,1024]{1,0:T(8,128)(2,1)S(1)}, bf16[256,1024]{1,0:T(8,128)(2,1)S(1)}, u32[]{:S(2)}, u32[]{:S(2)}) collective-permute-start(bf16[256,1024]{1,0:T(8,128)(2,1)S(1)} %shard_map.47.refs_0_), channel_id=1, source_target_pairs={{0,16},{8,24},{16,0},{24,8},{1,17},{9,25},{17,1},{25,9},{2,18},{10... | collective-permute-start | bytes 1572872 | tf_op jit(solution)/shard_map/ppermute | solution.py:535
  85.1 1.9 %collective-permute-start.9 = (bf16[256,1024]{1,0:T(8,128)(2,1)S(1)}, bf16[256,1024]{1,0:T(8,128)(2,1)S(1)}, u32[]{:S(2)}, u32[]{:S(2)}) collective-permute-start(bf16[256,1024]{1,0:T(8,128)(2,1)S(1)} %shard_map.49.refs_0_), channel_id=1, source_target_pairs={{0,8},{8,0},{16,24},{24,16},{1,9},{9,1},{17,25},{25,17},{2,10},{10... | collective-permute-start | bytes 1572872 | tf_op jit(solution)/shard_map/ppermute | solution.py:531
  96.0 4.0 %collective-permute-start.10 = (f32[2,8,512]{2,1,0:T(8,128)S(1)}, f32[2,8,512]{2,1,0:T(8,128)S(1)}, u32[]{:S(2)}, u32[]{:S(2)}) collective-permute-start(f32[2,8,512]{2,1,0:T(8,128)S(1)} %shard_map.51.refs_0_), channel_id=1, source_target_pairs={{0,1},{1,0},{2,3},{3,2},{4,5},{5,4},{6,7},{7,6},{8,9},{9,8},{10,11... | collective-permute-start | bytes 98312 | tf_op jit(solution)/shard_map/ppermute | solution.py:548
  100.0 5.8 %collective-permute-start.13 = (f32[2,8,512]{2,1,0:T(8,128)S(1)}, f32[2,8,512]{2,1,0:T(8,128)S(1)}, u32[]{:S(2)}, u32[]{:S(2)}) collective-permute-start(f32[2,8,512]{2,1,0:T(8,128)S(1)} %shard_map.52.refs_0_.refs_8_), channel_id=1, source_target_pairs={{0,6},{1,7},{2,4},{3,5},{4,2},{5,3},{6,0},{7,1},{8,14},{9,15},{10,... | collective-permute-start | bytes 98312 | tf_op jit(solution)/shard_map/ppermute | solution.py:548
  101.5 4.8 %collective-permute-start.12 = (f32[2,8,512]{2,1,0:T(8,128)S(1)}, f32[2,8,512]{2,1,0:T(8,128)S(1)}, u32[]{:S(2)}, u32[]{:S(2)}) collective-permute-start(f32[2,8,512]{2,1,0:T(8,128)S(1)} %shard_map.52.refs_0_.refs_8_), channel_id=1, source_target_pairs={{0,4},{1,5},{2,6},{3,7},{4,0},{5,1},{6,2},{7,3},{8,12},{9,13},{10,... | collective-permute-start | bytes 98312 | tf_op jit(solution)/shard_map/ppermute | solution.py:548
  102.2 4.5 %collective-permute-start.11 = (f32[2,8,512]{2,1,0:T(8,128)S(1)}, f32[2,8,512]{2,1,0:T(8,128)S(1)}, u32[]{:S(2)}, u32[]{:S(2)}) collective-permute-start(f32[2,8,512]{2,1,0:T(8,128)S(1)} %shard_map.52.refs_0_.refs_8_), channel_id=1, source_target_pairs={{0,2},{1,3},{2,0},{3,1},{4,6},{5,7},{6,4},{7,5},{8,10},{9,11},{10,... | collective-permute-start | bytes 98312 | tf_op jit(solution)/shard_map/ppermute | solution.py:548
  115.2 3.0 %collective-permute-start.14 = (f32[1,1032,256]{2,1,0:T(8,128)S(1)}, f32[1,1032,256]{2,1,0:T(8,128)S(1)}, u32[]{:S(2)}, u32[]{:S(2)}) collective-permute-start(f32[1,1032,256]{2,1,0:T(8,128)S(1)} %get-tuple-element.46._), channel_id=1, source_target_pairs={{0,8},{8,0},{16,24},{24,16},{1,9},{9,1},{17,25},{25,17},{2,10},{10... | collective-permute-start | bytes 3170312 | tf_op jit(solution)/shard_map/ppermute | solution.py:531
  117.7 5.9 %collective-permute-start.15 = (f32[1,1032,256]{2,1,0:T(8,128)S(1)}, f32[1,1032,256]{2,1,0:T(8,128)S(1)}, u32[]{:S(2)}, u32[]{:S(2)}) collective-permute-start(f32[1,1032,256]{2,1,0:T(8,128)S(1)} %get-tuple-element.50.after_ref), channel_id=1, source_target_pairs={{0,8},{8,0},{16,24},{24,16},{1,9},{9,1},{17,25},{25,17},{2,10},{10... | collective-permute-start | bytes 3170312 | tf_op jit(solution)/shard_map/ppermute | solution.py:531
  119.0 14.1 %collective-permute-start.16 = (bf16[1040,256]{1,0:T(8,128)(2,1)S(1)}, bf16[1040,256]{1,0:T(8,128)(2,1)S(1)}, u32[]{:S(2)}, u32[]{:S(2)}) collective-permute-start(bf16[1040,256]{1,0:T(8,128)(2,1)S(1)} %bitcast.9), channel_id=1, source_target_pairs={{0,16},{8,24},{16,0},{24,8},{1,17},{9,25},{17,1},{25,9},{2,18},{10... | collective-permute-start | bytes 1597448 | tf_op jit(solution)/shard_map/ppermute | solution.py:535
where the time goes:
time: 135 us
  Pallas kernels  66 us (49%)
  waiting for transfers between devices  34.3 us (25%)
  starting transfers between devices  19.9 us (15%)
  local copies, waits for them, and re-layouts  8.57 us (6%)
  other arithmetic  5.54 us (4%)
    pallas_call x3, Pallas kernels, scores(): pl.pallas_call(body, in_specs=[VMEM] * (count + 1) + [ANY] * len(more), o...  32.6 us
    pallas_call x4, Pallas kernels, weigh(): pl.pallas_call(functools.partial(weigh_body, by_rows, len(stats), n_tops,...  24.1 us
    ppermute x3, waiting for transfers between devices, to_chip(): return lax.ppermute(value, 'pts', moves)  21.3 us
    ppermute x8, starting transfers between devices, over_centroids(): sets.append(lax.ppermute(sets[0], 'cen', moves))  13.9 us
    ppermute x8, waiting for transfers between devices, over_centroids(): sets.append(lax.ppermute(sets[0], 'cen', moves))  10.7 us
    unnamed x4, local copies, waits for them, and re-layouts  8.57 us
    ppermute x3, starting transfers between devices, to_chip(): return lax.ppermute(value, 'pts', moves)  4.77 us
    pallas_call x2, Pallas kernels, weigh_kept(): pl.pallas_call(functools.partial(weigh_kept_body, kind, extra), in_specs=...  4.74 us
  transfers between devices with their start and end apart: 17, of which 12 were waited for; matrix products, arithmetic and copies ran while one was open for 0% of the time, Pallas kernels for 18%

commit v1 on v0

--- a/solution.py
+++ b/solution.py
@@ -10,6 +10,7 @@
 ITERS = 2
 F32 = jnp.float32
 BF16 = jnp.bfloat16
+LOAD_VMEM = 38
 SCORE_VMEM = 34
 WEIGH_VMEM = 34
 KEPT_VMEM = 20
@@ -72,6 +73,47 @@
     power = jnp.floor(jnp.log2(size))
     steps = 128.0 * (power - LOWEST + (size * jnp.exp2(-power) - 1.0))
     return jnp.where(wide < 0.0, -steps, steps) * (scale * (1.0 / LEVELS))
+
+
+def load_body(c_hbm, sums_ref, x_hbm, x_ref, units_ref, rows_ref, row_sems, point_sem):
+    row_step = rows_ref.shape[0] // row_sems.shape[0]
+
+    def rows_of(number):
+        part = pl.ds(number * row_step, row_step)
+        return pltpu.make_async_copy(c_hbm.at[part, :], rows_ref.at[part, :], row_sems.at[number])
+
+    all_points = pltpu.make_async_copy(x_hbm, x_ref, point_sem)
+    for number in range(row_sems.shape[0]):
+        rows_of(number).start()
+    all_points.start()
+    for number in range(row_sems.shape[0]):
+        rows_of(number).wait()
+        part = slice(number * row_step, (number + 1) * row_step)
+        scale = to_column(lax.rsqrt(sums_ref[:, part] + 1e-06), row_step)[:, 0:1]
+        units_ref[part, :] = (rows_ref[part, :] * scale).astype(BF16)
+    all_points.wait()
+
+
+def load(centroids, points):
+    square_sums = jnp.sum(centroids * centroids, axis=1)[None]
+    return pl.pallas_call(
+        load_body,
+        in_specs=[ANY, VMEM, ANY],
+        out_specs=[VMEM] * 2,
+        out_shape=[
+            jax.ShapeDtypeStruct(points.shape, BF16),
+            jax.ShapeDtypeStruct(centroids.shape, BF16),
+        ],
+        scratch_shapes=[
+            pltpu.VMEM(centroids.shape, F32),
+            pltpu.SemaphoreType.DMA((divisor(centroids.shape[0] // 16, 4),)),
+            pltpu.SemaphoreType.DMA(()),
+        ],
+        compiler_params=params(LOAD_VMEM),
+        cost_estimate=pl.CostEstimate(
+            flops=4 * centroids.size, bytes_accessed=4 * centroids.size + 2 * points.size, transcendentals=0
+        ),
+    )(centroids, square_sums, points)
 
 
 def score_points(raw, units, x_ref, e_parts, stat_ref, stage, semaphores):
@@ -131,17 +173,18 @@
     score_points(raw, units, x_ref, target, stat_ref, stage, semaphores)
 
 
-def next_scores_body(raw, count, away, *refs):
+def next_scores_body(raw, count, pieces, away, *refs):
     unit_refs = refs[:count]
     x_ref = refs[count]
     e_hbm, stat_ref, units, stage, semaphores = refs[-5:]
     rows = unit_refs[0].shape[0]
-    pair = CORES * rows
+    pair = CORES * pieces * rows
     chip, core = place()
     chips = e_hbm.shape[0] // pair
     for number, ref in enumerate(unit_refs):
-        of_pair = core if number % CORES == 0 else 1 - core
-        start = pl.multiple_of((number - number % CORES + of_pair) * rows, rows)
+        group, who, piece = number // (CORES * pieces), number // pieces % CORES, number % pieces
+        of_pair = (core if who == 0 else 1 - core) * pieces + piece
+        start = pl.multiple_of((group * CORES * pieces + of_pair) * rows, rows)
         units[pl.ds(start, rows), :] = ref[...]
 
     def target_of(number):
@@ -149,18 +192,18 @@
         return lambda columns: e_hbm.at[pl.ds(start, pair), columns]
 
     targets = [
-        (slice(number * pair, (number + 1) * pair), target_of(number)) for number in range(count // CORES)
+        (slice(number * pair, (number + 1) * pair), target_of(number)) for number in range(count // (CORES * pieces))
     ]
     score_points(raw, units, x_ref, targets, stat_ref, stage, semaphores)
 
 
-def scores(raw, blocks, points, away=None, shifted=None):
+def scores(raw, blocks, points, pieces=1, away=None, shifted=None):
     total, width = points.shape
     count = len(blocks)
     rows = sum(block.shape[0] for block in blocks)
     all_rows = rows if shifted is None else shifted.shape[0]
     stat = stat_shape(total)
-    parts = 1 if away is None else count // CORES
+    parts = 1 if away is None else count // (CORES * pieces)
     more = [] if shifted is None or away == 0 else [shifted]
     scratch = [
         pltpu.VMEM((divisor(stat[1], 2), rows, stat[2]), F32),
@@ -171,7 +214,7 @@
     if away is None:
         body = functools.partial(first_scores_body, raw)
     else:
-        body = functools.partial(next_scores_body, raw, count, away)
+        body = functools.partial(next_scores_body, raw, count, pieces, away)
     return pl.pallas_call(
         body,
         in_specs=[VMEM] * (count + 1) + [ANY] * len(more),
@@ -392,38 +435,43 @@
     )(*stats, *tops, shifted, points, after)
 
 
-def fold_body(rows, lines, mine_ref, theirs_ref, after_ref, out_ref):
-    width = out_ref.shape[1]
-    step = divisor(rows, 128) if lines == 1 else width
-    out_ref[rows:, :] = jnp.zeros((out_ref.shape[0] - rows, width), BF16)
-    scales = []
-    for start in range(0, rows, step):
-        part = slice(start, start + step)
-        total = mine_ref[part, :] + theirs_ref[part, :]
-        top = jnp.max(jnp.abs(total), axis=1, keepdims=True)
-        scale = jnp.maximum(top * 1.01, 1e-30).astype(BF16)
-        out_ref[part, :] = encode(total, scale.astype(F32))
-        scales.append(jnp.broadcast_to(scale.astype(F32), (step, 128)).T[0:1, :])
-    mass = mine_ref[rows : rows + lines, :] + theirs_ref[rows : rows + lines, :]
-    if lines == 1:
-        out_ref[rows : rows + 1, :rows] = jnp.concatenate(scales, axis=1).astype(BF16)
-    else:
-        out_ref[rows : rows + lines, :] = jnp.concatenate(scales, axis=0).astype(BF16)
-    for number in range(1, 4):
-        rounded = mass.astype(BF16)
-        out_ref[rows + number * lines : rows + (number + 1) * lines, :] = rounded
-        mass = mass - rounded.astype(F32)
-
-
-def fold(mine, theirs, after):
+def fold_body(rows, lines, pieces, mine_ref, theirs_ref, after_ref, *out_refs):
+    width = out_refs[0].shape[1]
+    count = rows // pieces
+    step = divisor(count, 128) if lines == 1 else width
+    all_masses = mine_ref[rows : rows + lines, :] + theirs_ref[rows : rows + lines, :]
+    for piece, out_ref in enumerate(out_refs):
+        out_ref[count:, :] = jnp.zeros((out_ref.shape[0] - count, width), BF16)
+        scales = []
+        for start in range(0, count, step):
+            part = slice(piece * count + start, piece * count + start + step)
+            total = mine_ref[part, :] + theirs_ref[part, :]
+            top = jnp.max(jnp.abs(total), axis=1, keepdims=True)
+            scale = jnp.maximum(top * 1.01, 1e-30).astype(BF16).astype(F32)
+            out_ref[start : start + step, :] = encode(total, scale)
+            scales.append(jnp.broadcast_to(scale, (step, 128)).T[0:1, :])
+        if lines == 1:
+            out_ref[count : count + 1, :count] = jnp.concatenate(scales, axis=1).astype(BF16)
+            mass, used = all_masses[:, piece * count : (piece + 1) * count], slice(0, count)
+        else:
+            out_ref[count : count + lines, :] = jnp.concatenate(scales, axis=0).astype(BF16)
+            mass, used = all_masses, slice(None)
+        for number in range(1, 4):
+            rounded = mass.astype(BF16)
+            out_ref[count + number * lines : count + (number + 1) * lines, used] = rounded
+            mass = mass - rounded.astype(F32)
+
+
+def fold(pieces, mine, theirs, after):
     others, height, width = mine.shape
-    out_height = coded_height(height, width)
-    return pl.pallas_call(
-        functools.partial(fold_body, *shape_of(height, width)),
+    rows, lines = shape_of(height, width)
+    coded = (rows // pieces + round_up(4 * lines, 16), width)
+    return pl.pallas_call(
+        functools.partial(fold_body, rows, lines, pieces),
         grid=(others,),
         in_specs=[pl.BlockSpec((None, height, width), lambda d: (d, 0, 0))] * 2 + [ANY],
-        out_specs=pl.BlockSpec((None, out_height, width), lambda d: (d, 0, 0)),
-        out_shape=jax.ShapeDtypeStruct((others, out_height, width), BF16),
+        out_specs=[pl.BlockSpec((None, *coded), lambda d: (d, 0, 0))] * pieces,
+        out_shape=[jax.ShapeDtypeStruct((others, *coded), BF16)] * pieces,
         compiler_params=params(10),
         cost_estimate=pl.CostEstimate(
             flops=20 * others * height * width,
@@ -440,20 +488,18 @@
     return rows, -(-rows // width)
 
 
-def coded_height(height, width):
-    rows, lines = shape_of(height, width)
-    return rows + round_up(4 * lines, 16)
-
-
-def finish_body(rows, lines, as_units, mine_ref, theirs_ref, *refs):
-    code_refs, out_ref = refs[:-1], refs[-1]
-    width = out_ref.shape[1]
-    step = divisor(rows, 128) if lines == 1 else width
+def finish_body(rows, lines, piece, as_units, mine_ref, theirs_ref, *refs):
+    code_refs, (_, out_ref) = refs[:-2], refs[-2:]
+    count, width = out_ref.shape
+    step = divisor(count, 128) if lines == 1 else width
     mass = mine_ref[rows : rows + lines, :] + theirs_ref[rows : rows + lines, :]
+    if lines == 1:
+        mass = mass[:, piece * count : (piece + 1) * count]
+    used = slice(0, count) if lines == 1 else slice(None)
     for ref in code_refs:
         for number in range(1, 4):
-            start = rows + number * lines
-            mass = mass + ref[start : start + lines, :].astype(F32)
+            start = count + number * lines
+            mass = mass + ref[start : start + lines, used].astype(F32)
 
     def column(values, number):
         if lines == 1:
@@ -462,30 +508,33 @@
             line = values[number : number + 1, :]
         return to_column(line, step)[:, 0:1]
 
-    scales = [ref[rows : rows + lines, :].astype(F32) for ref in code_refs]
-    for number in range(rows // step):
+    scales = [ref[count : count + lines, used].astype(F32) for ref in code_refs]
+    for number in range(count // step):
         part = slice(number * step, (number + 1) * step)
-        total = mine_ref[part, :] + theirs_ref[part, :]
+        near = slice(piece * count + number * step, piece * count + (number + 1) * step)
+        total = mine_ref[near, :] + theirs_ref[near, :]
         for ref, scale in zip(code_refs, scales):
             total = total + decode(ref[part, :], column(scale, number))
         means = total / jnp.maximum(column(mass, number), 1.0)
         out_ref[part, :] = normalize_rows(means).astype(BF16) if as_units else means
 
 
-def finish(as_units, mine, theirs, codes):
+def finish(as_units, piece, pieces, mine, theirs, codes, after):
     height, width = mine.shape
     rows, lines = shape_of(height, width)
-    out_type = BF16 if as_units else F32
-    return pl.pallas_call(
-        functools.partial(finish_body, rows, lines, as_units),
-        out_shape=jax.ShapeDtypeStruct((rows, width), out_type),
+    count = rows // pieces
+    return pl.pallas_call(
+        functools.partial(finish_body, rows, lines, piece, as_units),
+        in_specs=[VMEM] * (2 + len(codes)) + [ANY],
+        out_specs=VMEM,
+        out_shape=jax.ShapeDtypeStruct((count, width), BF16 if as_units else F32),
         compiler_params=params(10),
         cost_estimate=pl.CostEstimate(
-            flops=30 * rows * width,
-            bytes_accessed=(12 + 2 * len(codes)) * rows * width,
-            transcendentals=2 * rows * width,
+            flops=30 * count * width,
+            bytes_accessed=(12 + 2 * len(codes)) * count * width,
+            transcendentals=2 * count * width,
         ),
-    )(mine, theirs, *codes)
+    )(mine, theirs, *codes, after)
 
 
 def keep_body(value_ref, after_ref, out_ref):
@@ -567,27 +616,36 @@
         far_found = to_partner(far_theirs)
         (near_theirs,) = weighted(THEIRS, far_theirs)
         near_found = to_partner(near_theirs)
-        coded = fold(far_mine, far_found, near_theirs)
-        codes = [to_chip(coded[away - 1], away) for away in range(1, chips)]
-        (near_mine,) = weighted(OWN, coded)
-        return finish(by_rows, near_mine[0], near_found[0], codes), points
-
-    square_sums = jnp.sum(centroids * centroids, axis=1)
-    units = (centroids * lax.rsqrt(square_sums + 1e-06)[:, None]).astype(BF16)
+        coded = fold(pieces if by_rows else 1, far_mine, far_found, near_theirs)
+        codes = [[to_chip(each[away - 1], away) for away in range(1, chips)] for each in coded]
+        (near_mine,) = weighted(OWN, coded[0])
+        found, away_found, after = [], [], coded[0]
+        for piece, each in enumerate(codes):
+            found.append(finish(by_rows, piece, len(codes), near_mine[0], near_found[0], each, after))
+            if by_rows:
+                away_found.append([to_chip(found[-1], -away) for away in range(1, chips)])
+                after = away_found[-1][-1]
+        return found, away_found, points
+
+    block = centroids.shape[0] // n_pts
+    pieces = 2 if block % 256 == 0 else 1
+    points, units = load(centroids, points)
     points, shifted, own = scores(ITERS > 1, [units], points)
     stats = over_centroids(own)
     tops = [own]
     for iteration in range(1, ITERS):
         raw = iteration + 1 < ITERS
-        mine, points = sums_over_pts(True, stats, tops, shifted, points)
-        away_units = [to_chip(mine, -away) for away in range(1, chips)]
-        points, shifted, near_own = scores(raw, [mine, to_partner(mine)], points, 0, shifted)
-        away_units = [keep_until(unit, near_own) for unit in away_units]
-        blocks = [unit for mine in away_units for unit in (mine, to_partner(mine))]
-        points, shifted, far_own = scores(raw, blocks, points, 1, shifted)
+        mine, away_mine, points = sums_over_pts(True, stats, tops, shifted, points)
+        near_units = mine + [to_partner(unit) for unit in mine]
+        points, shifted, near_own = scores(raw, near_units, points, pieces, 0, shifted)
+        far_units = []
+        for units in zip(*away_mine):
+            units = [keep_until(unit, near_own) for unit in units]
+            far_units += units + [to_partner(unit) for unit in units]
+        points, shifted, far_own = scores(raw, far_units, points, pieces, 1, shifted)
         tops = [near_own, far_own]
         stats = over_centroids(merged([near_own, far_own]))
-    means, _ = sums_over_pts(False, stats, tops, shifted, points)
+    (means,), _, _ = sums_over_pts(False, stats, tops, shifted, points)
     return (means, log_norms(stats))
 
 

time: 135 us -> 133 us (0.985)
  local copies, waits for them, and re-layouts: 8.57 us -> 2.8 us
  Pallas kernels: 66 us -> 69.7 us
  other arithmetic: 5.54 us -> 2.53 us
  starting transfers between devices: 19.9 us -> 22.5 us
    unnamed x4 -> x3, local copies, waits for them, and re-layouts: 8.57 us -> 2.8 us
    pallas_call x4 -> x6, Pallas kernels: 4.45 us -> 8.24 us  [the longest x1 3.7 us: load(): pl.pallas_call(load_body, in_specs=[ANY, VMEM, ANY], out_specs=[VMEM] * 2...]
    convert_element_type x1 -> x0, other arithmetic: 2.85 us -> none  [on_device(): units = (centroids * lax.rsqrt(square_sums + 1e-06)[:, None]).astype(BF16)]
    ppermute x3 -> x5, starting transfers between devices: 4.77 us -> 6.78 us  [to_chip(): return lax.ppermute(value, 'pts', moves)]
    ppermute x3 -> x5, waiting for transfers between devices: 21.3 us -> 21.9 us  [to_chip(): return lax.ppermute(value, 'pts', moves)]
  transfers between devices with their start and end apart: 17 -> 21, of which waited for: 12 -> 13; matrix products, arithmetic and copies ran while one was open for 0% -> 0% of each run, Pallas kernels for 18% -> 19%
where the time goes in v1:
time: 133 us; the launch traced here: 132 us
  Pallas kernels  69.7 us (52%)
  waiting for transfers between devices  34 us (26%)
  starting transfers between devices  22.5 us (17%)
  local copies, waits for them, and re-layouts  2.8 us (2%)
  other arithmetic  2.53 us (2%)
    pallas_call x3, Pallas kernels, scores(): pl.pallas_call(body, in_specs=[VMEM] * (count + 1) + [ANY] * len(more), o...  32.5 us
    pallas_call x4, Pallas kernels, weigh(): pl.pallas_call(functools.partial(weigh_body, by_rows, len(stats), n_tops,...  24.1 us
    ppermute x5, waiting for transfers between devices, to_chip(): return lax.ppermute(value, 'pts', moves)  21.9 us
    ppermute x8, starting transfers between devices, over_centroids(): sets.append(lax.ppermute(sets[0], 'cen', moves))  13.9 us
    ppermute x8, waiting for transfers between devices, over_centroids(): sets.append(lax.ppermute(sets[0], 'cen', moves))  10.7 us
    ppermute x5, starting transfers between devices, to_chip(): return lax.ppermute(value, 'pts', moves)  6.78 us
    pallas_call x2, Pallas kernels, weigh_kept(): pl.pallas_call(functools.partial(weigh_kept_body, kind, extra), in_specs=...  4.74 us
    pallas_call x1, Pallas kernels, load(): pl.pallas_call(load_body, in_specs=[ANY, VMEM, ANY], out_specs=[VMEM] * 2...  3.7 us
  transfers between devices with their start and end apart: 21, of which 13 were waited for; matrix products, arithmetic and copies ran while one was open for 0% of the time, Pallas kernels for 19%

profile of v1, /device:TPU:0, one launch (start us, length us, event | category | flops | bytes accessed | tf_op | source)
XLA Modules:
  0.0 132.3 jit_solution(963185012292645872)
XLA Ops:
  0.6 2.5 %multiply_reduce_fusion = f32[1024]{0:T(1024)S(1)} fusion(f32[1024,1024]{1,0:T(8,128)} %c_hbm.1), kind=kLoop, calls=%fused_computation | loop fusion | flops 2096128 | bytes 4198400 | tf_op jit(solution)/shard_map/reduce_sum | solution.py:98
  3.2 2.2 %copy-done = f32[1024,1024]{1,0:T(8,128)S(1)} copy-done((f32[1024,1024]{1,0:T(8,128)S(1)}, f32[1024,1024]{1,0:T(8,128)}, u32[]{:S(2)}) %copy-start) | copy-done | bytes 4194328
  5.4 3.7 %shard_map.41 = (bf16[4096,1024]{1,0:T(8,128)(2,1)S(1)}, bf16[1024,1024]{1,0:T(8,128)(2,1)S(1)}) custom-call(f32[1024,1024]{1,0:T(8,128)S(1)} %copy-done, f32[1,1024]{1,0:T(1,128)S(1)} %bitcast.19, bf16[4096,1024]{1,0:T(8,128)(2,1)} %x_hbm.1), custom_call_target="tpu_custom_call" | custom-call | flops 4194304 | bytes 12582912 | tf_op jit(solution)/shard_map/pallas_call | solution.py:99
  9.1 14.3 %shard_map.42 = (bf16[4096,1024]{1,0:T(8,128)(2,1)S(1)}, f32[1024,4096]{1,0:T(8,128)}, f32[2,8,512]{2,1,0:T(8,128)S(1)}) custom-call(bf16[1024,1024]{1,0:T(8,128)(2,1)S(1)} %get-tuple-element.31.units, bf16[4096,1024]{1,0:T(8,128)(2,1)S(1)} %get-tuple-element.32.x_ref), custom_call_target="tpu_custom_call", output_to_operand_aliasing={{0}: (1, {})} | custom-call | flops 8589934592 | bytes 25165824 | tf_op jit(solution)/shard_map/pallas_call | solution.py:218
  23.4 3.0 %collective-permute-start = (f32[2,8,512]{2,1,0:T(8,128)S(1)}, f32[2,8,512]{2,1,0:T(8,128)S(1)}, u32[]{:S(2)}, u32[]{:S(2)}) collective-permute-start(f32[2,8,512]{2,1,0:T(8,128)S(1)} %get-tuple-element.33.refs_0_.refs_4_), channel_id=1, source_target_pairs={{0,1},{1,0},{2,3},{3,2},{4,5},{5,4},{6,7},{7,6},{8,9},{9,8},{10,11... | collective-permute-start | bytes 98312 | tf_op jit(solution)/shard_map/ppermute | solution.py:597
  26.4 1.9 %collective-permute-done.refs_1_ = f32[2,8,512]{2,1,0:T(8,128)S(1)} collective-permute-done((f32[2,8,512]{2,1,0:T(8,128)S(1)}, f32[2,8,512]{2,1,0:T(8,128)S(1)}, u32[]{:S(2)}, u32[]{:S(2)}) %collective-permute-start) | collective-permute-done | bytes 32800 | tf_op jit(solution)/shard_map/ppermute | solution.py:597
  28.3 4.2 %collective-permute-start.3 = (f32[2,8,512]{2,1,0:T(8,128)S(1)}, f32[2,8,512]{2,1,0:T(8,128)S(1)}, u32[]{:S(2)}, u32[]{:S(2)}) collective-permute-start(f32[2,8,512]{2,1,0:T(8,128)S(1)} %shard_map.43.refs_0_.refs_7_), channel_id=1, source_target_pairs={{0,6},{1,7},{2,4},{3,5},{4,2},{5,3},{6,0},{7,1},{8,14},{9,15},{10,... | collective-permute-start | bytes 98312 | tf_op jit(solution)/shard_map/ppermute | solution.py:597
  32.5 0.6 collective-permute-start.1
  33.2 1.3 collective-permute-done.3.refs_3_
  34.4 2.9 %collective-permute-done.2.refs_2_ = f32[2,8,512]{2,1,0:T(8,128)S(1)} collective-permute-done((f32[2,8,512]{2,1,0:T(8,128)S(1)}, f32[2,8,512]{2,1,0:T(8,128)S(1)}, u32[]{:S(2)}, u32[]{:S(2)}) %collective-permute-start.2) | collective-permute-done | bytes 32800 | tf_op jit(solution)/shard_map/ppermute | solution.py:597
  37.3 6.9 %shard_map.44 = (f32[1,264,1024]{2,1,0:T(8,128)S(1)}, f32[1,264,1024]{2,1,0:T(8,128)S(1)}, bf16[4096,1024]{1,0:T(8,128)(2,1)S(1)}) custom-call(f32[2,8,512]{2,1,0:T(8,128)S(1)} %shard_map.43.refs_0_.refs_7_, f32[2,8,512]{2,1,0:T(8,128)S(1)} %collective-permute-done.1.refs_1_, ...), custom_call_target="tpu_custom_call", output_to_operand_aliasing={{2}: (6, {})} | custom-call | flops 4294967296 | bytes 16777216 | tf_op jit(solution)/shard_map/pallas_call | solution.py:413
  44.3 0.1 collective-permute-start.4
  44.3 4.4 %shard_map.45 = (f32[1,264,1024]{2,1,0:T(8,128)S(1)}, bf16[4096,1024]{1,0:T(8,128)(2,1)S(1)}) custom-call(f32[2,8,512]{2,1,0:T(8,128)S(1)} %shard_map.43.refs_0_.refs_7_, f32[2,8,512]{2,1,0:T(8,128)S(1)} %collective-permute-done.1.refs_1_, f32[2,8,512]{2,1,0:T(8,128)S(1)} %collective-permute-done.2.refs_2_, ...), custom_call_target="tpu_custom_call", output_to_operand_aliasing={{1}: (6, {})} | custom-call | flops 2147483648 | bytes 12582912 | tf_op jit(solution)/shard_map/pallas_call | solution.py:413
  48.7 0.6 collective-permute-start.5
  49.3 0.7 shard_map.46
  50.0 1.6 %collective-permute-start.6 = (bf16[144,1024]{1,0:T(8,128)(2,1)S(1)}, bf16[144,1024]{1,0:T(8,128)(2,1)S(1)}, u32[]{:S(2)}, u32[]{:S(2)}) collective-permute-start(bf16[144,1024]{1,0:T(8,128)(2,1)S(1)} %bitcast.15), channel_id=1, source_target_pairs={{0,16},{8,24},{16,0},{24,8},{1,17},{9,25},{17,1},{25,9},{2,18},{10... | collective-permute-start | bytes 884744 | tf_op jit(solution)/shard_map/ppermute | solution.py:584
  51.5 0.5 collective-permute-start.7
  52.1 4.4 %shard_map.47 = (f32[1,264,1024]{2,1,0:T(8,128)S(1)}, bf16[4096,1024]{1,0:T(8,128)(2,1)S(1)}) custom-call(f32[2,8,512]{2,1,0:T(8,128)S(1)} %shard_map.43.refs_0_.refs_7_, f32[2,8,512]{2,1,0:T(8,128)S(1)} %collective-permute-done.1.refs_1_, f32[2,8,512]{2,1,0:T(8,128)S(1)} %collective-permute-done.2.refs_2_, ...), custom_call_target="tpu_custom_call", output_to_operand_aliasing={{1}: (6, {})} | custom-call | flops 2147483648 | bytes 12582912 | tf_op jit(solution)/shard_map/pallas_call | solution.py:413
  56.4 3.4 %collective-permute-done.6.refs_0_ = bf16[144,1024]{1,0:T(8,128)(2,1)S(1)} collective-permute-done((bf16[144,1024]{1,0:T(8,128)(2,1)S(1)}, bf16[144,1024]{1,0:T(8,128)(2,1)S(1)}, u32[]{:S(2)}, u32[]{:S(2)}) %collective-permute-start.6) | collective-permute-done | bytes 294944 | tf_op jit(solution)/shard_map/ppermute | solution.py:584
  59.9 0.5 shard_map.48.refs_0_
  60.4 1.6 %collective-permute-start.8 = (bf16[128,1024]{1,0:T(8,128)(2,1)S(1)}, bf16[128,1024]{1,0:T(8,128)(2,1)S(1)}, u32[]{:S(2)}, u32[]{:S(2)}) collective-permute-start(bf16[128,1024]{1,0:T(8,128)(2,1)S(1)} %shard_map.48.refs_0_), channel_id=1, source_target_pairs={{0,16},{8,24},{16,0},{24,8},{1,17},{9,25},{17,1},{25,9},{2,18},{10... | collective-permute-start | bytes 786440 | tf_op jit(solution)/shard_map/ppermute | solution.py:584
  62.0 4.2 %collective-permute-done.7.refs_0_ = bf16[144,1024]{1,0:T(8,128)(2,1)S(1)} collective-permute-done((bf16[144,1024]{1,0:T(8,128)(2,1)S(1)}, bf16[144,1024]{1,0:T(8,128)(2,1)S(1)}, u32[]{:S(2)}, u32[]{:S(2)}) %collective-permute-start.7) | collective-permute-done | bytes 294944 | tf_op jit(solution)/shard_map/ppermute | solution.py:584
  66.2 4.7 %collective-permute-done.8.refs_1_.value_ref = bf16[128,1024]{1,0:T(8,128)(2,1)S(1)} collective-permute-done((bf16[128,1024]{1,0:T(8,128)(2,1)S(1)}, bf16[128,1024]{1,0:T(8,128)(2,1)S(1)}, u32[]{:S(2)}, u32[]{:S(2)}) %collective-permute-start.8) | collective-permute-done | bytes 262176 | tf_op jit(solution)/shard_map/ppermute | solution.py:584
  70.9 0.5 shard_map.49.refs_1_
  71.5 1.6 %collective-permute-start.11 = (bf16[128,1024]{1,0:T(8,128)(2,1)S(1)}, bf16[128,1024]{1,0:T(8,128)(2,1)S(1)}, u32[]{:S(2)}, u32[]{:S(2)}) collective-permute-start(bf16[128,1024]{1,0:T(8,128)(2,1)S(1)} %shard_map.49.refs_1_), channel_id=1, source_target_pairs={{0,16},{8,24},{16,0},{24,8},{1,17},{9,25},{17,1},{25,9},{2,18},{10... | collective-permute-start | bytes 786440 | tf_op jit(solution)/shard_map/ppermute | solution.py:584
  73.1 9.2 %shard_map.50 = (bf16[4096,1024]{1,0:T(8,128)(2,1)S(1)}, f32[1024,4096]{1,0:T(8,128)}, f32[2,8,512]{2,1,0:T(8,128)S(1)}) custom-call(bf16[128,1024]{1,0:T(8,128)(2,1)S(1)} %shard_map.48.refs_0_, bf16[128,1024]{1,0:T(8,128)(2,1)S(1)} %shard_map.49.refs_1_, bf16[128,1024]{1,0:T(8,128)(2,1)S(1)} %collective-permute-done.9.refs_2_, ...), custom_call_target="tpu_custom_call", output_to_operand_aliasing={{0}: (4, {})} | custom-call | flops 4294967296 | bytes 16777216 | tf_op jit(solution)/shard_map/pallas_call | solution.py:218
  82.3 0.2 collective-permute-start.12
  82.5 0.3 collective-permute-start.13
  82.9 1.0 collective-permute-done.12.refs_2_
  83.9 0.4 collective-permute-done.13.refs_3_
  84.3 8.9 %shard_map.53 = (bf16[4096,1024]{1,0:T(8,128)(2,1)S(1)}, f32[1024,4096]{1,0:T(8,128)}, f32[2,8,512]{2,1,0:T(8,128)S(1)}) custom-call(bf16[128,1024]{1,0:T(8,128)(2,1)S(1)} %shard_map.51.refs_0_, bf16[128,1024]{1,0:T(8,128)(2,1)S(1)} %shard_map.52.refs_1_, ...), custom_call_target="tpu_custom_call", output_to_operand_aliasing={{0}: (4, {}), {1}: (5, {})} | custom-call | flops 4294967296 | bytes 16777216 | tf_op jit(solution)/shard_map/pallas_call | solution.py:218
  93.2 1.6 %collective-permute-start.14 = (f32[2,8,512]{2,1,0:T(8,128)S(1)}, f32[2,8,512]{2,1,0:T(8,128)S(1)}, u32[]{:S(2)}, u32[]{:S(2)}) collective-permute-start(f32[2,8,512]{2,1,0:T(8,128)S(1)} %shard_map.54.refs_0_), channel_id=1, source_target_pairs={{0,1},{1,0},{2,3},{3,2},{4,5},{5,4},{6,7},{7,6},{8,9},{9,8},{10,11... | collective-permute-start | bytes 98312 | tf_op jit(solution)/shard_map/ppermute | solution.py:597
  94.8 2.4 %collective-permute-done.14.refs_1_ = f32[2,8,512]{2,1,0:T(8,128)S(1)} collective-permute-done((f32[2,8,512]{2,1,0:T(8,128)S(1)}, f32[2,8,512]{2,1,0:T(8,128)S(1)}, u32[]{:S(2)}, u32[]{:S(2)}) %collective-permute-start.14) | collective-permute-done | bytes 32800 | tf_op jit(solution)/shard_map/ppermute | solution.py:597
  97.2 1.5 %collective-permute-start.17 = (f32[2,8,512]{2,1,0:T(8,128)S(1)}, f32[2,8,512]{2,1,0:T(8,128)S(1)}, u32[]{:S(2)}, u32[]{:S(2)}) collective-permute-start(f32[2,8,512]{2,1,0:T(8,128)S(1)} %shard_map.55.refs_0_.refs_8_), channel_id=1, source_target_pairs={{0,6},{1,7},{2,4},{3,5},{4,2},{5,3},{6,0},{7,1},{8,14},{9,15},{10,... | collective-permute-start | bytes 98312 | tf_op jit(solution)/shard_map/ppermute | solution.py:597
  98.8 0.6 collective-permute-start.16
  99.4 2.3 %collective-permute-start.15 = (f32[2,8,512]{2,1,0:T(8,128)S(1)}, f32[2,8,512]{2,1,0:T(8,128)S(1)}, u32[]{:S(2)}, u32[]{:S(2)}) collective-permute-start(f32[2,8,512]{2,1,0:T(8,128)S(1)} %shard_map.55.refs_0_.refs_8_), channel_id=1, source_target_pairs={{0,2},{1,3},{2,0},{3,1},{4,6},{5,7},{6,4},{7,5},{8,10},{9,11},{10,... | collective-permute-start | bytes 98312 | tf_op jit(solution)/shard_map/ppermute | solution.py:597
  101.7 1.3 %collective-permute-done.17.refs_3_ = f32[2,8,512]{2,1,0:T(8,128)S(1)} collective-permute-done((f32[2,8,512]{2,1,0:T(8,128)S(1)}, f32[2,8,512]{2,1,0:T(8,128)S(1)}, u32[]{:S(2)}, u32[]{:S(2)}) %collective-permute-start.17) | collective-permute-done | bytes 32800 | tf_op jit(solution)/shard_map/ppermute | solution.py:597
  103.0 0.7 collective-permute-done.16.refs_2_
  103.7 0.2 collective-permute-done.15.refs_1_
  103.9 8.5 %shard_map.56 = (f32[1,1032,256]{2,1,0:T(8,128)S(1)}, f32[1,1032,256]{2,1,0:T(8,128)S(1)}, bf16[4096,1024]{1,0:T(8,128)(2,1)S(1)}, bf16[1024,4096]{1,0:T(8,128)(2,1)S(1)}, f32[1,1024]{1,0:T(1,128)S(1)}) custom-call(f32[2,8,512]{2,1,0:T(8,128)S(1)} %shard_map.55.refs_0_.refs_8_, ...), custom_call_target="tpu_custom_call", output_to_operand_aliasing={{2}: (7, {})} | custom-call | flops 4294967296 | bytes 20971520 | tf_op jit(solution)/shard_map/pallas_call | solution.py:413
  112.5 2.4 %shard_map.57 = (f32[1,1032,256]{2,1,0:T(8,128)S(1)}, bf16[1024,4096]{1,0:T(8,128)(2,1)S(1)}, bf16[4096,1024]{1,0:T(8,128)(2,1)S(1)}) custom-call(bf16[1024,4096]{1,0:T(8,128)(2,1)S(1)} %get-tuple-element.51.kept_ref, f32[1,1024]{1,0:T(1,128)S(1)} %get-tuple-element.52.mass_ref, ...), custom_call_target="tpu_custom_call", output_to_operand_aliasing={{1}: (0, {}), {2}: (2, {})} | custom-call | flops 2147483648 | bytes 10485760 | tf_op jit(solution)/shard_map/pallas_call | solution.py:374
  114.9 0.5 collective-permute-start.19
  115.4 0.8 shard_map.58._.refs_1_
  116.2 1.5 %collective-permute-start.20 = (bf16[1040,256]{1,0:T(8,128)(2,1)S(1)}, bf16[1040,256]{1,0:T(8,128)(2,1)S(1)}, u32[]{:S(2)}, u32[]{:S(2)}) collective-permute-start(bf16[1040,256]{1,0:T(8,128)(2,1)S(1)} %bitcast.10), channel_id=1, source_target_pairs={{0,16},{8,24},{16,0},{24,8},{1,17},{9,25},{17,1},{25,9},{2,18},{10... | collective-permute-start | bytes 1597448 | tf_op jit(solution)/shard_map/ppermute | solution.py:584
  117.8 0.6 copy.18
  118.4 2.4 %shard_map.59 = (f32[1,1032,256]{2,1,0:T(8,128)S(1)}, bf16[1024,4096]{1,0:T(8,128)(2,1)S(1)}, bf16[4096,1024]{1,0:T(8,128)(2,1)S(1)}) custom-call(bf16[1024,4096]{1,0:T(8,128)(2,1)S(1)} %get-tuple-element.55.kept_ref, f32[1,1024]{1,0:T(1,128)S(1)} %get-tuple-element.52.mass_ref, ...), custom_call_target="tpu_custom_call", output_to_operand_aliasing={{1}: (0, {}), {2}: (2, {})} | custom-call | flops 2147483648 | bytes 10485760 | tf_op jit(solution)/shard_map/pallas_call | solution.py:374
  120.8 9.5 %collective-permute-done.20.refs_0_ = bf16[1040,256]{1,0:T(8,128)(2,1)S(1)} collective-permute-done((bf16[1040,256]{1,0:T(8,128)(2,1)S(1)}, bf16[1040,256]{1,0:T(8,128)(2,1)S(1)}, u32[]{:S(2)}, u32[]{:S(2)}) %collective-permute-start.20) | collective-permute-done | bytes 532512 | tf_op jit(solution)/shard_map/ppermute | solution.py:584
  130.3 2.0 %shard_map.60 = f32[1024,256]{1,0:T(8,128)} custom-call(f32[1032,256]{1,0:T(8,128)S(1)} %bitcast.17, f32[1032,256]{1,0:T(8,128)S(1)} %bitcast.16, bf16[1040,256]{1,0:T(8,128)(2,1)S(1)} %collective-permute-done.20.refs_0_, bf16[1,1040,256]{2,1,0:T(8,128)(2,1)S(1)} %shard_map.58._.refs_1_), custom_call_target="tpu_custom_call" | custom-call | flops 7864320 | bytes 3670016 | tf_op jit(solution)/shard_map/pallas_call | solution.py:526
  (19 shorter events, 0.3 us)
Async XLA Ops:
  3.2 2.2 %copy-start = (f32[1024,1024]{1,0:T(8,128)S(1)}, f32[1024,1024]{1,0:T(8,128)}, u32[]{:S(2)}) copy-start(f32[1024,1024]{1,0:T(8,128)} %c_hbm.1) | copy-start | bytes 12582916
  23.4 4.9 %collective-permute-start = (f32[2,8,512]{2,1,0:T(8,128)S(1)}, f32[2,8,512]{2,1,0:T(8,128)S(1)}, u32[]{:S(2)}, u32[]{:S(2)}) collective-permute-start(f32[2,8,512]{2,1,0:T(8,128)S(1)} %get-tuple-element.33.refs_0_.refs_4_), channel_id=1, source_target_pairs={{0,1},{1,0},{2,3},{3,2},{4,5},{5,4},{6,7},{7,6},{8,9},{9,8},{10,11... | collective-permute-start | bytes 98312 | tf_op jit(solution)/shard_map/ppermute | solution.py:597
  28.3 6.1 %collective-permute-start.3 = (f32[2,8,512]{2,1,0:T(8,128)S(1)}, f32[2,8,512]{2,1,0:T(8,128)S(1)}, u32[]{:S(2)}, u32[]{:S(2)}) collective-permute-start(f32[2,8,512]{2,1,0:T(8,128)S(1)} %shard_map.43.refs_0_.refs_7_), channel_id=1, source_target_pairs={{0,6},{1,7},{2,4},{3,5},{4,2},{5,3},{6,0},{7,1},{8,14},{9,15},{10,... | collective-permute-start | bytes 98312 | tf_op jit(solution)/shard_map/ppermute | solution.py:597
  32.5 4.8 %collective-permute-start.2 = (f32[2,8,512]{2,1,0:T(8,128)S(1)}, f32[2,8,512]{2,1,0:T(8,128)S(1)}, u32[]{:S(2)}, u32[]{:S(2)}) collective-permute-start(f32[2,8,512]{2,1,0:T(8,128)S(1)} %shard_map.43.refs_0_.refs_7_), channel_id=1, source_target_pairs={{0,4},{1,5},{2,6},{3,7},{4,0},{5,1},{6,2},{7,3},{8,12},{9,13},{10,... | collective-permute-start | bytes 98312 | tf_op jit(solution)/shard_map/ppermute | solution.py:597
  32.5 4.8 %collective-permute-start.1 = (f32[2,8,512]{2,1,0:T(8,128)S(1)}, f32[2,8,512]{2,1,0:T(8,128)S(1)}, u32[]{:S(2)}, u32[]{:S(2)}) collective-permute-start(f32[2,8,512]{2,1,0:T(8,128)S(1)} %shard_map.43.refs_0_.refs_7_), channel_id=1, source_target_pairs={{0,2},{1,3},{2,0},{3,1},{4,6},{5,7},{6,4},{7,5},{8,10},{9,11},{10,... | collective-permute-start | bytes 98312 | tf_op jit(solution)/shard_map/ppermute | solution.py:597
  44.3 5.0 %collective-permute-start.4 = (f32[1,264,1024]{2,1,0:T(8,128)S(1)}, f32[1,264,1024]{2,1,0:T(8,128)S(1)}, u32[]{:S(2)}, u32[]{:S(2)}) collective-permute-start(f32[1,264,1024]{2,1,0:T(8,128)S(1)} %get-tuple-element.37.refs_7_), channel_id=1, source_target_pairs={{0,8},{8,0},{16,24},{24,16},{1,9},{9,1},{17,25},{25,17},{2,10},{10... | collective-permute-start | bytes 3244040 | tf_op jit(solution)/shard_map/ppermute | solution.py:580
  48.7 7.7 %collective-permute-start.5 = (f32[1,264,1024]{2,1,0:T(8,128)S(1)}, f32[1,264,1024]{2,1,0:T(8,128)S(1)}, u32[]{:S(2)}, u32[]{:S(2)}) collective-permute-start(f32[1,264,1024]{2,1,0:T(8,128)S(1)} %get-tuple-element.40.after_ref), channel_id=1, source_target_pairs={{0,8},{8,0},{16,24},{24,16},{1,9},{9,1},{17,25},{25,17},{2,10},{10... | collective-permute-start | bytes 3244040 | tf_op jit(solution)/shard_map/ppermute | solution.py:580
  50.0 9.9 %collective-permute-start.6 = (bf16[144,1024]{1,0:T(8,128)(2,1)S(1)}, bf16[144,1024]{1,0:T(8,128)(2,1)S(1)}, u32[]{:S(2)}, u32[]{:S(2)}) collective-permute-start(bf16[144,1024]{1,0:T(8,128)(2,1)S(1)} %bitcast.15), channel_id=1, source_target_pairs={{0,16},{8,24},{16,0},{24,8},{1,17},{9,25},{17,1},{25,9},{2,18},{10... | collective-permute-start | bytes 884744 | tf_op jit(solution)/shard_map/ppermute | solution.py:584
  51.5 14.7 %collective-permute-start.7 = (bf16[144,1024]{1,0:T(8,128)(2,1)S(1)}, bf16[144,1024]{1,0:T(8,128)(2,1)S(1)}, u32[]{:S(2)}, u32[]{:S(2)}) collective-permute-start(bf16[144,1024]{1,0:T(8,128)(2,1)S(1)} %bitcast.20), channel_id=1, source_target_pairs={{0,16},{8,24},{16,0},{24,8},{1,17},{9,25},{17,1},{25,9},{2,18},{10... | collective-permute-start | bytes 884744 | tf_op jit(solution)/shard_map/ppermute | solution.py:584
  60.4 10.5 %collective-permute-start.8 = (bf16[128,1024]{1,0:T(8,128)(2,1)S(1)}, bf16[128,1024]{1,0:T(8,128)(2,1)S(1)}, u32[]{:S(2)}, u32[]{:S(2)}) collective-permute-start(bf16[128,1024]{1,0:T(8,128)(2,1)S(1)} %shard_map.48.refs_0_), channel_id=1, source_target_pairs={{0,16},{8,24},{16,0},{24,8},{1,17},{9,25},{17,1},{25,9},{2,18},{10... | collective-permute-start | bytes 786440 | tf_op jit(solution)/shard_map/ppermute | solution.py:584
  62.0 11.1 %collective-permute-start.9 = (bf16[128,1024]{1,0:T(8,128)(2,1)S(1)}, bf16[128,1024]{1,0:T(8,128)(2,1)S(1)}, u32[]{:S(2)}, u32[]{:S(2)}) collective-permute-start(bf16[128,1024]{1,0:T(8,128)(2,1)S(1)} %shard_map.48.refs_0_), channel_id=1, source_target_pairs={{0,8},{8,0},{16,24},{24,16},{1,9},{9,1},{17,25},{25,17},{2,10},{10... | collective-permute-start | bytes 786440 | tf_op jit(solution)/shard_map/ppermute | solution.py:580
  71.4 1.7 %collective-permute-start.10 = (bf16[128,1024]{1,0:T(8,128)(2,1)S(1)}, bf16[128,1024]{1,0:T(8,128)(2,1)S(1)}, u32[]{:S(2)}, u32[]{:S(2)}) collective-permute-start(bf16[128,1024]{1,0:T(8,128)(2,1)S(1)} %shard_map.49.refs_1_), channel_id=1, source_target_pairs={{0,8},{8,0},{16,24},{24,16},{1,9},{9,1},{17,25},{25,17},{2,10},{10... | collective-permute-start | bytes 786440 | tf_op jit(solution)/shard_map/ppermute | solution.py:580
  71.5 11.0 %collective-permute-start.11 = (bf16[128,1024]{1,0:T(8,128)(2,1)S(1)}, bf16[128,1024]{1,0:T(8,128)(2,1)S(1)}, u32[]{:S(2)}, u32[]{:S(2)}) collective-permute-start(bf16[128,1024]{1,0:T(8,128)(2,1)S(1)} %shard_map.49.refs_1_), channel_id=1, source_target_pairs={{0,16},{8,24},{16,0},{24,8},{1,17},{9,25},{17,1},{25,9},{2,18},{10... | collective-permute-start | bytes 786440 | tf_op jit(solution)/shard_map/ppermute | solution.py:584
  82.3 1.6 %collective-permute-start.12 = (bf16[128,1024]{1,0:T(8,128)(2,1)S(1)}, bf16[128,1024]{1,0:T(8,128)(2,1)S(1)}, u32[]{:S(2)}, u32[]{:S(2)}) collective-permute-start(bf16[128,1024]{1,0:T(8,128)(2,1)S(1)} %shard_map.51.refs_0_), channel_id=1, source_target_pairs={{0,8},{8,0},{16,24},{24,16},{1,9},{9,1},{17,25},{25,17},{2,10},{10... | collective-permute-start | bytes 786440 | tf_op jit(solution)/shard_map/ppermute | solution.py:580
  82.5 1.7 %collective-permute-start.13 = (bf16[128,1024]{1,0:T(8,128)(2,1)S(1)}, bf16[128,1024]{1,0:T(8,128)(2,1)S(1)}, u32[]{:S(2)}, u32[]{:S(2)}) collective-permute-start(bf16[128,1024]{1,0:T(8,128)(2,1)S(1)} %shard_map.52.refs_1_), channel_id=1, source_target_pairs={{0,8},{8,0},{16,24},{24,16},{1,9},{9,1},{17,25},{25,17},{2,10},{10... | collective-permute-start | bytes 786440 | tf_op jit(solution)/shard_map/ppermute | solution.py:580
  93.2 4.0 %collective-permute-start.14 = (f32[2,8,512]{2,1,0:T(8,128)S(1)}, f32[2,8,512]{2,1,0:T(8,128)S(1)}, u32[]{:S(2)}, u32[]{:S(2)}) collective-permute-start(f32[2,8,512]{2,1,0:T(8,128)S(1)} %shard_map.54.refs_0_), channel_id=1, source_target_pairs={{0,1},{1,0},{2,3},{3,2},{4,5},{5,4},{6,7},{7,6},{8,9},{9,8},{10,11... | collective-permute-start | bytes 98312 | tf_op jit(solution)/shard_map/ppermute | solution.py:597
  97.2 5.8 %collective-permute-start.17 = (f32[2,8,512]{2,1,0:T(8,128)S(1)}, f32[2,8,512]{2,1,0:T(8,128)S(1)}, u32[]{:S(2)}, u32[]{:S(2)}) collective-permute-start(f32[2,8,512]{2,1,0:T(8,128)S(1)} %shard_map.55.refs_0_.refs_8_), channel_id=1, source_target_pairs={{0,6},{1,7},{2,4},{3,5},{4,2},{5,3},{6,0},{7,1},{8,14},{9,15},{10,... | collective-permute-start | bytes 98312 | tf_op jit(solution)/shard_map/ppermute | solution.py:597
  98.8 4.9 %collective-permute-start.16 = (f32[2,8,512]{2,1,0:T(8,128)S(1)}, f32[2,8,512]{2,1,0:T(8,128)S(1)}, u32[]{:S(2)}, u32[]{:S(2)}) collective-permute-start(f32[2,8,512]{2,1,0:T(8,128)S(1)} %shard_map.55.refs_0_.refs_8_), channel_id=1, source_target_pairs={{0,4},{1,5},{2,6},{3,7},{4,0},{5,1},{6,2},{7,3},{8,12},{9,13},{10,... | collective-permute-start | bytes 98312 | tf_op jit(solution)/shard_map/ppermute | solution.py:597
  99.4 4.5 %collective-permute-start.15 = (f32[2,8,512]{2,1,0:T(8,128)S(1)}, f32[2,8,512]{2,1,0:T(8,128)S(1)}, u32[]{:S(2)}, u32[]{:S(2)}) collective-permute-start(f32[2,8,512]{2,1,0:T(8,128)S(1)} %shard_map.55.refs_0_.refs_8_), channel_id=1, source_target_pairs={{0,2},{1,3},{2,0},{3,1},{4,6},{5,7},{6,4},{7,5},{8,10},{9,11},{10,... | collective-permute-start | bytes 98312 | tf_op jit(solution)/shard_map/ppermute | solution.py:597
  112.4 3.0 %collective-permute-start.18 = (f32[1,1032,256]{2,1,0:T(8,128)S(1)}, f32[1,1032,256]{2,1,0:T(8,128)S(1)}, u32[]{:S(2)}, u32[]{:S(2)}) collective-permute-start(f32[1,1032,256]{2,1,0:T(8,128)S(1)} %get-tuple-element.54._), channel_id=1, source_target_pairs={{0,8},{8,0},{16,24},{24,16},{1,9},{9,1},{17,25},{25,17},{2,10},{10... | collective-permute-start | bytes 3170312 | tf_op jit(solution)/shard_map/ppermute | solution.py:580
  114.9 5.9 %collective-permute-start.19 = (f32[1,1032,256]{2,1,0:T(8,128)S(1)}, f32[1,1032,256]{2,1,0:T(8,128)S(1)}, u32[]{:S(2)}, u32[]{:S(2)}) collective-permute-start(f32[1,1032,256]{2,1,0:T(8,128)S(1)} %get-tuple-element.58.after_ref), channel_id=1, source_target_pairs={{0,8},{8,0},{16,24},{24,16},{1,9},{9,1},{17,25},{25,17},{2,10},{10... | collective-permute-start | bytes 3170312 | tf_op jit(solution)/shard_map/ppermute | solution.py:580
  116.2 14.1 %collective-permute-start.20 = (bf16[1040,256]{1,0:T(8,128)(2,1)S(1)}, bf16[1040,256]{1,0:T(8,128)(2,1)S(1)}, u32[]{:S(2)}, u32[]{:S(2)}) collective-permute-start(bf16[1040,256]{1,0:T(8,128)(2,1)S(1)} %bitcast.10), channel_id=1, source_target_pairs={{0,16},{8,24},{16,0},{24,8},{1,17},{9,25},{17,1},{25,9},{2,18},{10... | collective-permute-start | bytes 1597448 | tf_op jit(solution)/shard_map/ppermute | solution.py:584

commit v2 on v1

--- a/solution.py
+++ b/solution.py
@@ -75,45 +75,26 @@
     return jnp.where(wide < 0.0, -steps, steps) * (scale * (1.0 / LEVELS))
 
 
-def load_body(c_hbm, sums_ref, x_hbm, x_ref, units_ref, rows_ref, row_sems, point_sem):
-    row_step = rows_ref.shape[0] // row_sems.shape[0]
-
-    def rows_of(number):
-        part = pl.ds(number * row_step, row_step)
-        return pltpu.make_async_copy(c_hbm.at[part, :], rows_ref.at[part, :], row_sems.at[number])
-
-    all_points = pltpu.make_async_copy(x_hbm, x_ref, point_sem)
-    for number in range(row_sems.shape[0]):
-        rows_of(number).start()
-    all_points.start()
-    for number in range(row_sems.shape[0]):
-        rows_of(number).wait()
-        part = slice(number * row_step, (number + 1) * row_step)
-        scale = to_column(lax.rsqrt(sums_ref[:, part] + 1e-06), row_step)[:, 0:1]
-        units_ref[part, :] = (rows_ref[part, :] * scale).astype(BF16)
-    all_points.wait()
-
-
-def load(centroids, points):
+def first_units_body(c_ref, sums_ref, units_ref):
+    step = divisor(units_ref.shape[0], 128)
+    for start in range(0, units_ref.shape[0], step):
+        part = slice(start, start + step)
+        scale = to_column(lax.rsqrt(sums_ref[:, part] + 1e-06), step)[:, 0:1]
+        units_ref[part, :] = (c_ref[part, :] * scale).astype(BF16)
+
+
+def first_units(centroids):
     square_sums = jnp.sum(centroids * centroids, axis=1)[None]
     return pl.pallas_call(
-        load_body,
-        in_specs=[ANY, VMEM, ANY],
-        out_specs=[VMEM] * 2,
-        out_shape=[
-            jax.ShapeDtypeStruct(points.shape, BF16),
-            jax.ShapeDtypeStruct(centroids.shape, BF16),
-        ],
-        scratch_shapes=[
-            pltpu.VMEM(centroids.shape, F32),
-            pltpu.SemaphoreType.DMA((divisor(centroids.shape[0] // 16, 4),)),
-            pltpu.SemaphoreType.DMA(()),
-        ],
-        compiler_params=params(LOAD_VMEM),
+        first_units_body,
+        in_specs=[VMEM, VMEM],
+        out_specs=VMEM,
+        out_shape=jax.ShapeDtypeStruct(centroids.shape, BF16),
+        compiler_params=params(10),
         cost_estimate=pl.CostEstimate(
-            flops=4 * centroids.size, bytes_accessed=4 * centroids.size + 2 * points.size, transcendentals=0
+            flops=4 * centroids.size, bytes_accessed=4 * centroids.size, transcendentals=0
         ),
-    )(centroids, square_sums, points)
+    )(centroids, square_sums)
 
 
 def score_points(raw, units, x_ref, e_parts, stat_ref, stage, semaphores):
@@ -168,7 +149,7 @@
     return (2, total // line, line)
 
 
-def first_scores_body(raw, units, x_ref, _, e_hbm, stat_ref, stage, semaphores):
+def first_scores_body(raw, units, x_ref, e_hbm, stat_ref, stage, semaphores):
     target = [(slice(None), lambda columns: e_hbm.at[:, columns])]
     score_points(raw, units, x_ref, target, stat_ref, stage, semaphores)
 
@@ -218,13 +199,12 @@
     return pl.pallas_call(
         body,
         in_specs=[VMEM] * (count + 1) + [ANY] * len(more),
-        out_specs=[VMEM, ANY, VMEM],
+        out_specs=[ANY, VMEM],
         out_shape=[
-            jax.ShapeDtypeStruct(points.shape, BF16),
             jax.ShapeDtypeStruct((all_rows, total), F32),
             jax.ShapeDtypeStruct(stat, F32),
         ],
-        input_output_aliases={count + number: number for number in range(1 + len(more))},
+        input_output_aliases={count + 1: 0} if more else {},
         scratch_shapes=scratch,
         compiler_params=params(SCORE_VMEM),
         cost_estimate=pl.CostEstimate(
@@ -242,7 +222,7 @@
     parts = CORES if kind == FAR else 1
     stat_refs, refs = refs[:n_sets], refs[n_sets:]
     top_refs, (e_hbm, x_ref, _), refs = refs[:n_tops], refs[n_tops : n_tops + 3], refs[n_tops + 3 :]
-    out_refs, refs = refs[:parts], refs[parts + 1 :]
+    out_refs, refs = refs[:parts], refs[parts:]
     if not by_rows:
         (kept_ref, kept_mass_ref), refs = refs[:2], refs[2:]
     scale_refs, refs = refs[:2], refs[2:]
@@ -357,7 +337,7 @@
                 ]
 
 
-def weigh_kept_body(kind, extra, kept_ref, mass_ref, x_ref, _, out_ref, kept_out, x_out, sum_ref):
+def weigh_kept_body(kind, extra, kept_ref, mass_ref, x_ref, _, out_ref, kept_out, sum_ref):
     chip, core = place()
     span = sum_ref.shape[1]
     total = x_ref.shape[0]
@@ -374,13 +354,12 @@
     return pl.pallas_call(
         functools.partial(weigh_kept_body, kind, extra),
         in_specs=[VMEM] * 3 + [ANY],
-        out_specs=[VMEM] * 3,
-        input_output_aliases={0: 1, 2: 2},
+        out_specs=[VMEM] * 2,
+        input_output_aliases={0: 1},
         scratch_shapes=[pltpu.VMEM((rows, cols), F32)],
         out_shape=[
             jax.ShapeDtypeStruct((1, rows + extra, cols), F32),
             jax.ShapeDtypeStruct(kept.shape, BF16),
-            jax.ShapeDtypeStruct(points.shape, BF16),
         ],
         compiler_params=params(KEPT_VMEM),
         cost_estimate=pl.CostEstimate(
@@ -413,8 +392,7 @@
     return pl.pallas_call(
         functools.partial(weigh_body, by_rows, len(stats), n_tops, kind, others, extra, pair),
         in_specs=[VMEM] * (len(stats) + n_tops) + [ANY, VMEM, ANY],
-        out_specs=[VMEM] * (parts + (1 if by_rows else 3)),
-        input_output_aliases={len(stats) + n_tops + 1: parts},
+        out_specs=[VMEM] * (parts + len(kept)),
         scratch_shapes=[pltpu.VMEM(stats[0].shape[1:], F32)] * 2
         + [pltpu.VMEM((sums[0], chunk), BF16)] * (2 if by_rows else 0)
         + [
@@ -424,7 +402,6 @@
             pltpu.SemaphoreType.DMA((slots,)),
         ],
         out_shape=[jax.ShapeDtypeStruct((others, rows + extra, cols), F32)] * parts
-        + [jax.ShapeDtypeStruct(points.shape, BF16)]
         + kept,
         compiler_params=params(WEIGH_VMEM),
         cost_estimate=pl.CostEstimate(
@@ -598,18 +575,17 @@
             done *= ways
         return sets
 
-    def sums_over_pts(by_rows, stats, tops, shifted, points):
+    def sums_over_pts(by_rows, stats, tops, shifted):
         kept = mass = None
 
         def weighted(kind, after):
-            nonlocal points, kept, mass
+            nonlocal kept, mass
             if by_rows:
-                *found, points = weigh(by_rows, kind, chips, stats, tops, shifted, points, after)
+                return weigh(by_rows, kind, chips, stats, tops, shifted, points, after)
+            if kind == FAR:
+                *found, kept, mass = weigh(by_rows, kind, chips, stats, tops, shifted, points, after)
                 return found
-            if kind == FAR:
-                *found, points, kept, mass = weigh(by_rows, kind, chips, stats, tops, shifted, points, after)
-                return found
-            *found, kept, points = weigh_kept(kind, n_pts, kept, mass, points, after)
+            *found, kept = weigh_kept(kind, n_pts, kept, mass, points, after)
             return found
 
         far_mine, far_theirs = weighted(FAR, stats[0])
@@ -625,27 +601,26 @@
             if by_rows:
                 away_found.append([to_chip(found[-1], -away) for away in range(1, chips)])
                 after = away_found[-1][-1]
-        return found, away_found, points
-
-    block = centroids.shape[0] // n_pts
-    pieces = 2 if block % 256 == 0 else 1
-    points, units = load(centroids, points)
-    points, shifted, own = scores(ITERS > 1, [units], points)
+        return found, away_found
+
+    pieces = 1
+    units = first_units(centroids)
+    shifted, own = scores(ITERS > 1, [units], points)
     stats = over_centroids(own)
     tops = [own]
     for iteration in range(1, ITERS):
         raw = iteration + 1 < ITERS
-        mine, away_mine, points = sums_over_pts(True, stats, tops, shifted, points)
+        mine, away_mine = sums_over_pts(True, stats, tops, shifted)
         near_units = mine + [to_partner(unit) for unit in mine]
-        points, shifted, near_own = scores(raw, near_units, points, pieces, 0, shifted)
+        shifted, near_own = scores(raw, near_units, points, pieces, 0, shifted)
         far_units = []
         for units in zip(*away_mine):
             units = [keep_until(unit, near_own) for unit in units]
             far_units += units + [to_partner(unit) for unit in units]
-        points, shifted, far_own = scores(raw, far_units, points, pieces, 1, shifted)
+        shifted, far_own = scores(raw, far_units, points, pieces, 1, shifted)
         tops = [near_own, far_own]
         stats = over_centroids(merged([near_own, far_own]))
-    (means,), _, _ = sums_over_pts(False, stats, tops, shifted, points)
+    (means,), _ = sums_over_pts(False, stats, tops, shifted)
     return (means, log_norms(stats))
 
 

time: 133 us -> 128 us (0.962)
  Pallas kernels: 69.7 us -> 66.3 us
  starting transfers between devices: 22.5 us -> 19.9 us
    pallas_call x1, Pallas kernels: 3.7 us -> 0.43 us  [first_units(): pl.pallas_call(first_units_body, in_specs=[VMEM, VMEM], out_specs=VMEM, o...]
    ppermute x5 -> x3, starting transfers between devices: 6.78 us -> 4.7 us  [to_chip(): return lax.ppermute(value, 'pts', moves)]
    unnamed x3 -> x5, local copies, waits for them, and re-layouts: 2.8 us -> 3.38 us
    ppermute x5 -> x3, waiting for transfers between devices: 21.9 us -> 21.4 us  [to_chip(): return lax.ppermute(value, 'pts', moves)]
    pallas_call x3 -> x2, Pallas kernels: 3.07 us -> 2.98 us  [finish(): pl.pallas_call(functools.partial(finish_body, rows, lines, piece, as_unit...]
  transfers between devices with their start and end apart: 21 -> 17, of which waited for: 13 -> 12; matrix products, arithmetic and copies ran while one was open for 0% -> 0% of each run, Pallas kernels for 19% -> 19%
where the time goes in v2:
time: 128 us; the launch traced here: 127 us
  Pallas kernels  66.3 us (52%)
  waiting for transfers between devices  34.4 us (27%)
  starting transfers between devices  19.9 us (16%)
  local copies, waits for them, and re-layouts  3.38 us (3%)
  other arithmetic  2.68 us (2%)
    pallas_call x3, Pallas kernels, scores(): pl.pallas_call(body, in_specs=[VMEM] * (count + 1) + [ANY] * len(more), o...  32.5 us
    pallas_call x4, Pallas kernels, weigh(): pl.pallas_call(functools.partial(weigh_body, by_rows, len(stats), n_tops,...  24.2 us
    ppermute x3, waiting for transfers between devices, to_chip(): return lax.ppermute(value, 'pts', moves)  21.4 us
    ppermute x8, starting transfers between devices, over_centroids(): sets.append(lax.ppermute(sets[0], 'cen', moves))  13.9 us
    ppermute x8, waiting for transfers between devices, over_centroids(): sets.append(lax.ppermute(sets[0], 'cen', moves))  10.7 us
    pallas_call x2, Pallas kernels, weigh_kept(): pl.pallas_call(functools.partial(weigh_kept_body, kind, extra), in_specs=...  4.74 us
    ppermute x3, starting transfers between devices, to_chip(): return lax.ppermute(value, 'pts', moves)  4.7 us
    unnamed x5, local copies, waits for them, and re-layouts  3.38 us
  transfers between devices with their start and end apart: 17, of which 12 were waited for; matrix products, arithmetic and copies ran while one was open for 0% of the time, Pallas kernels for 19%

profile of v2, /device:TPU:0, one launch (start us, length us, event | category | flops | bytes accessed | tf_op | source)
XLA Modules:
  0.0 127.4 jit_solution(1739243513179576344)
XLA Ops:
  0.6 2.7 %multiply_reduce_fusion = f32[1024]{0:T(1024)S(1)} fusion(f32[1024,1024]{1,0:T(8,128)} %c_ref.1), kind=kLoop, calls=%fused_computation | loop fusion | flops 2096128 | bytes 4198400 | tf_op jit(solution)/shard_map/reduce_sum | solution.py:87
  3.3 0.0 copy-start.1
  3.3 2.6 %copy-done.1 = f32[1024,1024]{1,0:T(8,128)S(1)} copy-done((f32[1024,1024]{1,0:T(8,128)S(1)}, f32[1024,1024]{1,0:T(8,128)}, u32[]{:S(2)}) %copy-start.1) | copy-done | bytes 4194328
  5.9 0.4 shard_map.41.units
  6.3 0.2 copy-done
  6.5 14.3 %shard_map.42 = (f32[1024,4096]{1,0:T(8,128)}, f32[2,8,512]{2,1,0:T(8,128)S(1)}) custom-call(bf16[1024,1024]{1,0:T(8,128)(2,1)S(1)} %shard_map.41.units, bf16[4096,1024]{1,0:T(8,128)(2,1)S(1)} %copy-done), custom_call_target="tpu_custom_call" | custom-call | flops 8589934592 | bytes 25165824 | tf_op jit(solution)/shard_map/pallas_call | solution.py:199
  20.9 3.0 %collective-permute-start = (f32[2,8,512]{2,1,0:T(8,128)S(1)}, f32[2,8,512]{2,1,0:T(8,128)S(1)}, u32[]{:S(2)}, u32[]{:S(2)}) collective-permute-start(f32[2,8,512]{2,1,0:T(8,128)S(1)} %get-tuple-element.17.refs_0_.refs_4_), channel_id=1, source_target_pairs={{0,1},{1,0},{2,3},{3,2},{4,5},{5,4},{6,7},{7,6},{8,9},{9,8},{10,11... | collective-permute-start | bytes 98312 | tf_op jit(solution)/shard_map/ppermute | solution.py:574
  23.9 1.9 %collective-permute-done.refs_1_ = f32[2,8,512]{2,1,0:T(8,128)S(1)} collective-permute-done((f32[2,8,512]{2,1,0:T(8,128)S(1)}, f32[2,8,512]{2,1,0:T(8,128)S(1)}, u32[]{:S(2)}, u32[]{:S(2)}) %collective-permute-start) | collective-permute-done | bytes 32800 | tf_op jit(solution)/shard_map/ppermute | solution.py:574
  25.8 4.2 %collective-permute-start.3 = (f32[2,8,512]{2,1,0:T(8,128)S(1)}, f32[2,8,512]{2,1,0:T(8,128)S(1)}, u32[]{:S(2)}, u32[]{:S(2)}) collective-permute-start(f32[2,8,512]{2,1,0:T(8,128)S(1)} %shard_map.43.refs_0_.refs_7_), channel_id=1, source_target_pairs={{0,6},{1,7},{2,4},{3,5},{4,2},{5,3},{6,0},{7,1},{8,14},{9,15},{10,... | collective-permute-start | bytes 98312 | tf_op jit(solution)/shard_map/ppermute | solution.py:574
  30.0 0.6 collective-permute-start.1
  30.7 1.3 %collective-permute-done.3.refs_3_ = f32[2,8,512]{2,1,0:T(8,128)S(1)} collective-permute-done((f32[2,8,512]{2,1,0:T(8,128)S(1)}, f32[2,8,512]{2,1,0:T(8,128)S(1)}, u32[]{:S(2)}, u32[]{:S(2)}) %collective-permute-start.3) | collective-permute-done | bytes 32800 | tf_op jit(solution)/shard_map/ppermute | solution.py:574
  31.9 2.9 %collective-permute-done.2.refs_2_ = f32[2,8,512]{2,1,0:T(8,128)S(1)} collective-permute-done((f32[2,8,512]{2,1,0:T(8,128)S(1)}, f32[2,8,512]{2,1,0:T(8,128)S(1)}, u32[]{:S(2)}, u32[]{:S(2)}) %collective-permute-start.2) | collective-permute-done | bytes 32800 | tf_op jit(solution)/shard_map/ppermute | solution.py:574
  34.8 0.0 collective-permute-done.1.refs_1_
  34.8 6.9 %shard_map.44 = (f32[1,264,1024]{2,1,0:T(8,128)S(1)}, f32[1,264,1024]{2,1,0:T(8,128)S(1)}) custom-call(f32[2,8,512]{2,1,0:T(8,128)S(1)} %shard_map.43.refs_0_.refs_7_, f32[2,8,512]{2,1,0:T(8,128)S(1)} %collective-permute-done.1.refs_1_, f32[2,8,512]{2,1,0:T(8,128)S(1)} %collective-permute-done.2.refs_2_, f32[2,8,512]{2,1,0:T(8,128)S(1)} %collective-permute-done.3.refs_3_, ...), custom_call_target="tpu_custom_call" | custom-call | flops 4294967296 | bytes 16777216 | tf_op jit(solution)/shard_map/pallas_call | solution.py:392
  41.8 0.1 collective-permute-start.4
  41.8 4.4 %shard_map.45.after_ref = f32[1,264,1024]{2,1,0:T(8,128)S(1)} custom-call(f32[2,8,512]{2,1,0:T(8,128)S(1)} %shard_map.43.refs_0_.refs_7_, f32[2,8,512]{2,1,0:T(8,128)S(1)} %collective-permute-done.1.refs_1_, f32[2,8,512]{2,1,0:T(8,128)S(1)} %collective-permute-done.2.refs_2_, f32[2,8,512]{2,1,0:T(8,128)S(1)} %collective-permute-done.3.refs_3_, ...), custom_call_target="tpu_custom_call" | custom-call | flops 2147483648 | bytes 12582912 | tf_op jit(solution)/shard_map/pallas_call | solution.py:392
  46.2 0.6 collective-permute-start.5
  46.8 0.7 shard_map.46.refs_7_.refs_1_
  47.5 1.6 %collective-permute-start.6 = (bf16[272,1024]{1,0:T(8,128)(2,1)S(1)}, bf16[272,1024]{1,0:T(8,128)(2,1)S(1)}, u32[]{:S(2)}, u32[]{:S(2)}) collective-permute-start(bf16[272,1024]{1,0:T(8,128)(2,1)S(1)} %bitcast.9), channel_id=1, source_target_pairs={{0,16},{8,24},{16,0},{24,8},{1,17},{9,25},{17,1},{25,9},{2,18},{10... | collective-permute-start | bytes 1671176 | tf_op jit(solution)/shard_map/ppermute | solution.py:561
  49.0 4.4 %shard_map.47 = f32[1,264,1024]{2,1,0:T(8,128)S(1)} custom-call(f32[2,8,512]{2,1,0:T(8,128)S(1)} %shard_map.43.refs_0_.refs_7_, f32[2,8,512]{2,1,0:T(8,128)S(1)} %collective-permute-done.1.refs_1_, f32[2,8,512]{2,1,0:T(8,128)S(1)} %collective-permute-done.2.refs_2_, f32[2,8,512]{2,1,0:T(8,128)S(1)} %collective-permute-done.3.refs_3_, ...), custom_call_target="tpu_custom_call" | custom-call | flops 2147483648 | bytes 12582912 | tf_op jit(solution)/shard_map/pallas_call | solution.py:392
  53.4 8.6 %collective-permute-done.6.refs_0_ = bf16[272,1024]{1,0:T(8,128)(2,1)S(1)} collective-permute-done((bf16[272,1024]{1,0:T(8,128)(2,1)S(1)}, bf16[272,1024]{1,0:T(8,128)(2,1)S(1)}, u32[]{:S(2)}, u32[]{:S(2)}) %collective-permute-start.6) | collective-permute-done | bytes 557088 | tf_op jit(solution)/shard_map/ppermute | solution.py:561
  62.1 0.9 shard_map.48.refs_0_
  63.0 0.1 collective-permute-start.7
  63.1 1.6 %collective-permute-start.8 = (bf16[256,1024]{1,0:T(8,128)(2,1)S(1)}, bf16[256,1024]{1,0:T(8,128)(2,1)S(1)}, u32[]{:S(2)}, u32[]{:S(2)}) collective-permute-start(bf16[256,1024]{1,0:T(8,128)(2,1)S(1)} %shard_map.48.refs_0_), channel_id=1, source_target_pairs={{0,16},{8,24},{16,0},{24,8},{1,17},{9,25},{17,1},{25,9},{2,18},{10... | collective-permute-start | bytes 1572872 | tf_op jit(solution)/shard_map/ppermute | solution.py:561
  64.7 0.3 collective-permute-done.7.refs_1_
  65.0 9.2 %shard_map.49 = (f32[1024,4096]{1,0:T(8,128)}, f32[2,8,512]{2,1,0:T(8,128)S(1)}) custom-call(bf16[256,1024]{1,0:T(8,128)(2,1)S(1)} %shard_map.48.refs_0_, bf16[256,1024]{1,0:T(8,128)(2,1)S(1)} %collective-permute-done.7.refs_1_, bf16[4096,1024]{1,0:T(8,128)(2,1)S(1)} %copy-done), custom_call_target="tpu_custom_call" | custom-call | flops 4294967296 | bytes 16777216 | tf_op jit(solution)/shard_map/pallas_call | solution.py:199
  74.2 3.3 %collective-permute-done.8.value_ref = bf16[256,1024]{1,0:T(8,128)(2,1)S(1)} collective-permute-done((bf16[256,1024]{1,0:T(8,128)(2,1)S(1)}, bf16[256,1024]{1,0:T(8,128)(2,1)S(1)}, u32[]{:S(2)}, u32[]{:S(2)}) %collective-permute-start.8) | collective-permute-done | bytes 524320 | tf_op jit(solution)/shard_map/ppermute | solution.py:561
  77.4 1.9 %collective-permute-done.9.refs_1_ = bf16[256,1024]{1,0:T(8,128)(2,1)S(1)} collective-permute-done((bf16[256,1024]{1,0:T(8,128)(2,1)S(1)}, bf16[256,1024]{1,0:T(8,128)(2,1)S(1)}, u32[]{:S(2)}, u32[]{:S(2)}) %collective-permute-start.9) | collective-permute-done | bytes 524320 | tf_op jit(solution)/shard_map/ppermute | solution.py:557
  79.4 8.9 %shard_map.51 = (f32[1024,4096]{1,0:T(8,128)}, f32[2,8,512]{2,1,0:T(8,128)S(1)}) custom-call(bf16[256,1024]{1,0:T(8,128)(2,1)S(1)} %shard_map.50.refs_0_, bf16[256,1024]{1,0:T(8,128)(2,1)S(1)} %collective-permute-done.9.refs_1_, bf16[4096,1024]{1,0:T(8,128)(2,1)S(1)} %copy-done, f32[1024,4096]{1,0:T(8,128)} %get-tuple-element.22.refs_3_), custom_call_target="tpu_custom_call", output_to_operand_aliasing={{0}: (3, {})} | custom-call | flops 4294967296 | bytes 16777216 | tf_op jit(solution)/shard_map/pallas_call | solution.py:199
  88.3 1.5 %collective-permute-start.10 = (f32[2,8,512]{2,1,0:T(8,128)S(1)}, f32[2,8,512]{2,1,0:T(8,128)S(1)}, u32[]{:S(2)}, u32[]{:S(2)}) collective-permute-start(f32[2,8,512]{2,1,0:T(8,128)S(1)} %shard_map.52.refs_0_), channel_id=1, source_target_pairs={{0,1},{1,0},{2,3},{3,2},{4,5},{5,4},{6,7},{7,6},{8,9},{9,8},{10,11... | collective-permute-start | bytes 98312 | tf_op jit(solution)/shard_map/ppermute | solution.py:574
  89.9 2.4 %collective-permute-done.10.refs_1_ = f32[2,8,512]{2,1,0:T(8,128)S(1)} collective-permute-done((f32[2,8,512]{2,1,0:T(8,128)S(1)}, f32[2,8,512]{2,1,0:T(8,128)S(1)}, u32[]{:S(2)}, u32[]{:S(2)}) %collective-permute-start.10) | collective-permute-done | bytes 32800 | tf_op jit(solution)/shard_map/ppermute | solution.py:574
  92.3 1.5 %collective-permute-start.13 = (f32[2,8,512]{2,1,0:T(8,128)S(1)}, f32[2,8,512]{2,1,0:T(8,128)S(1)}, u32[]{:S(2)}, u32[]{:S(2)}) collective-permute-start(f32[2,8,512]{2,1,0:T(8,128)S(1)} %shard_map.53.refs_0_.refs_8_), channel_id=1, source_target_pairs={{0,6},{1,7},{2,4},{3,5},{4,2},{5,3},{6,0},{7,1},{8,14},{9,15},{10,... | collective-permute-start | bytes 98312 | tf_op jit(solution)/shard_map/ppermute | solution.py:574
  93.9 0.6 collective-permute-start.12
  94.5 2.3 %collective-permute-start.11 = (f32[2,8,512]{2,1,0:T(8,128)S(1)}, f32[2,8,512]{2,1,0:T(8,128)S(1)}, u32[]{:S(2)}, u32[]{:S(2)}) collective-permute-start(f32[2,8,512]{2,1,0:T(8,128)S(1)} %shard_map.53.refs_0_.refs_8_), channel_id=1, source_target_pairs={{0,2},{1,3},{2,0},{3,1},{4,6},{5,7},{6,4},{7,5},{8,10},{9,11},{10,... | collective-permute-start | bytes 98312 | tf_op jit(solution)/shard_map/ppermute | solution.py:574
  96.8 1.3 %collective-permute-done.13.refs_3_ = f32[2,8,512]{2,1,0:T(8,128)S(1)} collective-permute-done((f32[2,8,512]{2,1,0:T(8,128)S(1)}, f32[2,8,512]{2,1,0:T(8,128)S(1)}, u32[]{:S(2)}, u32[]{:S(2)}) %collective-permute-start.13) | collective-permute-done | bytes 32800 | tf_op jit(solution)/shard_map/ppermute | solution.py:574
  98.1 0.7 collective-permute-done.12.refs_2_
  98.8 0.2 collective-permute-done.11.refs_1_
  99.0 8.5 %shard_map.54 = (f32[1,1032,256]{2,1,0:T(8,128)S(1)}, f32[1,1032,256]{2,1,0:T(8,128)S(1)}, bf16[1024,4096]{1,0:T(8,128)(2,1)S(1)}, f32[1,1024]{1,0:T(1,128)S(1)}) custom-call(f32[2,8,512]{2,1,0:T(8,128)S(1)} %shard_map.53.refs_0_.refs_8_, f32[2,8,512]{2,1,0:T(8,128)S(1)} %collective-permute-done.11.refs_1_, ...), custom_call_target="tpu_custom_call" | custom-call | flops 4294967296 | bytes 20971520 | tf_op jit(solution)/shard_map/pallas_call | solution.py:392
  107.5 0.1 collective-permute-start.14
  107.6 2.4 %shard_map.55 = (f32[1,1032,256]{2,1,0:T(8,128)S(1)}, bf16[1024,4096]{1,0:T(8,128)(2,1)S(1)}) custom-call(bf16[1024,4096]{1,0:T(8,128)(2,1)S(1)} %get-tuple-element.25.kept_ref, f32[1,1024]{1,0:T(1,128)S(1)} %get-tuple-element.26.mass_ref, bf16[4096,1024]{1,0:T(8,128)(2,1)S(1)} %copy-done, ...), custom_call_target="tpu_custom_call", output_to_operand_aliasing={{1}: (0, {})} | custom-call | flops 2147483648 | bytes 10485760 | tf_op jit(solution)/shard_map/pallas_call | solution.py:354
  110.0 0.5 collective-permute-start.15
  110.5 0.8 shard_map.56._.refs_1_
  111.3 1.6 %collective-permute-start.16 = (bf16[1040,256]{1,0:T(8,128)(2,1)S(1)}, bf16[1040,256]{1,0:T(8,128)(2,1)S(1)}, u32[]{:S(2)}, u32[]{:S(2)}) collective-permute-start(bf16[1040,256]{1,0:T(8,128)(2,1)S(1)} %bitcast.10), channel_id=1, source_target_pairs={{0,16},{8,24},{16,0},{24,8},{1,17},{9,25},{17,1},{25,9},{2,18},{10... | collective-permute-start | bytes 1597448 | tf_op jit(solution)/shard_map/ppermute | solution.py:561
  112.9 0.6 copy.8
  113.5 2.4 %shard_map.57 = (f32[1,1032,256]{2,1,0:T(8,128)S(1)}, bf16[1024,4096]{1,0:T(8,128)(2,1)S(1)}) custom-call(bf16[1024,4096]{1,0:T(8,128)(2,1)S(1)} %get-tuple-element.28.kept_ref, f32[1,1024]{1,0:T(1,128)S(1)} %get-tuple-element.26.mass_ref, bf16[4096,1024]{1,0:T(8,128)(2,1)S(1)} %copy-done, ...), custom_call_target="tpu_custom_call", output_to_operand_aliasing={{1}: (0, {})} | custom-call | flops 2147483648 | bytes 10485760 | tf_op jit(solution)/shard_map/pallas_call | solution.py:354
  115.9 0.0 collective-permute-done.15
  115.9 9.5 %collective-permute-done.16.refs_0_ = bf16[1040,256]{1,0:T(8,128)(2,1)S(1)} collective-permute-done((bf16[1040,256]{1,0:T(8,128)(2,1)S(1)}, bf16[1040,256]{1,0:T(8,128)(2,1)S(1)}, u32[]{:S(2)}, u32[]{:S(2)}) %collective-permute-start.16) | collective-permute-done | bytes 532512 | tf_op jit(solution)/shard_map/ppermute | solution.py:561
  125.4 2.0 %shard_map.58 = f32[1024,256]{1,0:T(8,128)} custom-call(f32[1032,256]{1,0:T(8,128)S(1)} %bitcast.14, f32[1032,256]{1,0:T(8,128)S(1)} %bitcast.13, bf16[1040,256]{1,0:T(8,128)(2,1)S(1)} %collective-permute-done.16.refs_0_, bf16[1,1040,256]{2,1,0:T(8,128)(2,1)S(1)} %shard_map.56._.refs_1_), custom_call_target="tpu_custom_call" | custom-call | flops 7864320 | bytes 3670016 | tf_op jit(solution)/shard_map/pallas_call | solution.py:503
  (11 shorter events, 0.1 us)
Async XLA Ops:
  0.6 5.9 %copy-start = (bf16[4096,1024]{1,0:T(8,128)(2,1)S(1)}, bf16[4096,1024]{1,0:T(8,128)(2,1)}, u32[]{:S(2)}) copy-start(bf16[4096,1024]{1,0:T(8,128)(2,1)} %x_ref.5) | copy-start | bytes 25165828
  3.3 2.6 %copy-start.1 = (f32[1024,1024]{1,0:T(8,128)S(1)}, f32[1024,1024]{1,0:T(8,128)}, u32[]{:S(2)}) copy-start(f32[1024,1024]{1,0:T(8,128)} %c_ref.1) | copy-start | bytes 12582916
  20.9 4.9 %collective-permute-start = (f32[2,8,512]{2,1,0:T(8,128)S(1)}, f32[2,8,512]{2,1,0:T(8,128)S(1)}, u32[]{:S(2)}, u32[]{:S(2)}) collective-permute-start(f32[2,8,512]{2,1,0:T(8,128)S(1)} %get-tuple-element.17.refs_0_.refs_4_), channel_id=1, source_target_pairs={{0,1},{1,0},{2,3},{3,2},{4,5},{5,4},{6,7},{7,6},{8,9},{9,8},{10,11... | collective-permute-start | bytes 98312 | tf_op jit(solution)/shard_map/ppermute | solution.py:574
  25.8 6.1 %collective-permute-start.3 = (f32[2,8,512]{2,1,0:T(8,128)S(1)}, f32[2,8,512]{2,1,0:T(8,128)S(1)}, u32[]{:S(2)}, u32[]{:S(2)}) collective-permute-start(f32[2,8,512]{2,1,0:T(8,128)S(1)} %shard_map.43.refs_0_.refs_7_), channel_id=1, source_target_pairs={{0,6},{1,7},{2,4},{3,5},{4,2},{5,3},{6,0},{7,1},{8,14},{9,15},{10,... | collective-permute-start | bytes 98312 | tf_op jit(solution)/shard_map/ppermute | solution.py:574
  30.0 4.8 %collective-permute-start.2 = (f32[2,8,512]{2,1,0:T(8,128)S(1)}, f32[2,8,512]{2,1,0:T(8,128)S(1)}, u32[]{:S(2)}, u32[]{:S(2)}) collective-permute-start(f32[2,8,512]{2,1,0:T(8,128)S(1)} %shard_map.43.refs_0_.refs_7_), channel_id=1, source_target_pairs={{0,4},{1,5},{2,6},{3,7},{4,0},{5,1},{6,2},{7,3},{8,12},{9,13},{10,... | collective-permute-start | bytes 98312 | tf_op jit(solution)/shard_map/ppermute | solution.py:574
  30.0 4.8 %collective-permute-start.1 = (f32[2,8,512]{2,1,0:T(8,128)S(1)}, f32[2,8,512]{2,1,0:T(8,128)S(1)}, u32[]{:S(2)}, u32[]{:S(2)}) collective-permute-start(f32[2,8,512]{2,1,0:T(8,128)S(1)} %shard_map.43.refs_0_.refs_7_), channel_id=1, source_target_pairs={{0,2},{1,3},{2,0},{3,1},{4,6},{5,7},{6,4},{7,5},{8,10},{9,11},{10,... | collective-permute-start | bytes 98312 | tf_op jit(solution)/shard_map/ppermute | solution.py:574
  41.8 5.0 %collective-permute-start.4 = (f32[1,264,1024]{2,1,0:T(8,128)S(1)}, f32[1,264,1024]{2,1,0:T(8,128)S(1)}, u32[]{:S(2)}, u32[]{:S(2)}) collective-permute-start(f32[1,264,1024]{2,1,0:T(8,128)S(1)} %get-tuple-element.20.refs_7_), channel_id=1, source_target_pairs={{0,8},{8,0},{16,24},{24,16},{1,9},{9,1},{17,25},{25,17},{2,10},{10... | collective-permute-start | bytes 3244040 | tf_op jit(solution)/shard_map/ppermute | solution.py:557
  46.2 7.2 %collective-permute-start.5 = (f32[1,264,1024]{2,1,0:T(8,128)S(1)}, f32[1,264,1024]{2,1,0:T(8,128)S(1)}, u32[]{:S(2)}, u32[]{:S(2)}) collective-permute-start(f32[1,264,1024]{2,1,0:T(8,128)S(1)} %shard_map.45.after_ref), channel_id=1, source_target_pairs={{0,8},{8,0},{16,24},{24,16},{1,9},{9,1},{17,25},{25,17},{2,10},{10... | collective-permute-start | bytes 3244040 | tf_op jit(solution)/shard_map/ppermute | solution.py:557
  47.5 14.6 %collective-permute-start.6 = (bf16[272,1024]{1,0:T(8,128)(2,1)S(1)}, bf16[272,1024]{1,0:T(8,128)(2,1)S(1)}, u32[]{:S(2)}, u32[]{:S(2)}) collective-permute-start(bf16[272,1024]{1,0:T(8,128)(2,1)S(1)} %bitcast.9), channel_id=1, source_target_pairs={{0,16},{8,24},{16,0},{24,8},{1,17},{9,25},{17,1},{25,9},{2,18},{10... | collective-permute-start | bytes 1671176 | tf_op jit(solution)/shard_map/ppermute | solution.py:561
  63.0 2.0 %collective-permute-start.7 = (bf16[256,1024]{1,0:T(8,128)(2,1)S(1)}, bf16[256,1024]{1,0:T(8,128)(2,1)S(1)}, u32[]{:S(2)}, u32[]{:S(2)}) collective-permute-start(bf16[256,1024]{1,0:T(8,128)(2,1)S(1)} %shard_map.48.refs_0_), channel_id=1, source_target_pairs={{0,8},{8,0},{16,24},{24,16},{1,9},{9,1},{17,25},{25,17},{2,10},{10... | collective-permute-start | bytes 1572872 | tf_op jit(solution)/shard_map/ppermute | solution.py:557
  63.1 14.3 %collective-permute-start.8 = (bf16[256,1024]{1,0:T(8,128)(2,1)S(1)}, bf16[256,1024]{1,0:T(8,128)(2,1)S(1)}, u32[]{:S(2)}, u32[]{:S(2)}) collective-permute-start(bf16[256,1024]{1,0:T(8,128)(2,1)S(1)} %shard_map.48.refs_0_), channel_id=1, source_target_pairs={{0,16},{8,24},{16,0},{24,8},{1,17},{9,25},{17,1},{25,9},{2,18},{10... | collective-permute-start | bytes 1572872 | tf_op jit(solution)/shard_map/ppermute | solution.py:561
  77.4 1.9 %collective-permute-start.9 = (bf16[256,1024]{1,0:T(8,128)(2,1)S(1)}, bf16[256,1024]{1,0:T(8,128)(2,1)S(1)}, u32[]{:S(2)}, u32[]{:S(2)}) collective-permute-start(bf16[256,1024]{1,0:T(8,128)(2,1)S(1)} %shard_map.50.refs_0_), channel_id=1, source_target_pairs={{0,8},{8,0},{16,24},{24,16},{1,9},{9,1},{17,25},{25,17},{2,10},{10... | collective-permute-start | bytes 1572872 | tf_op jit(solution)/shard_map/ppermute | solution.py:557
  88.3 4.0 %collective-permute-start.10 = (f32[2,8,512]{2,1,0:T(8,128)S(1)}, f32[2,8,512]{2,1,0:T(8,128)S(1)}, u32[]{:S(2)}, u32[]{:S(2)}) collective-permute-start(f32[2,8,512]{2,1,0:T(8,128)S(1)} %shard_map.52.refs_0_), channel_id=1, source_target_pairs={{0,1},{1,0},{2,3},{3,2},{4,5},{5,4},{6,7},{7,6},{8,9},{9,8},{10,11... | collective-permute-start | bytes 98312 | tf_op jit(solution)/shard_map/ppermute | solution.py:574
  92.3 5.8 %collective-permute-start.13 = (f32[2,8,512]{2,1,0:T(8,128)S(1)}, f32[2,8,512]{2,1,0:T(8,128)S(1)}, u32[]{:S(2)}, u32[]{:S(2)}) collective-permute-start(f32[2,8,512]{2,1,0:T(8,128)S(1)} %shard_map.53.refs_0_.refs_8_), channel_id=1, source_target_pairs={{0,6},{1,7},{2,4},{3,5},{4,2},{5,3},{6,0},{7,1},{8,14},{9,15},{10,... | collective-permute-start | bytes 98312 | tf_op jit(solution)/shard_map/ppermute | solution.py:574
  93.9 4.9 %collective-permute-start.12 = (f32[2,8,512]{2,1,0:T(8,128)S(1)}, f32[2,8,512]{2,1,0:T(8,128)S(1)}, u32[]{:S(2)}, u32[]{:S(2)}) collective-permute-start(f32[2,8,512]{2,1,0:T(8,128)S(1)} %shard_map.53.refs_0_.refs_8_), channel_id=1, source_target_pairs={{0,4},{1,5},{2,6},{3,7},{4,0},{5,1},{6,2},{7,3},{8,12},{9,13},{10,... | collective-permute-start | bytes 98312 | tf_op jit(solution)/shard_map/ppermute | solution.py:574
  94.5 4.5 %collective-permute-start.11 = (f32[2,8,512]{2,1,0:T(8,128)S(1)}, f32[2,8,512]{2,1,0:T(8,128)S(1)}, u32[]{:S(2)}, u32[]{:S(2)}) collective-permute-start(f32[2,8,512]{2,1,0:T(8,128)S(1)} %shard_map.53.refs_0_.refs_8_), channel_id=1, source_target_pairs={{0,2},{1,3},{2,0},{3,1},{4,6},{5,7},{6,4},{7,5},{8,10},{9,11},{10,... | collective-permute-start | bytes 98312 | tf_op jit(solution)/shard_map/ppermute | solution.py:574
  107.5 3.0 %collective-permute-start.14 = (f32[1,1032,256]{2,1,0:T(8,128)S(1)}, f32[1,1032,256]{2,1,0:T(8,128)S(1)}, u32[]{:S(2)}, u32[]{:S(2)}) collective-permute-start(f32[1,1032,256]{2,1,0:T(8,128)S(1)} %get-tuple-element.27._), channel_id=1, source_target_pairs={{0,8},{8,0},{16,24},{24,16},{1,9},{9,1},{17,25},{25,17},{2,10},{10... | collective-permute-start | bytes 3170312 | tf_op jit(solution)/shard_map/ppermute | solution.py:557
  110.0 5.9 %collective-permute-start.15 = (f32[1,1032,256]{2,1,0:T(8,128)S(1)}, f32[1,1032,256]{2,1,0:T(8,128)S(1)}, u32[]{:S(2)}, u32[]{:S(2)}) collective-permute-start(f32[1,1032,256]{2,1,0:T(8,128)S(1)} %get-tuple-element.30.after_ref), channel_id=1, source_target_pairs={{0,8},{8,0},{16,24},{24,16},{1,9},{9,1},{17,25},{25,17},{2,10},{10... | collective-permute-start | bytes 3170312 | tf_op jit(solution)/shard_map/ppermute | solution.py:557
  111.3 14.1 %collective-permute-start.16 = (bf16[1040,256]{1,0:T(8,128)(2,1)S(1)}, bf16[1040,256]{1,0:T(8,128)(2,1)S(1)}, u32[]{:S(2)}, u32[]{:S(2)}) collective-permute-start(bf16[1040,256]{1,0:T(8,128)(2,1)S(1)} %bitcast.10), channel_id=1, source_target_pairs={{0,16},{8,24},{16,0},{24,8},{1,17},{9,25},{17,1},{25,9},{2,18},{10... | collective-permute-start | bytes 1597448 | tf_op jit(solution)/shard_map/ppermute | solution.py:561

commit v3 on v2

--- a/solution.py
+++ b/solution.py
@@ -16,6 +16,7 @@
 KEPT_VMEM = 20
 CHUNK_LINES = 2
 WEIGH_SLOTS = 2
+PIECES = 4
 LEVELS = 30000.0
 LOWEST = -117.0
 
@@ -83,7 +84,18 @@
         units_ref[part, :] = (c_ref[part, :] * scale).astype(BF16)
 
 
+def copy_body(in_ref, out_ref):
+    out_ref[...] = in_ref[...]
+
+
 def first_units(centroids):
+    centroids = pl.pallas_call(
+        copy_body,
+        in_specs=[VMEM],
+        out_specs=VMEM,
+        out_shape=jax.ShapeDtypeStruct(centroids.shape, F32),
+        compiler_params=params(10),
+    )(centroids)
     square_sums = jnp.sum(centroids * centroids, axis=1)[None]
     return pl.pallas_call(
         first_units_body,
@@ -97,6 +109,12 @@
     )(centroids, square_sums)
 
 
+def total_of(values):
+    rows, width = values.shape
+    groups = divisor(rows // 8, 16)
+    return jnp.sum(values.reshape(groups, rows // groups, width).sum(axis=0), axis=0, keepdims=True)
+
+
 def score_points(raw, units, x_ref, e_parts, stat_ref, stage, semaphores):
     line = stat_ref.shape[2]
     lines = stage.shape[0]
@@ -120,17 +138,19 @@
 
             tops, totals = [], []
             for offset in range(0, line, sub):
-                logits = lax.dot_general(
+                part = (slot, slice(None), slice(offset, offset + sub))
+                stage[part] = lax.dot_general(
                     units[...],
                     x_ref[pl.ds(pl.multiple_of(number * line + offset, sub), sub), :],
                     (((1,), (1,)), ((), ())),
                     preferred_element_type=F32,
                 )
-                top = jnp.max(logits, axis=0, keepdims=True)
-                shifted = jnp.exp(logits - top)
-                stage[slot, :, offset : offset + sub] = logits if raw else shifted
+                top = jnp.max(stage[part], axis=0, keepdims=True)
+                shifted = jnp.exp(stage[part] - top)
+                if not raw:
+                    stage[part] = shifted
                 tops.append(top)
-                totals.append(jnp.sum(shifted, axis=0, keepdims=True))
+                totals.append(total_of(shifted))
             stat_ref[0, pl.ds(number, 1), :] = jnp.concatenate(tops, axis=1)
             stat_ref[1, pl.ds(number, 1), :] = jnp.concatenate(totals, axis=1)
             for copy in copies(number, slot):
@@ -218,11 +238,17 @@
 FAR, THEIRS, OWN = range(3)
 
 
-def weigh_body(by_rows, n_sets, n_tops, kind, others, extra, pair, *refs):
+def weigh_body(by_rows, n_sets, n_tops, n_found, cuts, kind, others, extra, pair, *refs):
     parts = CORES if kind == FAR else 1
     stat_refs, refs = refs[:n_sets], refs[n_sets:]
     top_refs, (e_hbm, x_ref, _), refs = refs[:n_tops], refs[n_tops : n_tops + 3], refs[n_tops + 3 :]
-    out_refs, refs = refs[:parts], refs[parts:]
+    found_refs, refs = refs[:n_found], refs[n_found:]
+    cut_refs = ()
+    if cuts:
+        cut_refs, refs = refs[: len(cuts) - 1], refs[len(cuts) - 1 :]
+        out_refs, refs = refs[-1:], refs[:-1]
+    else:
+        out_refs, refs = refs[:parts], refs[parts:]
     if not by_rows:
         (kept_ref, kept_mass_ref), refs = refs[:2], refs[2:]
     scale_refs, refs = refs[:2], refs[2:]
@@ -309,6 +335,12 @@
             if kept:
                 kept_mass_ref[...] = mass
             write_sums(by_rows, other, core, out_refs, sum_ref, mass, extra)
+    for number, ref in enumerate(cut_refs):
+        ref[...] = out_refs[0][0, cuts[number] : cuts[number + 1], :]
+    start = 0
+    for ref in found_refs:
+        out_refs[0][0, start : start + ref.shape[0], :] += ref[...]
+        start += ref.shape[0]
 
 
 def write_sums(by_rows, other, core, out_refs, sum_ref, mass, extra):
@@ -368,7 +400,7 @@
     )(kept, mass, points, after)
 
 
-def weigh(by_rows, kind, chips, stats, tops, shifted, points, after):
+def weigh(by_rows, kind, chips, stats, tops, shifted, points, after, found=()):
     total, width = points.shape
     pair = shifted.shape[0] // chips
     parts, others = (CORES, chips - 1) if kind == FAR else (1, 1)
@@ -389,10 +421,18 @@
         sums = (rows, cols * parts)
     n_tops = len(tops)
     extra = round_up(-(-rows // cols), 8)
-    return pl.pallas_call(
-        functools.partial(weigh_body, by_rows, len(stats), n_tops, kind, others, extra, pair),
-        in_specs=[VMEM] * (len(stats) + n_tops) + [ANY, VMEM, ANY],
-        out_specs=[VMEM] * (parts + len(kept)),
+    outs = [jax.ShapeDtypeStruct((others, rows + extra, cols), F32)] * parts
+    cuts, whole = (), []
+    if by_rows and kind == THEIRS:
+        cuts = [round_up(rows * part // PIECES, 8) for part in range(PIECES)] + [rows + extra]
+        outs = [jax.ShapeDtypeStruct((end - start, cols), F32) for start, end in zip(cuts, cuts[1:])]
+        whole = [pltpu.VMEM((1, rows + extra, cols), F32)]
+    return pl.pallas_call(
+        functools.partial(
+            weigh_body, by_rows, len(stats), n_tops, len(found), cuts, kind, others, extra, pair
+        ),
+        in_specs=[VMEM] * (len(stats) + n_tops) + [ANY, VMEM, ANY] + [VMEM] * len(found),
+        out_specs=[VMEM] * (len(outs) + len(kept)),
         scratch_shapes=[pltpu.VMEM(stats[0].shape[1:], F32)] * 2
         + [pltpu.VMEM((sums[0], chunk), BF16)] * (2 if by_rows else 0)
         + [
@@ -400,16 +440,16 @@
             pltpu.VMEM((sums[0], 128), F32),
             pltpu.VMEM(sums, F32),
             pltpu.SemaphoreType.DMA((slots,)),
-        ],
-        out_shape=[jax.ShapeDtypeStruct((others, rows + extra, cols), F32)] * parts
-        + kept,
+        ]
+        + whole,
+        out_shape=outs + kept,
         compiler_params=params(WEIGH_VMEM),
         cost_estimate=pl.CostEstimate(
-            flops=2 * others * sums[0] * sums[1] * total,
-            bytes_accessed=2 * others * total * (sums[1] + 2 * sums[0]),
+            flops=0 if found else 2 * others * sums[0] * sums[1] * total,
+            bytes_accessed=0 if found else 2 * others * total * (sums[1] + 2 * sums[0]),
             transcendentals=0,
         ),
-    )(*stats, *tops, shifted, points, after)
+    )(*stats, *tops, shifted, points, after, *found)
 
 
 def fold_body(rows, lines, pieces, mine_ref, theirs_ref, after_ref, *out_refs):
@@ -458,6 +498,20 @@
     )(mine, theirs, after)
 
 
+def plain_fold_body(mine_ref, theirs_ref, out_ref):
+    out_ref[...] = mine_ref[...] + theirs_ref[...]
+
+
+def plain_fold(mine, theirs):
+    return pl.pallas_call(
+        plain_fold_body,
+        in_specs=[VMEM] * 2,
+        out_specs=VMEM,
+        out_shape=jax.ShapeDtypeStruct(mine.shape, F32),
+        compiler_params=params(10),
+    )(mine, theirs)
+
+
 def shape_of(height, width):
     rows = height - 8
     while rows + round_up(-(-rows // width), 8) != height:
@@ -465,16 +519,16 @@
     return rows, -(-rows // width)
 
 
-def finish_body(rows, lines, piece, as_units, mine_ref, theirs_ref, *refs):
-    code_refs, (_, out_ref) = refs[:-2], refs[-2:]
+def finish_body(rows, lines, piece, as_units, n_near, *refs):
+    near_refs, code_refs, (_, out_ref) = refs[:n_near], refs[n_near:-2], refs[-2:]
     count, width = out_ref.shape
     step = divisor(count, 128) if lines == 1 else width
-    mass = mine_ref[rows : rows + lines, :] + theirs_ref[rows : rows + lines, :]
+    mass = functools.reduce(jnp.add, [ref[rows : rows + lines, :] for ref in near_refs])
     if lines == 1:
         mass = mass[:, piece * count : (piece + 1) * count]
     used = slice(0, count) if lines == 1 else slice(None)
     for ref in code_refs:
-        for number in range(1, 4):
+        for number in range(0, 1) if as_units else range(1, 4):
             start = count + number * lines
             mass = mass + ref[start : start + lines, used].astype(F32)
 
@@ -489,20 +543,21 @@
     for number in range(count // step):
         part = slice(number * step, (number + 1) * step)
         near = slice(piece * count + number * step, piece * count + (number + 1) * step)
-        total = mine_ref[near, :] + theirs_ref[near, :]
+        total = functools.reduce(jnp.add, [ref[near, :] for ref in near_refs])
         for ref, scale in zip(code_refs, scales):
-            total = total + decode(ref[part, :], column(scale, number))
+            found = ref[part, :]
+            total = total + (found if as_units else decode(found, column(scale, number)))
         means = total / jnp.maximum(column(mass, number), 1.0)
         out_ref[part, :] = normalize_rows(means).astype(BF16) if as_units else means
 
 
-def finish(as_units, piece, pieces, mine, theirs, codes, after):
-    height, width = mine.shape
+def finish(as_units, piece, pieces, near, codes, after):
+    height, width = near[0].shape
     rows, lines = shape_of(height, width)
     count = rows // pieces
     return pl.pallas_call(
-        functools.partial(finish_body, rows, lines, piece, as_units),
-        in_specs=[VMEM] * (2 + len(codes)) + [ANY],
+        functools.partial(finish_body, rows, lines, piece, as_units, len(near)),
+        in_specs=[VMEM] * (len(near) + len(codes)) + [ANY],
         out_specs=VMEM,
         out_shape=jax.ShapeDtypeStruct((count, width), BF16 if as_units else F32),
         compiler_params=params(10),
@@ -511,7 +566,7 @@
             bytes_accessed=(12 + 2 * len(codes)) * count * width,
             transcendentals=2 * count * width,
         ),
-    )(mine, theirs, *codes, after)
+    )(*near, *codes, after)
 
 
 def keep_body(value_ref, after_ref, out_ref):
@@ -578,10 +633,10 @@
     def sums_over_pts(by_rows, stats, tops, shifted):
         kept = mass = None
 
-        def weighted(kind, after):
+        def weighted(kind, after, found=()):
             nonlocal kept, mass
             if by_rows:
-                return weigh(by_rows, kind, chips, stats, tops, shifted, points, after)
+                return weigh(by_rows, kind, chips, stats, tops, shifted, points, after, found)
             if kind == FAR:
                 *found, kept, mass = weigh(by_rows, kind, chips, stats, tops, shifted, points, after)
                 return found
@@ -590,14 +645,21 @@
 
         far_mine, far_theirs = weighted(FAR, stats[0])
         far_found = to_partner(far_theirs)
-        (near_theirs,) = weighted(THEIRS, far_theirs)
-        near_found = to_partner(near_theirs)
-        coded = fold(pieces if by_rows else 1, far_mine, far_found, near_theirs)
-        codes = [[to_chip(each[away - 1], away) for away in range(1, chips)] for each in coded]
-        (near_mine,) = weighted(OWN, coded[0])
+        if by_rows:
+            coded = [plain_fold(far_mine, far_found)]
+            codes = [[to_chip(each[away - 1], away) for away in range(1, chips)] for each in coded]
+            near_found = [to_partner(piece) for piece in weighted(THEIRS, coded[0])]
+            near = [each[0] for each in weighted(OWN, coded[0], near_found)]
+        else:
+            (near_theirs,) = weighted(THEIRS, far_theirs)
+            near_found = to_partner(near_theirs)
+            coded = fold(1, far_mine, far_found, near_theirs)
+            codes = [[to_chip(each[away - 1], away) for away in range(1, chips)] for each in coded]
+            (near_mine,) = weighted(OWN, coded[0])
+            near = [near_mine[0], near_found[0]]
         found, away_found, after = [], [], coded[0]
         for piece, each in enumerate(codes):
-            found.append(finish(by_rows, piece, len(codes), near_mine[0], near_found[0], each, after))
+            found.append(finish(by_rows, piece, len(codes), near, each, after))
             if by_rows:
                 away_found.append([to_chip(found[-1], -away) for away in range(1, chips)])
                 after = away_found[-1][-1]

time: 128 us -> 135 us (1.055)
  waiting for transfers between devices: 34.4 us -> 43.3 us
  other arithmetic: 2.68 us -> 0.34 us
  local copies, waits for them, and re-layouts: 3.38 us -> 5.26 us
    ppermute x3, waiting for transfers between devices: 21.4 us -> 25.9 us  [to_chip(): return lax.ppermute(value, 'pts', moves)]
    ppermute x6 -> x9, waiting for transfers between devices: 2.24 us -> 6.62 us  [to_partner(): return lax.ppermute(value, 'pts', [(i, i ^ 1) for i in range(n_pts)])]
    reduce_sum x1, other arithmetic: 2.68 us -> 0.34 us  [first_units(): square_sums = jnp.sum(centroids * centroids, axis=1)[None]]
    unnamed x5 -> x7, local copies, waits for them, and re-layouts: 3.38 us -> 5.26 us
  transfers between devices with their start and end apart: 17 -> 20, of which waited for: 12 -> 16; matrix products, arithmetic and copies ran while one was open for 0% -> 0% of each run, Pallas kernels for 19% -> 17%
where the time goes in v3:
time: 135 us
  Pallas kernels  65.1 us (48%)
  waiting for transfers between devices  43.3 us (32%)
  starting transfers between devices  20.4 us (15%)
  local copies, waits for them, and re-layouts  5.26 us (4%)
    pallas_call x3, Pallas kernels, scores(): pl.pallas_call(body, in_specs=[VMEM] * (count + 1) + [ANY] * len(more), o...  32.1 us
    ppermute x3, waiting for transfers between devices, to_chip(): return lax.ppermute(value, 'pts', moves)  25.9 us
    pallas_call x4, Pallas kernels, weigh(): pl.pallas_call(functools.partial(weigh_body, by_rows, len(stats), n_tops,...  24.2 us
    ppermute x8, starting transfers between devices, over_centroids(): sets.append(lax.ppermute(sets[0], 'cen', moves))  13.8 us
    ppermute x8, waiting for transfers between devices, over_centroids(): sets.append(lax.ppermute(sets[0], 'cen', moves))  10.7 us
    ppermute x9, waiting for transfers between devices, to_partner(): return lax.ppermute(value, 'pts', [(i, i ^ 1) for i in range(n_pts)])  6.62 us
    unnamed x7, local copies, waits for them, and re-layouts  5.26 us
    pallas_call x2, Pallas kernels, weigh_kept(): pl.pallas_call(functools.partial(weigh_kept_body, kind, extra), in_specs=...  4.74 us
  transfers between devices with their start and end apart: 20, of which 16 were waited for; matrix products, arithmetic and copies ran while one was open for 0% of the time, Pallas kernels for 17%

profile of v3, /device:TPU:0, one launch (start us, length us, event | category | flops | bytes accessed | tf_op | source)
XLA Modules:
  0.0 135.2 jit_solution(15466169138746049683)
XLA Ops:
  0.6 2.2 %copy-done = f32[1024,1024]{1,0:T(8,128)S(1)} copy-done((f32[1024,1024]{1,0:T(8,128)S(1)}, f32[1024,1024]{1,0:T(8,128)}, u32[]{:S(2)}) %copy-start) | copy-done | bytes 4194328
  2.8 0.3 shard_map.41.c_ref
  3.1 0.3 multiply_reduce_fusion
  3.5 0.4 shard_map.42.units
  3.9 1.1 slice-done
  5.0 1.3 slice-done.1
  6.4 14.2 %shard_map.43 = (f32[1024,4096]{1,0:T(8,128)}, f32[2,8,512]{2,1,0:T(8,128)S(1)}) custom-call(bf16[1024,1024]{1,0:T(8,128)(2,1)S(1)} %shard_map.42.units, bf16[4096,1024]{1,0:T(8,128)(2,1)S(1)} %bitcast.9), custom_call_target="tpu_custom_call" | custom-call | flops 8589934592 | bytes 25165824 | tf_op jit(solution)/shard_map/pallas_call | solution.py:219
  20.6 3.0 %collective-permute-start = (f32[2,8,512]{2,1,0:T(8,128)S(1)}, f32[2,8,512]{2,1,0:T(8,128)S(1)}, u32[]{:S(2)}, u32[]{:S(2)}) collective-permute-start(f32[2,8,512]{2,1,0:T(8,128)S(1)} %get-tuple-element.21.refs_0_.refs_4_), channel_id=1, source_target_pairs={{0,1},{1,0},{2,3},{3,2},{4,5},{5,4},{6,7},{7,6},{8,9},{9,8},{10,11... | collective-permute-start | bytes 98312 | tf_op jit(solution)/shard_map/ppermute | solution.py:629
  23.6 1.9 %collective-permute-done.refs_1_ = f32[2,8,512]{2,1,0:T(8,128)S(1)} collective-permute-done((f32[2,8,512]{2,1,0:T(8,128)S(1)}, f32[2,8,512]{2,1,0:T(8,128)S(1)}, u32[]{:S(2)}, u32[]{:S(2)}) %collective-permute-start) | collective-permute-done | bytes 32800 | tf_op jit(solution)/shard_map/ppermute | solution.py:629
  25.5 4.2 %collective-permute-start.3 = (f32[2,8,512]{2,1,0:T(8,128)S(1)}, f32[2,8,512]{2,1,0:T(8,128)S(1)}, u32[]{:S(2)}, u32[]{:S(2)}) collective-permute-start(f32[2,8,512]{2,1,0:T(8,128)S(1)} %shard_map.44.refs_0_.refs_7_), channel_id=1, source_target_pairs={{0,6},{1,7},{2,4},{3,5},{4,2},{5,3},{6,0},{7,1},{8,14},{9,15},{10,... | collective-permute-start | bytes 98312 | tf_op jit(solution)/shard_map/ppermute | solution.py:629
  29.7 0.6 collective-permute-start.1
  30.3 1.3 collective-permute-done.3.refs_3_
  31.6 2.9 %collective-permute-done.2.refs_2_ = f32[2,8,512]{2,1,0:T(8,128)S(1)} collective-permute-done((f32[2,8,512]{2,1,0:T(8,128)S(1)}, f32[2,8,512]{2,1,0:T(8,128)S(1)}, u32[]{:S(2)}, u32[]{:S(2)}) %collective-permute-start.2) | collective-permute-done | bytes 32800 | tf_op jit(solution)/shard_map/ppermute | solution.py:629
  34.5 6.9 %shard_map.45 = (f32[1,264,1024]{2,1,0:T(8,128)S(1)}, f32[1,264,1024]{2,1,0:T(8,128)S(1)}) custom-call(f32[2,8,512]{2,1,0:T(8,128)S(1)} %shard_map.44.refs_0_.refs_7_, f32[2,8,512]{2,1,0:T(8,128)S(1)} %collective-permute-done.1.refs_1_, f32[2,8,512]{2,1,0:T(8,128)S(1)} %collective-permute-done.2.refs_2_, f32[2,8,512]{2,1,0:T(8,128)S(1)} %collective-permute-done.3.refs_3_, ...), custom_call_target="tpu_custom_call" | custom-call | flops 4294967296 | bytes 16777216 | tf_op jit(solution)/shard_map/pallas_call | solution.py:430
  41.5 2.7 %collective-permute-done.4.theirs_ref = f32[1,264,1024]{2,1,0:T(8,128)S(1)} collective-permute-done((f32[1,264,1024]{2,1,0:T(8,128)S(1)}, f32[1,264,1024]{2,1,0:T(8,128)S(1)}, u32[]{:S(2)}, u32[]{:S(2)}) %collective-permute-start.4) | collective-permute-done | bytes 1081376 | tf_op jit(solution)/shard_map/ppermute | solution.py:612
  44.3 1.6 %collective-permute-start.9 = (f32[264,1024]{1,0:T(8,128)S(1)}, f32[264,1024]{1,0:T(8,128)S(1)}, u32[]{:S(2)}, u32[]{:S(2)}) collective-permute-start(f32[264,1024]{1,0:T(8,128)S(1)} %bitcast.10), channel_id=1, source_target_pairs={{0,16},{8,24},{16,0},{24,8},{1,17},{9,25},{17,1},{25,9},{2,18},{10... | collective-permute-start | bytes 3244040 | tf_op jit(solution)/shard_map/ppermute | solution.py:616
  45.9 4.4 %shard_map.47 = (f32[64,1024]{1,0:T(8,128)S(1)}, f32[64,1024]{1,0:T(8,128)S(1)}, f32[64,1024]{1,0:T(8,128)S(1)}, f32[72,1024]{1,0:T(8,128)S(1)}) custom-call(f32[2,8,512]{2,1,0:T(8,128)S(1)} %shard_map.44.refs_0_.refs_7_, f32[2,8,512]{2,1,0:T(8,128)S(1)} %collective-permute-done.1.refs_1_, f32[2,8,512]{2,1,0:T(8,128)S(1)} %collective-permute-done.2.refs_2_, ...), custom_call_target="tpu_custom_call" | custom-call | flops 2147483648 | bytes 12582912 | tf_op jit(solution)/shard_map/pallas_call | solution.py:430
  50.4 0.5 collective-permute-start.5
  50.9 0.4 collective-permute-start.7
  51.4 0.9 collective-permute-done.5.refs_8_
  52.3 0.4 collective-permute-done.6.refs_9_
  52.7 0.4 collective-permute-done.7.refs_10_
  53.1 4.4 %shard_map.48 = f32[1,264,1024]{2,1,0:T(8,128)S(1)} custom-call(f32[2,8,512]{2,1,0:T(8,128)S(1)} %shard_map.44.refs_0_.refs_7_, f32[2,8,512]{2,1,0:T(8,128)S(1)} %collective-permute-done.1.refs_1_, f32[2,8,512]{2,1,0:T(8,128)S(1)} %collective-permute-done.2.refs_2_, f32[2,8,512]{2,1,0:T(8,128)S(1)} %collective-permute-done.3.refs_3_, ...), custom_call_target="tpu_custom_call" | custom-call | tf_op jit(solution)/shard_map/pallas_call | solution.py:430
  57.5 12.8 %collective-permute-done.9.refs_1_ = f32[264,1024]{1,0:T(8,128)S(1)} collective-permute-done((f32[264,1024]{1,0:T(8,128)S(1)}, f32[264,1024]{1,0:T(8,128)S(1)}, u32[]{:S(2)}, u32[]{:S(2)}) %collective-permute-start.9) | collective-permute-done | bytes 1081376 | tf_op jit(solution)/shard_map/ppermute | solution.py:616
  70.3 0.4 shard_map.49.refs_0_
  70.7 1.6 %collective-permute-start.11 = (bf16[256,1024]{1,0:T(8,128)(2,1)S(1)}, bf16[256,1024]{1,0:T(8,128)(2,1)S(1)}, u32[]{:S(2)}, u32[]{:S(2)}) collective-permute-start(bf16[256,1024]{1,0:T(8,128)(2,1)S(1)} %shard_map.49.refs_0_), channel_id=1, source_target_pairs={{0,16},{8,24},{16,0},{24,8},{1,17},{9,25},{17,1},{25,9},{2,18},{10... | collective-permute-start | bytes 1572872 | tf_op jit(solution)/shard_map/ppermute | solution.py:616
  72.3 0.3 collective-permute-done.10.refs_1_
  72.6 8.8 %shard_map.50 = (f32[1024,4096]{1,0:T(8,128)}, f32[2,8,512]{2,1,0:T(8,128)S(1)}) custom-call(bf16[256,1024]{1,0:T(8,128)(2,1)S(1)} %shard_map.49.refs_0_, bf16[256,1024]{1,0:T(8,128)(2,1)S(1)} %collective-permute-done.10.refs_1_, bf16[4096,1024]{1,0:T(8,128)(2,1)S(1)} %bitcast.9), custom_call_target="tpu_custom_call" | custom-call | flops 4294967296 | bytes 16777216 | tf_op jit(solution)/shard_map/pallas_call | solution.py:219
  81.5 3.6 %collective-permute-done.11.value_ref = bf16[256,1024]{1,0:T(8,128)(2,1)S(1)} collective-permute-done((bf16[256,1024]{1,0:T(8,128)(2,1)S(1)}, bf16[256,1024]{1,0:T(8,128)(2,1)S(1)}, u32[]{:S(2)}, u32[]{:S(2)}) %collective-permute-start.11) | collective-permute-done | bytes 524320 | tf_op jit(solution)/shard_map/ppermute | solution.py:616
  85.1 1.9 %collective-permute-done.12.refs_1_ = bf16[256,1024]{1,0:T(8,128)(2,1)S(1)} collective-permute-done((bf16[256,1024]{1,0:T(8,128)(2,1)S(1)}, bf16[256,1024]{1,0:T(8,128)(2,1)S(1)}, u32[]{:S(2)}, u32[]{:S(2)}) %collective-permute-start.12) | collective-permute-done | bytes 524320 | tf_op jit(solution)/shard_map/ppermute | solution.py:612
  87.0 9.0 %shard_map.52 = (f32[1024,4096]{1,0:T(8,128)}, f32[2,8,512]{2,1,0:T(8,128)S(1)}) custom-call(bf16[256,1024]{1,0:T(8,128)(2,1)S(1)} %shard_map.51.refs_0_, bf16[256,1024]{1,0:T(8,128)(2,1)S(1)} %collective-permute-done.12.refs_1_, bf16[4096,1024]{1,0:T(8,128)(2,1)S(1)} %bitcast.9, f32[1024,4096]{1,0:T(8,128)} %get-tuple-element.30.refs_3_), custom_call_target="tpu_custom_call", output_to_operand_aliasing={{0}: (3, {})} | custom-call | flops 4294967296 | bytes 16777216 | tf_op jit(solution)/shard_map/pallas_call | solution.py:219
  96.1 1.5 %collective-permute-start.13 = (f32[2,8,512]{2,1,0:T(8,128)S(1)}, f32[2,8,512]{2,1,0:T(8,128)S(1)}, u32[]{:S(2)}, u32[]{:S(2)}) collective-permute-start(f32[2,8,512]{2,1,0:T(8,128)S(1)} %shard_map.53.refs_0_), channel_id=1, source_target_pairs={{0,1},{1,0},{2,3},{3,2},{4,5},{5,4},{6,7},{7,6},{8,9},{9,8},{10,11... | collective-permute-start | bytes 98312 | tf_op jit(solution)/shard_map/ppermute | solution.py:629
  97.6 2.4 %collective-permute-done.13.refs_1_ = f32[2,8,512]{2,1,0:T(8,128)S(1)} collective-permute-done((f32[2,8,512]{2,1,0:T(8,128)S(1)}, f32[2,8,512]{2,1,0:T(8,128)S(1)}, u32[]{:S(2)}, u32[]{:S(2)}) %collective-permute-start.13) | collective-permute-done | bytes 32800 | tf_op jit(solution)/shard_map/ppermute | solution.py:629
  100.1 1.5 %collective-permute-start.16 = (f32[2,8,512]{2,1,0:T(8,128)S(1)}, f32[2,8,512]{2,1,0:T(8,128)S(1)}, u32[]{:S(2)}, u32[]{:S(2)}) collective-permute-start(f32[2,8,512]{2,1,0:T(8,128)S(1)} %shard_map.54.refs_0_.refs_8_), channel_id=1, source_target_pairs={{0,6},{1,7},{2,4},{3,5},{4,2},{5,3},{6,0},{7,1},{8,14},{9,15},{10,... | collective-permute-start | bytes 98312 | tf_op jit(solution)/shard_map/ppermute | solution.py:629
  101.6 0.6 collective-permute-start.15
  102.2 2.3 %collective-permute-start.14 = (f32[2,8,512]{2,1,0:T(8,128)S(1)}, f32[2,8,512]{2,1,0:T(8,128)S(1)}, u32[]{:S(2)}, u32[]{:S(2)}) collective-permute-start(f32[2,8,512]{2,1,0:T(8,128)S(1)} %shard_map.54.refs_0_.refs_8_), channel_id=1, source_target_pairs={{0,2},{1,3},{2,0},{3,1},{4,6},{5,7},{6,4},{7,5},{8,10},{9,11},{10,... | collective-permute-start | bytes 98312 | tf_op jit(solution)/shard_map/ppermute | solution.py:629
  104.5 1.3 collective-permute-done.16.refs_3_
  105.9 0.6 collective-permute-done.15.refs_2_
  106.4 0.3 collective-permute-done.14.refs_1_
  106.8 8.5 %shard_map.55 = (f32[1,1032,256]{2,1,0:T(8,128)S(1)}, f32[1,1032,256]{2,1,0:T(8,128)S(1)}, bf16[1024,4096]{1,0:T(8,128)(2,1)S(1)}, f32[1,1024]{1,0:T(1,128)S(1)}) custom-call(f32[2,8,512]{2,1,0:T(8,128)S(1)} %shard_map.54.refs_0_.refs_8_, f32[2,8,512]{2,1,0:T(8,128)S(1)} %collective-permute-done.14.refs_1_, ...), custom_call_target="tpu_custom_call" | custom-call | flops 4294967296 | bytes 20971520 | tf_op jit(solution)/shard_map/pallas_call | solution.py:430
  115.3 2.4 %shard_map.56 = (f32[1,1032,256]{2,1,0:T(8,128)S(1)}, bf16[1024,4096]{1,0:T(8,128)(2,1)S(1)}) custom-call(bf16[1024,4096]{1,0:T(8,128)(2,1)S(1)} %get-tuple-element.33.kept_ref, f32[1,1024]{1,0:T(1,128)S(1)} %get-tuple-element.34.mass_ref, bf16[4096,1024]{1,0:T(8,128)(2,1)S(1)} %bitcast.9, ...), custom_call_target="tpu_custom_call", output_to_operand_aliasing={{1}: (0, {})} | custom-call | flops 2147483648 | bytes 10485760 | tf_op jit(solution)/shard_map/pallas_call | solution.py:386
  117.7 0.5 collective-permute-start.18
  118.3 0.8 shard_map.57._.refs_3_
  119.0 1.6 %collective-permute-start.19 = (bf16[1040,256]{1,0:T(8,128)(2,1)S(1)}, bf16[1040,256]{1,0:T(8,128)(2,1)S(1)}, u32[]{:S(2)}, u32[]{:S(2)}) collective-permute-start(bf16[1040,256]{1,0:T(8,128)(2,1)S(1)} %bitcast.11), channel_id=1, source_target_pairs={{0,16},{8,24},{16,0},{24,8},{1,17},{9,25},{17,1},{25,9},{2,18},{10... | collective-permute-start | bytes 1597448 | tf_op jit(solution)/shard_map/ppermute | solution.py:616
  120.6 0.6 copy.8
  121.3 2.4 %shard_map.58 = (f32[1,1032,256]{2,1,0:T(8,128)S(1)}, bf16[1024,4096]{1,0:T(8,128)(2,1)S(1)}) custom-call(bf16[1024,4096]{1,0:T(8,128)(2,1)S(1)} %get-tuple-element.36.kept_ref, f32[1,1024]{1,0:T(1,128)S(1)} %get-tuple-element.34.mass_ref, bf16[4096,1024]{1,0:T(8,128)(2,1)S(1)} %bitcast.9, ...), custom_call_target="tpu_custom_call", output_to_operand_aliasing={{1}: (0, {})} | custom-call | flops 2147483648 | bytes 10485760 | tf_op jit(solution)/shard_map/pallas_call | solution.py:386
  123.6 9.5 %collective-permute-done.19.refs_2_ = bf16[1040,256]{1,0:T(8,128)(2,1)S(1)} collective-permute-done((bf16[1040,256]{1,0:T(8,128)(2,1)S(1)}, bf16[1040,256]{1,0:T(8,128)(2,1)S(1)}, u32[]{:S(2)}, u32[]{:S(2)}) %collective-permute-start.19) | collective-permute-done | bytes 532512 | tf_op jit(solution)/shard_map/ppermute | solution.py:616
  133.1 2.0 %shard_map.59 = f32[1024,256]{1,0:T(8,128)} custom-call(f32[1032,256]{1,0:T(8,128)S(1)} %bitcast.14, f32[1032,256]{1,0:T(8,128)S(1)} %bitcast.13, bf16[1040,256]{1,0:T(8,128)(2,1)S(1)} %collective-permute-done.19.refs_2_, bf16[1,1040,256]{2,1,0:T(8,128)(2,1)S(1)} %shard_map.57._.refs_3_), custom_call_target="tpu_custom_call" | custom-call | flops 7864320 | bytes 3670016 | tf_op jit(solution)/shard_map/pallas_call | solution.py:558
  (21 shorter events, 0.6 us)
Async XLA Ops:
  0.6 2.2 %copy-start = (f32[1024,1024]{1,0:T(8,128)S(1)}, f32[1024,1024]{1,0:T(8,128)}, u32[]{:S(2)}) copy-start(f32[1024,1024]{1,0:T(8,128)} %in_ref.1) | copy-start | bytes 12582916
  2.8 2.2 %slice-start = ((s8[8388608]{0:T(1024)(128)(4,1)}), s8[4194304]{0:T(1024)(128)(4,1)S(1)}, s32[]{:S(2)}) async-start(s8[8388608]{0:T(1024)(128)(4,1)} %bitcast.8), calls=%async_computation | async-start | bytes 8388608
  3.1 3.3 %slice-start.1 = ((s8[8388608]{0:T(1024)(128)(4,1)}), s8[4194304]{0:T(1024)(128)(4,1)S(1)}, s32[]{:S(2)}) async-start(s8[8388608]{0:T(1024)(128)(4,1)} %bitcast.8), calls=%async_computation.1 | async-start | bytes 8388608
  20.6 4.9 %collective-permute-start = (f32[2,8,512]{2,1,0:T(8,128)S(1)}, f32[2,8,512]{2,1,0:T(8,128)S(1)}, u32[]{:S(2)}, u32[]{:S(2)}) collective-permute-start(f32[2,8,512]{2,1,0:T(8,128)S(1)} %get-tuple-element.21.refs_0_.refs_4_), channel_id=1, source_target_pairs={{0,1},{1,0},{2,3},{3,2},{4,5},{5,4},{6,7},{7,6},{8,9},{9,8},{10,11... | collective-permute-start | bytes 98312 | tf_op jit(solution)/shard_map/ppermute | solution.py:629
  25.5 6.1 %collective-permute-start.3 = (f32[2,8,512]{2,1,0:T(8,128)S(1)}, f32[2,8,512]{2,1,0:T(8,128)S(1)}, u32[]{:S(2)}, u32[]{:S(2)}) collective-permute-start(f32[2,8,512]{2,1,0:T(8,128)S(1)} %shard_map.44.refs_0_.refs_7_), channel_id=1, source_target_pairs={{0,6},{1,7},{2,4},{3,5},{4,2},{5,3},{6,0},{7,1},{8,14},{9,15},{10,... | collective-permute-start | bytes 98312 | tf_op jit(solution)/shard_map/ppermute | solution.py:629
  29.7 4.8 %collective-permute-start.2 = (f32[2,8,512]{2,1,0:T(8,128)S(1)}, f32[2,8,512]{2,1,0:T(8,128)S(1)}, u32[]{:S(2)}, u32[]{:S(2)}) collective-permute-start(f32[2,8,512]{2,1,0:T(8,128)S(1)} %shard_map.44.refs_0_.refs_7_), channel_id=1, source_target_pairs={{0,4},{1,5},{2,6},{3,7},{4,0},{5,1},{6,2},{7,3},{8,12},{9,13},{10,... | collective-permute-start | bytes 98312 | tf_op jit(solution)/shard_map/ppermute | solution.py:629
  29.7 4.8 %collective-permute-start.1 = (f32[2,8,512]{2,1,0:T(8,128)S(1)}, f32[2,8,512]{2,1,0:T(8,128)S(1)}, u32[]{:S(2)}, u32[]{:S(2)}) collective-permute-start(f32[2,8,512]{2,1,0:T(8,128)S(1)} %shard_map.44.refs_0_.refs_7_), channel_id=1, source_target_pairs={{0,2},{1,3},{2,0},{3,1},{4,6},{5,7},{6,4},{7,5},{8,10},{9,11},{10,... | collective-permute-start | bytes 98312 | tf_op jit(solution)/shard_map/ppermute | solution.py:629
  41.4 2.8 %collective-permute-start.4 = (f32[1,264,1024]{2,1,0:T(8,128)S(1)}, f32[1,264,1024]{2,1,0:T(8,128)S(1)}, u32[]{:S(2)}, u32[]{:S(2)}) collective-permute-start(f32[1,264,1024]{2,1,0:T(8,128)S(1)} %get-tuple-element.24), channel_id=1, source_target_pairs={{0,8},{8,0},{16,24},{24,16},{1,9},{9,1},{17,25},{25,17},{2,10},{10... | collective-permute-start | bytes 3244040 | tf_op jit(solution)/shard_map/ppermute | solution.py:612
  44.3 26.0 %collective-permute-start.9 = (f32[264,1024]{1,0:T(8,128)S(1)}, f32[264,1024]{1,0:T(8,128)S(1)}, u32[]{:S(2)}, u32[]{:S(2)}) collective-permute-start(f32[264,1024]{1,0:T(8,128)S(1)} %bitcast.10), channel_id=1, source_target_pairs={{0,16},{8,24},{16,0},{24,8},{1,17},{9,25},{17,1},{25,9},{2,18},{10... | collective-permute-start | bytes 3244040 | tf_op jit(solution)/shard_map/ppermute | solution.py:616
  50.3 2.8 %collective-permute-start.8 = (f32[72,1024]{1,0:T(8,128)S(1)}, f32[72,1024]{1,0:T(8,128)S(1)}, u32[]{:S(2)}, u32[]{:S(2)}) collective-permute-start(f32[72,1024]{1,0:T(8,128)S(1)} %get-tuple-element.28), channel_id=1, source_target_pairs={{0,8},{8,0},{16,24},{24,16},{1,9},{9,1},{17,25},{25,17},{2,10},{10... | collective-permute-start | bytes 884744 | tf_op jit(solution)/shard_map/ppermute | solution.py:612
  50.4 1.9 %collective-permute-start.5 = (f32[64,1024]{1,0:T(8,128)S(1)}, f32[64,1024]{1,0:T(8,128)S(1)}, u32[]{:S(2)}, u32[]{:S(2)}) collective-permute-start(f32[64,1024]{1,0:T(8,128)S(1)} %get-tuple-element.25), channel_id=1, source_target_pairs={{0,8},{8,0},{16,24},{24,16},{1,9},{9,1},{17,25},{25,17},{2,10},{10... | collective-permute-start | bytes 786440 | tf_op jit(solution)/shard_map/ppermute | solution.py:612
  50.9 1.8 %collective-permute-start.6 = (f32[64,1024]{1,0:T(8,128)S(1)}, f32[64,1024]{1,0:T(8,128)S(1)}, u32[]{:S(2)}, u32[]{:S(2)}) collective-permute-start(f32[64,1024]{1,0:T(8,128)S(1)} %get-tuple-element.26), channel_id=1, source_target_pairs={{0,8},{8,0},{16,24},{24,16},{1,9},{9,1},{17,25},{25,17},{2,10},{10... | collective-permute-start | bytes 786440 | tf_op jit(solution)/shard_map/ppermute | solution.py:612
  50.9 2.1 %collective-permute-start.7 = (f32[64,1024]{1,0:T(8,128)S(1)}, f32[64,1024]{1,0:T(8,128)S(1)}, u32[]{:S(2)}, u32[]{:S(2)}) collective-permute-start(f32[64,1024]{1,0:T(8,128)S(1)} %get-tuple-element.27), channel_id=1, source_target_pairs={{0,8},{8,0},{16,24},{24,16},{1,9},{9,1},{17,25},{25,17},{2,10},{10... | collective-permute-start | bytes 786440 | tf_op jit(solution)/shard_map/ppermute | solution.py:612
  70.7 2.0 %collective-permute-start.10 = (bf16[256,1024]{1,0:T(8,128)(2,1)S(1)}, bf16[256,1024]{1,0:T(8,128)(2,1)S(1)}, u32[]{:S(2)}, u32[]{:S(2)}) collective-permute-start(bf16[256,1024]{1,0:T(8,128)(2,1)S(1)} %shard_map.49.refs_0_), channel_id=1, source_target_pairs={{0,8},{8,0},{16,24},{24,16},{1,9},{9,1},{17,25},{25,17},{2,10},{10... | collective-permute-start | bytes 1572872 | tf_op jit(solution)/shard_map/ppermute | solution.py:612
  70.7 14.3 %collective-permute-start.11 = (bf16[256,1024]{1,0:T(8,128)(2,1)S(1)}, bf16[256,1024]{1,0:T(8,128)(2,1)S(1)}, u32[]{:S(2)}, u32[]{:S(2)}) collective-permute-start(bf16[256,1024]{1,0:T(8,128)(2,1)S(1)} %shard_map.49.refs_0_), channel_id=1, source_target_pairs={{0,16},{8,24},{16,0},{24,8},{1,17},{9,25},{17,1},{25,9},{2,18},{10... | collective-permute-start | bytes 1572872 | tf_op jit(solution)/shard_map/ppermute | solution.py:616
  85.1 1.9 %collective-permute-start.12 = (bf16[256,1024]{1,0:T(8,128)(2,1)S(1)}, bf16[256,1024]{1,0:T(8,128)(2,1)S(1)}, u32[]{:S(2)}, u32[]{:S(2)}) collective-permute-start(bf16[256,1024]{1,0:T(8,128)(2,1)S(1)} %shard_map.51.refs_0_), channel_id=1, source_target_pairs={{0,8},{8,0},{16,24},{24,16},{1,9},{9,1},{17,25},{25,17},{2,10},{10... | collective-permute-start | bytes 1572872 | tf_op jit(solution)/shard_map/ppermute | solution.py:612
  96.1 4.0 %collective-permute-start.13 = (f32[2,8,512]{2,1,0:T(8,128)S(1)}, f32[2,8,512]{2,1,0:T(8,128)S(1)}, u32[]{:S(2)}, u32[]{:S(2)}) collective-permute-start(f32[2,8,512]{2,1,0:T(8,128)S(1)} %shard_map.53.refs_0_), channel_id=1, source_target_pairs={{0,1},{1,0},{2,3},{3,2},{4,5},{5,4},{6,7},{7,6},{8,9},{9,8},{10,11... | collective-permute-start | bytes 98312 | tf_op jit(solution)/shard_map/ppermute | solution.py:629
  100.1 5.8 %collective-permute-start.16 = (f32[2,8,512]{2,1,0:T(8,128)S(1)}, f32[2,8,512]{2,1,0:T(8,128)S(1)}, u32[]{:S(2)}, u32[]{:S(2)}) collective-permute-start(f32[2,8,512]{2,1,0:T(8,128)S(1)} %shard_map.54.refs_0_.refs_8_), channel_id=1, source_target_pairs={{0,6},{1,7},{2,4},{3,5},{4,2},{5,3},{6,0},{7,1},{8,14},{9,15},{10,... | collective-permute-start | bytes 98312 | tf_op jit(solution)/shard_map/ppermute | solution.py:629
  101.6 4.8 %collective-permute-start.15 = (f32[2,8,512]{2,1,0:T(8,128)S(1)}, f32[2,8,512]{2,1,0:T(8,128)S(1)}, u32[]{:S(2)}, u32[]{:S(2)}) collective-permute-start(f32[2,8,512]{2,1,0:T(8,128)S(1)} %shard_map.54.refs_0_.refs_8_), channel_id=1, source_target_pairs={{0,4},{1,5},{2,6},{3,7},{4,0},{5,1},{6,2},{7,3},{8,12},{9,13},{10,... | collective-permute-start | bytes 98312 | tf_op jit(solution)/shard_map/ppermute | solution.py:629
  102.2 4.5 %collective-permute-start.14 = (f32[2,8,512]{2,1,0:T(8,128)S(1)}, f32[2,8,512]{2,1,0:T(8,128)S(1)}, u32[]{:S(2)}, u32[]{:S(2)}) collective-permute-start(f32[2,8,512]{2,1,0:T(8,128)S(1)} %shard_map.54.refs_0_.refs_8_), channel_id=1, source_target_pairs={{0,2},{1,3},{2,0},{3,1},{4,6},{5,7},{6,4},{7,5},{8,10},{9,11},{10,... | collective-permute-start | bytes 98312 | tf_op jit(solution)/shard_map/ppermute | solution.py:629
  115.2 3.0 %collective-permute-start.17 = (f32[1,1032,256]{2,1,0:T(8,128)S(1)}, f32[1,1032,256]{2,1,0:T(8,128)S(1)}, u32[]{:S(2)}, u32[]{:S(2)}) collective-permute-start(f32[1,1032,256]{2,1,0:T(8,128)S(1)} %get-tuple-element.35._), channel_id=1, source_target_pairs={{0,8},{8,0},{16,24},{24,16},{1,9},{9,1},{17,25},{25,17},{2,10},{10... | collective-permute-start | bytes 3170312 | tf_op jit(solution)/shard_map/ppermute | solution.py:612
  117.7 5.9 %collective-permute-start.18 = (f32[1,1032,256]{2,1,0:T(8,128)S(1)}, f32[1,1032,256]{2,1,0:T(8,128)S(1)}, u32[]{:S(2)}, u32[]{:S(2)}) collective-permute-start(f32[1,1032,256]{2,1,0:T(8,128)S(1)} %get-tuple-element.38.after_ref), channel_id=1, source_target_pairs={{0,8},{8,0},{16,24},{24,16},{1,9},{9,1},{17,25},{25,17},{2,10},{10... | collective-permute-start | bytes 3170312 | tf_op jit(solution)/shard_map/ppermute | solution.py:612
  119.0 14.1 %collective-permute-start.19 = (bf16[1040,256]{1,0:T(8,128)(2,1)S(1)}, bf16[1040,256]{1,0:T(8,128)(2,1)S(1)}, u32[]{:S(2)}, u32[]{:S(2)}) collective-permute-start(bf16[1040,256]{1,0:T(8,128)(2,1)S(1)} %bitcast.11), channel_id=1, source_target_pairs={{0,16},{8,24},{16,0},{24,8},{1,17},{9,25},{17,1},{25,9},{2,18},{10... | collective-permute-start | bytes 1597448 | tf_op jit(solution)/shard_map/ppermute | solution.py:616

commit v4 on v3

--- a/solution.py
+++ b/solution.py
@@ -139,16 +139,15 @@
             tops, totals = [], []
             for offset in range(0, line, sub):
                 part = (slot, slice(None), slice(offset, offset + sub))
-                stage[part] = lax.dot_general(
+                logits = lax.dot_general(
                     units[...],
                     x_ref[pl.ds(pl.multiple_of(number * line + offset, sub), sub), :],
                     (((1,), (1,)), ((), ())),
                     preferred_element_type=F32,
                 )
-                top = jnp.max(stage[part], axis=0, keepdims=True)
-                shifted = jnp.exp(stage[part] - top)
-                if not raw:
-                    stage[part] = shifted
+                top = jnp.max(logits, axis=0, keepdims=True)
+                shifted = jnp.exp(logits - top)
+                stage[part] = logits if raw else shifted
                 tops.append(top)
                 totals.append(total_of(shifted))
             stat_ref[0, pl.ds(number, 1), :] = jnp.concatenate(tops, axis=1)
@@ -498,20 +497,6 @@
     )(mine, theirs, after)
 
 
-def plain_fold_body(mine_ref, theirs_ref, out_ref):
-    out_ref[...] = mine_ref[...] + theirs_ref[...]
-
-
-def plain_fold(mine, theirs):
-    return pl.pallas_call(
-        plain_fold_body,
-        in_specs=[VMEM] * 2,
-        out_specs=VMEM,
-        out_shape=jax.ShapeDtypeStruct(mine.shape, F32),
-        compiler_params=params(10),
-    )(mine, theirs)
-
-
 def shape_of(height, width):
     rows = height - 8
     while rows + round_up(-(-rows // width), 8) != height:
@@ -528,7 +513,7 @@
         mass = mass[:, piece * count : (piece + 1) * count]
     used = slice(0, count) if lines == 1 else slice(None)
     for ref in code_refs:
-        for number in range(0, 1) if as_units else range(1, 4):
+        for number in range(1, 4):
             start = count + number * lines
             mass = mass + ref[start : start + lines, used].astype(F32)
 
@@ -545,8 +530,7 @@
         near = slice(piece * count + number * step, piece * count + (number + 1) * step)
         total = functools.reduce(jnp.add, [ref[near, :] for ref in near_refs])
         for ref, scale in zip(code_refs, scales):
-            found = ref[part, :]
-            total = total + (found if as_units else decode(found, column(scale, number)))
+            total = total + decode(ref[part, :], column(scale, number))
         means = total / jnp.maximum(column(mass, number), 1.0)
         out_ref[part, :] = normalize_rows(means).astype(BF16) if as_units else means
 
@@ -646,7 +630,7 @@
         far_mine, far_theirs = weighted(FAR, stats[0])
         far_found = to_partner(far_theirs)
         if by_rows:
-            coded = [plain_fold(far_mine, far_found)]
+            coded = fold(pieces, far_mine, far_found, far_theirs)
             codes = [[to_chip(each[away - 1], away) for away in range(1, chips)] for each in coded]
             near_found = [to_partner(piece) for piece in weighted(THEIRS, coded[0])]
             near = [each[0] for each in weighted(OWN, coded[0], near_found)]

time: 135 us -> 125 us (0.926)
  waiting for transfers between devices: 43.3 us -> 31.8 us
    ppermute x3, waiting for transfers between devices: 25.9 us -> 14.4 us  [to_chip(): return lax.ppermute(value, 'pts', moves)]
  transfers between devices with their start and end apart: 20 -> 20, of which waited for: 16 -> 16; matrix products, arithmetic and copies ran while one was open for 0% -> 0% of each run, Pallas kernels for 17% -> 19%
where the time goes in v4:
time: 125 us
  Pallas kernels  66.2 us (53%)
  waiting for transfers between devices  31.8 us (25%)
  starting transfers between devices  20.4 us (16%)
  local copies, waits for them, and re-layouts  5.26 us (4%)
    pallas_call x3, Pallas kernels, scores(): pl.pallas_call(body, in_specs=[VMEM] * (count + 1) + [ANY] * len(more), o...  32.1 us
    pallas_call x4, Pallas kernels, weigh(): pl.pallas_call(functools.partial(weigh_body, by_rows, len(stats), n_tops,...  24.2 us
    ppermute x3, waiting for transfers between devices, to_chip(): return lax.ppermute(value, 'pts', moves)  14.4 us
    ppermute x8, starting transfers between devices, over_centroids(): sets.append(lax.ppermute(sets[0], 'cen', moves))  13.8 us
    ppermute x8, waiting for transfers between devices, over_centroids(): sets.append(lax.ppermute(sets[0], 'cen', moves))  10.7 us
    ppermute x9, waiting for transfers between devices, to_partner(): return lax.ppermute(value, 'pts', [(i, i ^ 1) for i in range(n_pts)])  6.62 us
    unnamed x7, local copies, waits for them, and re-layouts  5.26 us
    pallas_call x2, Pallas kernels, weigh_kept(): pl.pallas_call(functools.partial(weigh_kept_body, kind, extra), in_specs=...  4.74 us
  transfers between devices with their start and end apart: 20, of which 16 were waited for; matrix products, arithmetic and copies ran while one was open for 0% of the time, Pallas kernels for 19%

profile of v4, /device:TPU:0, one launch (start us, length us, event | category | flops | bytes accessed | tf_op | source)
XLA Modules:
  0.0 124.8 jit_solution(1330647061002771077)
XLA Ops:
  0.6 2.2 %copy-done = f32[1024,1024]{1,0:T(8,128)S(1)} copy-done((f32[1024,1024]{1,0:T(8,128)S(1)}, f32[1024,1024]{1,0:T(8,128)}, u32[]{:S(2)}) %copy-start) | copy-done | bytes 4194328
  3.1 0.3 multiply_reduce_fusion
  3.5 0.4 shard_map.42.units
  3.9 1.1 slice-done
  5.0 1.3 %slice-done.1 = s8[4194304]{0:T(1024)(128)(4,1)S(1)} async-done(((s8[8388608]{0:T(1024)(128)(4,1)}), s8[4194304]{0:T(1024)(128)(4,1)S(1)}, s32[]{:S(2)}) %slice-start.1) | async-done | bytes 4194328
  6.4 14.2 %shard_map.43 = (f32[1024,4096]{1,0:T(8,128)}, f32[2,8,512]{2,1,0:T(8,128)S(1)}) custom-call(bf16[1024,1024]{1,0:T(8,128)(2,1)S(1)} %shard_map.42.units, bf16[4096,1024]{1,0:T(8,128)(2,1)S(1)} %bitcast.9), custom_call_target="tpu_custom_call" | custom-call | flops 8589934592 | bytes 25165824 | tf_op jit(solution)/shard_map/pallas_call | solution.py:218
  20.6 3.0 %collective-permute-start = (f32[2,8,512]{2,1,0:T(8,128)S(1)}, f32[2,8,512]{2,1,0:T(8,128)S(1)}, u32[]{:S(2)}, u32[]{:S(2)}) collective-permute-start(f32[2,8,512]{2,1,0:T(8,128)S(1)} %get-tuple-element.21.refs_0_.refs_4_), channel_id=1, source_target_pairs={{0,1},{1,0},{2,3},{3,2},{4,5},{5,4},{6,7},{7,6},{8,9},{9,8},{10,11... | collective-permute-start | bytes 98312 | tf_op jit(solution)/shard_map/ppermute | solution.py:613
  23.6 1.9 %collective-permute-done.refs_1_ = f32[2,8,512]{2,1,0:T(8,128)S(1)} collective-permute-done((f32[2,8,512]{2,1,0:T(8,128)S(1)}, f32[2,8,512]{2,1,0:T(8,128)S(1)}, u32[]{:S(2)}, u32[]{:S(2)}) %collective-permute-start) | collective-permute-done | bytes 32800 | tf_op jit(solution)/shard_map/ppermute | solution.py:613
  25.5 4.2 %collective-permute-start.3 = (f32[2,8,512]{2,1,0:T(8,128)S(1)}, f32[2,8,512]{2,1,0:T(8,128)S(1)}, u32[]{:S(2)}, u32[]{:S(2)}) collective-permute-start(f32[2,8,512]{2,1,0:T(8,128)S(1)} %shard_map.44.refs_0_.refs_7_), channel_id=1, source_target_pairs={{0,6},{1,7},{2,4},{3,5},{4,2},{5,3},{6,0},{7,1},{8,14},{9,15},{10,... | collective-permute-start | bytes 98312 | tf_op jit(solution)/shard_map/ppermute | solution.py:613
  29.7 0.6 collective-permute-start.1
  30.3 1.3 %collective-permute-done.3.refs_3_ = f32[2,8,512]{2,1,0:T(8,128)S(1)} collective-permute-done((f32[2,8,512]{2,1,0:T(8,128)S(1)}, f32[2,8,512]{2,1,0:T(8,128)S(1)}, u32[]{:S(2)}, u32[]{:S(2)}) %collective-permute-start.3) | collective-permute-done | bytes 32800 | tf_op jit(solution)/shard_map/ppermute | solution.py:613
  31.6 2.9 %collective-permute-done.2.refs_2_ = f32[2,8,512]{2,1,0:T(8,128)S(1)} collective-permute-done((f32[2,8,512]{2,1,0:T(8,128)S(1)}, f32[2,8,512]{2,1,0:T(8,128)S(1)}, u32[]{:S(2)}, u32[]{:S(2)}) %collective-permute-start.2) | collective-permute-done | bytes 32800 | tf_op jit(solution)/shard_map/ppermute | solution.py:613
  34.5 6.9 %shard_map.45 = (f32[1,264,1024]{2,1,0:T(8,128)S(1)}, f32[1,264,1024]{2,1,0:T(8,128)S(1)}) custom-call(f32[2,8,512]{2,1,0:T(8,128)S(1)} %shard_map.44.refs_0_.refs_7_, f32[2,8,512]{2,1,0:T(8,128)S(1)} %collective-permute-done.1.refs_1_, f32[2,8,512]{2,1,0:T(8,128)S(1)} %collective-permute-done.2.refs_2_, f32[2,8,512]{2,1,0:T(8,128)S(1)} %collective-permute-done.3.refs_3_, ...), custom_call_target="tpu_custom_call" | custom-call | flops 4294967296 | bytes 16777216 | tf_op jit(solution)/shard_map/pallas_call | solution.py:429
  41.5 2.7 %collective-permute-done.4.theirs_ref = f32[1,264,1024]{2,1,0:T(8,128)S(1)} collective-permute-done((f32[1,264,1024]{2,1,0:T(8,128)S(1)}, f32[1,264,1024]{2,1,0:T(8,128)S(1)}, u32[]{:S(2)}, u32[]{:S(2)}) %collective-permute-start.4) | collective-permute-done | bytes 1081376 | tf_op jit(solution)/shard_map/ppermute | solution.py:596
  44.2 0.7 shard_map.46.refs_7_.refs_2_
  44.9 1.6 %collective-permute-start.9 = (bf16[272,1024]{1,0:T(8,128)(2,1)S(1)}, bf16[272,1024]{1,0:T(8,128)(2,1)S(1)}, u32[]{:S(2)}, u32[]{:S(2)}) collective-permute-start(bf16[272,1024]{1,0:T(8,128)(2,1)S(1)} %bitcast.10), channel_id=1, source_target_pairs={{0,16},{8,24},{16,0},{24,8},{1,17},{9,25},{17,1},{25,9},{2,18},{10... | collective-permute-start | bytes 1671176 | tf_op jit(solution)/shard_map/ppermute | solution.py:600
  46.5 4.4 %shard_map.47 = (f32[64,1024]{1,0:T(8,128)S(1)}, f32[64,1024]{1,0:T(8,128)S(1)}, f32[64,1024]{1,0:T(8,128)S(1)}, f32[72,1024]{1,0:T(8,128)S(1)}) custom-call(f32[2,8,512]{2,1,0:T(8,128)S(1)} %shard_map.44.refs_0_.refs_7_, f32[2,8,512]{2,1,0:T(8,128)S(1)} %collective-permute-done.1.refs_1_, f32[2,8,512]{2,1,0:T(8,128)S(1)} %collective-permute-done.2.refs_2_, ...), custom_call_target="tpu_custom_call" | custom-call | flops 2147483648 | bytes 12582912 | tf_op jit(solution)/shard_map/pallas_call | solution.py:429
  50.9 0.5 collective-permute-start.5
  51.5 0.4 collective-permute-start.7
  51.9 0.9 collective-permute-done.5.refs_8_
  52.9 0.4 collective-permute-done.6.refs_9_
  53.3 0.4 collective-permute-done.7.refs_10_
  53.6 4.4 %shard_map.48 = f32[1,264,1024]{2,1,0:T(8,128)S(1)} custom-call(f32[2,8,512]{2,1,0:T(8,128)S(1)} %shard_map.44.refs_0_.refs_7_, f32[2,8,512]{2,1,0:T(8,128)S(1)} %collective-permute-done.1.refs_1_, f32[2,8,512]{2,1,0:T(8,128)S(1)} %collective-permute-done.2.refs_2_, f32[2,8,512]{2,1,0:T(8,128)S(1)} %collective-permute-done.3.refs_3_, ...), custom_call_target="tpu_custom_call" | custom-call | tf_op jit(solution)/shard_map/pallas_call | solution.py:429
  58.0 1.6 %collective-permute-done.9.refs_1_ = bf16[272,1024]{1,0:T(8,128)(2,1)S(1)} collective-permute-done((bf16[272,1024]{1,0:T(8,128)(2,1)S(1)}, bf16[272,1024]{1,0:T(8,128)(2,1)S(1)}, u32[]{:S(2)}, u32[]{:S(2)}) %collective-permute-start.9) | collective-permute-done | bytes 557088 | tf_op jit(solution)/shard_map/ppermute | solution.py:600
  59.6 0.9 shard_map.49.refs_0_
  60.6 1.6 %collective-permute-start.11 = (bf16[256,1024]{1,0:T(8,128)(2,1)S(1)}, bf16[256,1024]{1,0:T(8,128)(2,1)S(1)}, u32[]{:S(2)}, u32[]{:S(2)}) collective-permute-start(bf16[256,1024]{1,0:T(8,128)(2,1)S(1)} %shard_map.49.refs_0_), channel_id=1, source_target_pairs={{0,16},{8,24},{16,0},{24,8},{1,17},{9,25},{17,1},{25,9},{2,18},{10... | collective-permute-start | bytes 1572872 | tf_op jit(solution)/shard_map/ppermute | solution.py:600
  62.2 0.3 collective-permute-done.10.refs_1_
  62.5 9.1 %shard_map.50 = (f32[1024,4096]{1,0:T(8,128)}, f32[2,8,512]{2,1,0:T(8,128)S(1)}) custom-call(bf16[256,1024]{1,0:T(8,128)(2,1)S(1)} %shard_map.49.refs_0_, bf16[256,1024]{1,0:T(8,128)(2,1)S(1)} %collective-permute-done.10.refs_1_, bf16[4096,1024]{1,0:T(8,128)(2,1)S(1)} %bitcast.9), custom_call_target="tpu_custom_call" | custom-call | flops 4294967296 | bytes 16777216 | tf_op jit(solution)/shard_map/pallas_call | solution.py:218
  71.6 3.4 %collective-permute-done.11.value_ref = bf16[256,1024]{1,0:T(8,128)(2,1)S(1)} collective-permute-done((bf16[256,1024]{1,0:T(8,128)(2,1)S(1)}, bf16[256,1024]{1,0:T(8,128)(2,1)S(1)}, u32[]{:S(2)}, u32[]{:S(2)}) %collective-permute-start.11) | collective-permute-done | bytes 524320 | tf_op jit(solution)/shard_map/ppermute | solution.py:600
  75.0 1.9 %collective-permute-done.12.refs_1_ = bf16[256,1024]{1,0:T(8,128)(2,1)S(1)} collective-permute-done((bf16[256,1024]{1,0:T(8,128)(2,1)S(1)}, bf16[256,1024]{1,0:T(8,128)(2,1)S(1)}, u32[]{:S(2)}, u32[]{:S(2)}) %collective-permute-start.12) | collective-permute-done | bytes 524320 | tf_op jit(solution)/shard_map/ppermute | solution.py:596
  76.9 8.8 %shard_map.52 = (f32[1024,4096]{1,0:T(8,128)}, f32[2,8,512]{2,1,0:T(8,128)S(1)}) custom-call(bf16[256,1024]{1,0:T(8,128)(2,1)S(1)} %shard_map.51.refs_0_, bf16[256,1024]{1,0:T(8,128)(2,1)S(1)} %collective-permute-done.12.refs_1_, bf16[4096,1024]{1,0:T(8,128)(2,1)S(1)} %bitcast.9, f32[1024,4096]{1,0:T(8,128)} %get-tuple-element.30.refs_3_), custom_call_target="tpu_custom_call", output_to_operand_aliasing={{0}: (3, {})} | custom-call | flops 4294967296 | bytes 16777216 | tf_op jit(solution)/shard_map/pallas_call | solution.py:218
  85.7 1.5 %collective-permute-start.13 = (f32[2,8,512]{2,1,0:T(8,128)S(1)}, f32[2,8,512]{2,1,0:T(8,128)S(1)}, u32[]{:S(2)}, u32[]{:S(2)}) collective-permute-start(f32[2,8,512]{2,1,0:T(8,128)S(1)} %shard_map.53.refs_0_), channel_id=1, source_target_pairs={{0,1},{1,0},{2,3},{3,2},{4,5},{5,4},{6,7},{7,6},{8,9},{9,8},{10,11... | collective-permute-start | bytes 98312 | tf_op jit(solution)/shard_map/ppermute | solution.py:613
  87.3 2.4 %collective-permute-done.13.refs_1_ = f32[2,8,512]{2,1,0:T(8,128)S(1)} collective-permute-done((f32[2,8,512]{2,1,0:T(8,128)S(1)}, f32[2,8,512]{2,1,0:T(8,128)S(1)}, u32[]{:S(2)}, u32[]{:S(2)}) %collective-permute-start.13) | collective-permute-done | bytes 32800 | tf_op jit(solution)/shard_map/ppermute | solution.py:613
  89.7 1.5 %collective-permute-start.16 = (f32[2,8,512]{2,1,0:T(8,128)S(1)}, f32[2,8,512]{2,1,0:T(8,128)S(1)}, u32[]{:S(2)}, u32[]{:S(2)}) collective-permute-start(f32[2,8,512]{2,1,0:T(8,128)S(1)} %shard_map.54.refs_0_.refs_8_), channel_id=1, source_target_pairs={{0,6},{1,7},{2,4},{3,5},{4,2},{5,3},{6,0},{7,1},{8,14},{9,15},{10,... | collective-permute-start | bytes 98312 | tf_op jit(solution)/shard_map/ppermute | solution.py:613
  91.2 0.6 collective-permute-start.15
  91.9 2.3 %collective-permute-start.14 = (f32[2,8,512]{2,1,0:T(8,128)S(1)}, f32[2,8,512]{2,1,0:T(8,128)S(1)}, u32[]{:S(2)}, u32[]{:S(2)}) collective-permute-start(f32[2,8,512]{2,1,0:T(8,128)S(1)} %shard_map.54.refs_0_.refs_8_), channel_id=1, source_target_pairs={{0,2},{1,3},{2,0},{3,1},{4,6},{5,7},{6,4},{7,5},{8,10},{9,11},{10,... | collective-permute-start | bytes 98312 | tf_op jit(solution)/shard_map/ppermute | solution.py:613
  94.2 1.3 %collective-permute-done.16.refs_3_ = f32[2,8,512]{2,1,0:T(8,128)S(1)} collective-permute-done((f32[2,8,512]{2,1,0:T(8,128)S(1)}, f32[2,8,512]{2,1,0:T(8,128)S(1)}, u32[]{:S(2)}, u32[]{:S(2)}) %collective-permute-start.16) | collective-permute-done | bytes 32800 | tf_op jit(solution)/shard_map/ppermute | solution.py:613
  95.5 0.6 collective-permute-done.15.refs_2_
  96.1 0.3 collective-permute-done.14.refs_1_
  96.4 8.5 %shard_map.55 = (f32[1,1032,256]{2,1,0:T(8,128)S(1)}, f32[1,1032,256]{2,1,0:T(8,128)S(1)}, bf16[1024,4096]{1,0:T(8,128)(2,1)S(1)}, f32[1,1024]{1,0:T(1,128)S(1)}) custom-call(f32[2,8,512]{2,1,0:T(8,128)S(1)} %shard_map.54.refs_0_.refs_8_, f32[2,8,512]{2,1,0:T(8,128)S(1)} %collective-permute-done.14.refs_1_, ...), custom_call_target="tpu_custom_call" | custom-call | flops 4294967296 | bytes 20971520 | tf_op jit(solution)/shard_map/pallas_call | solution.py:429
  105.0 2.4 %shard_map.56 = (f32[1,1032,256]{2,1,0:T(8,128)S(1)}, bf16[1024,4096]{1,0:T(8,128)(2,1)S(1)}) custom-call(bf16[1024,4096]{1,0:T(8,128)(2,1)S(1)} %get-tuple-element.33.kept_ref, f32[1,1024]{1,0:T(1,128)S(1)} %get-tuple-element.34.mass_ref, bf16[4096,1024]{1,0:T(8,128)(2,1)S(1)} %bitcast.9, ...), custom_call_target="tpu_custom_call", output_to_operand_aliasing={{1}: (0, {})} | custom-call | flops 2147483648 | bytes 10485760 | tf_op jit(solution)/shard_map/pallas_call | solution.py:385
  107.4 0.5 collective-permute-start.18
  107.9 0.8 shard_map.57._.refs_3_
  108.7 1.6 %collective-permute-start.19 = (bf16[1040,256]{1,0:T(8,128)(2,1)S(1)}, bf16[1040,256]{1,0:T(8,128)(2,1)S(1)}, u32[]{:S(2)}, u32[]{:S(2)}) collective-permute-start(bf16[1040,256]{1,0:T(8,128)(2,1)S(1)} %bitcast.11), channel_id=1, source_target_pairs={{0,16},{8,24},{16,0},{24,8},{1,17},{9,25},{17,1},{25,9},{2,18},{10... | collective-permute-start | bytes 1597448 | tf_op jit(solution)/shard_map/ppermute | solution.py:600
  110.3 0.6 copy.8
  110.9 2.4 %shard_map.58 = (f32[1,1032,256]{2,1,0:T(8,128)S(1)}, bf16[1024,4096]{1,0:T(8,128)(2,1)S(1)}) custom-call(bf16[1024,4096]{1,0:T(8,128)(2,1)S(1)} %get-tuple-element.36.kept_ref, f32[1,1024]{1,0:T(1,128)S(1)} %get-tuple-element.34.mass_ref, bf16[4096,1024]{1,0:T(8,128)(2,1)S(1)} %bitcast.9, ...), custom_call_target="tpu_custom_call", output_to_operand_aliasing={{1}: (0, {})} | custom-call | flops 2147483648 | bytes 10485760 | tf_op jit(solution)/shard_map/pallas_call | solution.py:385
  113.3 9.5 %collective-permute-done.19.refs_2_ = bf16[1040,256]{1,0:T(8,128)(2,1)S(1)} collective-permute-done((bf16[1040,256]{1,0:T(8,128)(2,1)S(1)}, bf16[1040,256]{1,0:T(8,128)(2,1)S(1)}, u32[]{:S(2)}, u32[]{:S(2)}) %collective-permute-start.19) | collective-permute-done | bytes 532512 | tf_op jit(solution)/shard_map/ppermute | solution.py:600
  122.8 2.0 %shard_map.59 = f32[1024,256]{1,0:T(8,128)} custom-call(f32[1032,256]{1,0:T(8,128)S(1)} %bitcast.14, f32[1032,256]{1,0:T(8,128)S(1)} %bitcast.13, bf16[1040,256]{1,0:T(8,128)(2,1)S(1)} %collective-permute-done.19.refs_2_, bf16[1,1040,256]{2,1,0:T(8,128)(2,1)S(1)} %shard_map.57._.refs_3_), custom_call_target="tpu_custom_call" | custom-call | flops 7864320 | bytes 3670016 | tf_op jit(solution)/shard_map/pallas_call | solution.py:542
  (21 shorter events, 0.7 us)
Async XLA Ops:
  0.6 2.2 %copy-start = (f32[1024,1024]{1,0:T(8,128)S(1)}, f32[1024,1024]{1,0:T(8,128)}, u32[]{:S(2)}) copy-start(f32[1024,1024]{1,0:T(8,128)} %in_ref.1) | copy-start | bytes 12582916
  2.8 2.2 %slice-start = ((s8[8388608]{0:T(1024)(128)(4,1)}), s8[4194304]{0:T(1024)(128)(4,1)S(1)}, s32[]{:S(2)}) async-start(s8[8388608]{0:T(1024)(128)(4,1)} %bitcast.8), calls=%async_computation | async-start | bytes 8388608
  3.1 3.3 %slice-start.1 = ((s8[8388608]{0:T(1024)(128)(4,1)}), s8[4194304]{0:T(1024)(128)(4,1)S(1)}, s32[]{:S(2)}) async-start(s8[8388608]{0:T(1024)(128)(4,1)} %bitcast.8), calls=%async_computation.1 | async-start | bytes 8388608
  20.6 4.9 %collective-permute-start = (f32[2,8,512]{2,1,0:T(8,128)S(1)}, f32[2,8,512]{2,1,0:T(8,128)S(1)}, u32[]{:S(2)}, u32[]{:S(2)}) collective-permute-start(f32[2,8,512]{2,1,0:T(8,128)S(1)} %get-tuple-element.21.refs_0_.refs_4_), channel_id=1, source_target_pairs={{0,1},{1,0},{2,3},{3,2},{4,5},{5,4},{6,7},{7,6},{8,9},{9,8},{10,11... | collective-permute-start | bytes 98312 | tf_op jit(solution)/shard_map/ppermute | solution.py:613
  25.5 6.1 %collective-permute-start.3 = (f32[2,8,512]{2,1,0:T(8,128)S(1)}, f32[2,8,512]{2,1,0:T(8,128)S(1)}, u32[]{:S(2)}, u32[]{:S(2)}) collective-permute-start(f32[2,8,512]{2,1,0:T(8,128)S(1)} %shard_map.44.refs_0_.refs_7_), channel_id=1, source_target_pairs={{0,6},{1,7},{2,4},{3,5},{4,2},{5,3},{6,0},{7,1},{8,14},{9,15},{10,... | collective-permute-start | bytes 98312 | tf_op jit(solution)/shard_map/ppermute | solution.py:613
  29.7 4.8 %collective-permute-start.2 = (f32[2,8,512]{2,1,0:T(8,128)S(1)}, f32[2,8,512]{2,1,0:T(8,128)S(1)}, u32[]{:S(2)}, u32[]{:S(2)}) collective-permute-start(f32[2,8,512]{2,1,0:T(8,128)S(1)} %shard_map.44.refs_0_.refs_7_), channel_id=1, source_target_pairs={{0,4},{1,5},{2,6},{3,7},{4,0},{5,1},{6,2},{7,3},{8,12},{9,13},{10,... | collective-permute-start | bytes 98312 | tf_op jit(solution)/shard_map/ppermute | solution.py:613
  29.7 4.8 %collective-permute-start.1 = (f32[2,8,512]{2,1,0:T(8,128)S(1)}, f32[2,8,512]{2,1,0:T(8,128)S(1)}, u32[]{:S(2)}, u32[]{:S(2)}) collective-permute-start(f32[2,8,512]{2,1,0:T(8,128)S(1)} %shard_map.44.refs_0_.refs_7_), channel_id=1, source_target_pairs={{0,2},{1,3},{2,0},{3,1},{4,6},{5,7},{6,4},{7,5},{8,10},{9,11},{10,... | collective-permute-start | bytes 98312 | tf_op jit(solution)/shard_map/ppermute | solution.py:613
  41.4 2.8 %collective-permute-start.4 = (f32[1,264,1024]{2,1,0:T(8,128)S(1)}, f32[1,264,1024]{2,1,0:T(8,128)S(1)}, u32[]{:S(2)}, u32[]{:S(2)}) collective-permute-start(f32[1,264,1024]{2,1,0:T(8,128)S(1)} %get-tuple-element.24.after_ref), channel_id=1, source_target_pairs={{0,8},{8,0},{16,24},{24,16},{1,9},{9,1},{17,25},{25,17},{2,10},{10... | collective-permute-start | bytes 3244040 | tf_op jit(solution)/shard_map/ppermute | solution.py:596
  44.9 14.7 %collective-permute-start.9 = (bf16[272,1024]{1,0:T(8,128)(2,1)S(1)}, bf16[272,1024]{1,0:T(8,128)(2,1)S(1)}, u32[]{:S(2)}, u32[]{:S(2)}) collective-permute-start(bf16[272,1024]{1,0:T(8,128)(2,1)S(1)} %bitcast.10), channel_id=1, source_target_pairs={{0,16},{8,24},{16,0},{24,8},{1,17},{9,25},{17,1},{25,9},{2,18},{10... | collective-permute-start | bytes 1671176 | tf_op jit(solution)/shard_map/ppermute | solution.py:600
  50.9 2.8 %collective-permute-start.8 = (f32[72,1024]{1,0:T(8,128)S(1)}, f32[72,1024]{1,0:T(8,128)S(1)}, u32[]{:S(2)}, u32[]{:S(2)}) collective-permute-start(f32[72,1024]{1,0:T(8,128)S(1)} %get-tuple-element.28), channel_id=1, source_target_pairs={{0,8},{8,0},{16,24},{24,16},{1,9},{9,1},{17,25},{25,17},{2,10},{10... | collective-permute-start | bytes 884744 | tf_op jit(solution)/shard_map/ppermute | solution.py:596
  50.9 1.9 %collective-permute-start.5 = (f32[64,1024]{1,0:T(8,128)S(1)}, f32[64,1024]{1,0:T(8,128)S(1)}, u32[]{:S(2)}, u32[]{:S(2)}) collective-permute-start(f32[64,1024]{1,0:T(8,128)S(1)} %get-tuple-element.25), channel_id=1, source_target_pairs={{0,8},{8,0},{16,24},{24,16},{1,9},{9,1},{17,25},{25,17},{2,10},{10... | collective-permute-start | bytes 786440 | tf_op jit(solution)/shard_map/ppermute | solution.py:596
  51.4 1.8 %collective-permute-start.6 = (f32[64,1024]{1,0:T(8,128)S(1)}, f32[64,1024]{1,0:T(8,128)S(1)}, u32[]{:S(2)}, u32[]{:S(2)}) collective-permute-start(f32[64,1024]{1,0:T(8,128)S(1)} %get-tuple-element.26), channel_id=1, source_target_pairs={{0,8},{8,0},{16,24},{24,16},{1,9},{9,1},{17,25},{25,17},{2,10},{10... | collective-permute-start | bytes 786440 | tf_op jit(solution)/shard_map/ppermute | solution.py:596
  51.5 2.1 %collective-permute-start.7 = (f32[64,1024]{1,0:T(8,128)S(1)}, f32[64,1024]{1,0:T(8,128)S(1)}, u32[]{:S(2)}, u32[]{:S(2)}) collective-permute-start(f32[64,1024]{1,0:T(8,128)S(1)} %get-tuple-element.27), channel_id=1, source_target_pairs={{0,8},{8,0},{16,24},{24,16},{1,9},{9,1},{17,25},{25,17},{2,10},{10... | collective-permute-start | bytes 786440 | tf_op jit(solution)/shard_map/ppermute | solution.py:596
  60.5 2.0 %collective-permute-start.10 = (bf16[256,1024]{1,0:T(8,128)(2,1)S(1)}, bf16[256,1024]{1,0:T(8,128)(2,1)S(1)}, u32[]{:S(2)}, u32[]{:S(2)}) collective-permute-start(bf16[256,1024]{1,0:T(8,128)(2,1)S(1)} %shard_map.49.refs_0_), channel_id=1, source_target_pairs={{0,8},{8,0},{16,24},{24,16},{1,9},{9,1},{17,25},{25,17},{2,10},{10... | collective-permute-start | bytes 1572872 | tf_op jit(solution)/shard_map/ppermute | solution.py:596
  60.6 14.3 %collective-permute-start.11 = (bf16[256,1024]{1,0:T(8,128)(2,1)S(1)}, bf16[256,1024]{1,0:T(8,128)(2,1)S(1)}, u32[]{:S(2)}, u32[]{:S(2)}) collective-permute-start(bf16[256,1024]{1,0:T(8,128)(2,1)S(1)} %shard_map.49.refs_0_), channel_id=1, source_target_pairs={{0,16},{8,24},{16,0},{24,8},{1,17},{9,25},{17,1},{25,9},{2,18},{10... | collective-permute-start | bytes 1572872 | tf_op jit(solution)/shard_map/ppermute | solution.py:600
  75.0 1.9 %collective-permute-start.12 = (bf16[256,1024]{1,0:T(8,128)(2,1)S(1)}, bf16[256,1024]{1,0:T(8,128)(2,1)S(1)}, u32[]{:S(2)}, u32[]{:S(2)}) collective-permute-start(bf16[256,1024]{1,0:T(8,128)(2,1)S(1)} %shard_map.51.refs_0_), channel_id=1, source_target_pairs={{0,8},{8,0},{16,24},{24,16},{1,9},{9,1},{17,25},{25,17},{2,10},{10... | collective-permute-start | bytes 1572872 | tf_op jit(solution)/shard_map/ppermute | solution.py:596
  85.7 4.0 %collective-permute-start.13 = (f32[2,8,512]{2,1,0:T(8,128)S(1)}, f32[2,8,512]{2,1,0:T(8,128)S(1)}, u32[]{:S(2)}, u32[]{:S(2)}) collective-permute-start(f32[2,8,512]{2,1,0:T(8,128)S(1)} %shard_map.53.refs_0_), channel_id=1, source_target_pairs={{0,1},{1,0},{2,3},{3,2},{4,5},{5,4},{6,7},{7,6},{8,9},{9,8},{10,11... | collective-permute-start | bytes 98312 | tf_op jit(solution)/shard_map/ppermute | solution.py:613
  89.7 5.8 %collective-permute-start.16 = (f32[2,8,512]{2,1,0:T(8,128)S(1)}, f32[2,8,512]{2,1,0:T(8,128)S(1)}, u32[]{:S(2)}, u32[]{:S(2)}) collective-permute-start(f32[2,8,512]{2,1,0:T(8,128)S(1)} %shard_map.54.refs_0_.refs_8_), channel_id=1, source_target_pairs={{0,6},{1,7},{2,4},{3,5},{4,2},{5,3},{6,0},{7,1},{8,14},{9,15},{10,... | collective-permute-start | bytes 98312 | tf_op jit(solution)/shard_map/ppermute | solution.py:613
  91.2 4.8 %collective-permute-start.15 = (f32[2,8,512]{2,1,0:T(8,128)S(1)}, f32[2,8,512]{2,1,0:T(8,128)S(1)}, u32[]{:S(2)}, u32[]{:S(2)}) collective-permute-start(f32[2,8,512]{2,1,0:T(8,128)S(1)} %shard_map.54.refs_0_.refs_8_), channel_id=1, source_target_pairs={{0,4},{1,5},{2,6},{3,7},{4,0},{5,1},{6,2},{7,3},{8,12},{9,13},{10,... | collective-permute-start | bytes 98312 | tf_op jit(solution)/shard_map/ppermute | solution.py:613
  91.9 4.5 %collective-permute-start.14 = (f32[2,8,512]{2,1,0:T(8,128)S(1)}, f32[2,8,512]{2,1,0:T(8,128)S(1)}, u32[]{:S(2)}, u32[]{:S(2)}) collective-permute-start(f32[2,8,512]{2,1,0:T(8,128)S(1)} %shard_map.54.refs_0_.refs_8_), channel_id=1, source_target_pairs={{0,2},{1,3},{2,0},{3,1},{4,6},{5,7},{6,4},{7,5},{8,10},{9,11},{10,... | collective-permute-start | bytes 98312 | tf_op jit(solution)/shard_map/ppermute | solution.py:613
  104.9 3.0 %collective-permute-start.17 = (f32[1,1032,256]{2,1,0:T(8,128)S(1)}, f32[1,1032,256]{2,1,0:T(8,128)S(1)}, u32[]{:S(2)}, u32[]{:S(2)}) collective-permute-start(f32[1,1032,256]{2,1,0:T(8,128)S(1)} %get-tuple-element.35._), channel_id=1, source_target_pairs={{0,8},{8,0},{16,24},{24,16},{1,9},{9,1},{17,25},{25,17},{2,10},{10... | collective-permute-start | bytes 3170312 | tf_op jit(solution)/shard_map/ppermute | solution.py:596
  107.4 5.9 %collective-permute-start.18 = (f32[1,1032,256]{2,1,0:T(8,128)S(1)}, f32[1,1032,256]{2,1,0:T(8,128)S(1)}, u32[]{:S(2)}, u32[]{:S(2)}) collective-permute-start(f32[1,1032,256]{2,1,0:T(8,128)S(1)} %get-tuple-element.38.after_ref), channel_id=1, source_target_pairs={{0,8},{8,0},{16,24},{24,16},{1,9},{9,1},{17,25},{25,17},{2,10},{10... | collective-permute-start | bytes 3170312 | tf_op jit(solution)/shard_map/ppermute | solution.py:596
  108.7 14.1 %collective-permute-start.19 = (bf16[1040,256]{1,0:T(8,128)(2,1)S(1)}, bf16[1040,256]{1,0:T(8,128)(2,1)S(1)}, u32[]{:S(2)}, u32[]{:S(2)}) collective-permute-start(bf16[1040,256]{1,0:T(8,128)(2,1)S(1)} %bitcast.11), channel_id=1, source_target_pairs={{0,16},{8,24},{16,0},{24,8},{1,17},{9,25},{17,1},{25,9},{2,18},{10... | collective-permute-start | bytes 1597448 | tf_op jit(solution)/shard_map/ppermute | solution.py:600

commit v5 on v4

--- a/solution.py
+++ b/solution.py
@@ -118,7 +118,7 @@
 def score_points(raw, units, x_ref, e_parts, stat_ref, stage, semaphores):
     line = stat_ref.shape[2]
     lines = stage.shape[0]
-    sub = divisor(line, 256)
+    sub = divisor(line, 512)
 
     def copies(number, slot):
         columns = pl.ds(pl.multiple_of(number * line, line), line)

time: 125 us -> 125 us (level)
  no operation moved by 1% of the time
where the time goes in v5:
time: 125 us
  Pallas kernels  66.2 us (53%)
  waiting for transfers between devices  31.8 us (25%)
  starting transfers between devices  20.4 us (16%)
  local copies, waits for them, and re-layouts  5.26 us (4%)
    pallas_call x3, Pallas kernels, scores(): pl.pallas_call(body, in_specs=[VMEM] * (count + 1) + [ANY] * len(more), o...  32.1 us
    pallas_call x4, Pallas kernels, weigh(): pl.pallas_call(functools.partial(weigh_body, by_rows, len(stats), n_tops,...  24.2 us
    ppermute x3, waiting for transfers between devices, to_chip(): return lax.ppermute(value, 'pts', moves)  14.5 us
    ppermute x8, starting transfers between devices, over_centroids(): sets.append(lax.ppermute(sets[0], 'cen', moves))  13.9 us
    ppermute x8, waiting for transfers between devices, over_centroids(): sets.append(lax.ppermute(sets[0], 'cen', moves))  10.7 us
    ppermute x9, waiting for transfers between devices, to_partner(): return lax.ppermute(value, 'pts', [(i, i ^ 1) for i in range(n_pts)])  6.61 us
    unnamed x7, local copies, waits for them, and re-layouts  5.26 us
    pallas_call x2, Pallas kernels, weigh_kept(): pl.pallas_call(functools.partial(weigh_kept_body, kind, extra), in_specs=...  4.74 us
  transfers between devices with their start and end apart: 20, of which 16 were waited for; matrix products, arithmetic and copies ran while one was open for 0% of the time, Pallas kernels for 19%

profile of v5, /device:TPU:0, one launch (start us, length us, event | category | flops | bytes accessed | tf_op | source)
XLA Modules:
  0.0 124.8 jit_solution(17979398695153312520)
XLA Ops:
  0.6 2.2 %copy-done = f32[1024,1024]{1,0:T(8,128)S(1)} copy-done((f32[1024,1024]{1,0:T(8,128)S(1)}, f32[1024,1024]{1,0:T(8,128)}, u32[]{:S(2)}) %copy-start) | copy-done | bytes 4194328
  3.1 0.3 multiply_reduce_fusion
  3.5 0.4 shard_map.42.units
  3.9 1.1 slice-done
  5.0 1.3 %slice-done.1 = s8[4194304]{0:T(1024)(128)(4,1)S(1)} async-done(((s8[8388608]{0:T(1024)(128)(4,1)}), s8[4194304]{0:T(1024)(128)(4,1)S(1)}, s32[]{:S(2)}) %slice-start.1) | async-done | bytes 4194328
  6.4 14.2 %shard_map.43 = (f32[1024,4096]{1,0:T(8,128)}, f32[2,8,512]{2,1,0:T(8,128)S(1)}) custom-call(bf16[1024,1024]{1,0:T(8,128)(2,1)S(1)} %shard_map.42.units, bf16[4096,1024]{1,0:T(8,128)(2,1)S(1)} %bitcast.9), custom_call_target="tpu_custom_call" | custom-call | flops 8589934592 | bytes 25165824 | tf_op jit(solution)/shard_map/pallas_call | solution.py:218
  20.6 3.0 %collective-permute-start = (f32[2,8,512]{2,1,0:T(8,128)S(1)}, f32[2,8,512]{2,1,0:T(8,128)S(1)}, u32[]{:S(2)}, u32[]{:S(2)}) collective-permute-start(f32[2,8,512]{2,1,0:T(8,128)S(1)} %get-tuple-element.21.refs_0_.refs_4_), channel_id=1, source_target_pairs={{0,1},{1,0},{2,3},{3,2},{4,5},{5,4},{6,7},{7,6},{8,9},{9,8},{10,11... | collective-permute-start | bytes 98312 | tf_op jit(solution)/shard_map/ppermute | solution.py:613
  23.6 1.9 %collective-permute-done.refs_1_ = f32[2,8,512]{2,1,0:T(8,128)S(1)} collective-permute-done((f32[2,8,512]{2,1,0:T(8,128)S(1)}, f32[2,8,512]{2,1,0:T(8,128)S(1)}, u32[]{:S(2)}, u32[]{:S(2)}) %collective-permute-start) | collective-permute-done | bytes 32800 | tf_op jit(solution)/shard_map/ppermute | solution.py:613
  25.5 4.2 %collective-permute-start.3 = (f32[2,8,512]{2,1,0:T(8,128)S(1)}, f32[2,8,512]{2,1,0:T(8,128)S(1)}, u32[]{:S(2)}, u32[]{:S(2)}) collective-permute-start(f32[2,8,512]{2,1,0:T(8,128)S(1)} %shard_map.44.refs_0_.refs_7_), channel_id=1, source_target_pairs={{0,6},{1,7},{2,4},{3,5},{4,2},{5,3},{6,0},{7,1},{8,14},{9,15},{10,... | collective-permute-start | bytes 98312 | tf_op jit(solution)/shard_map/ppermute | solution.py:613
  29.7 0.6 collective-permute-start.1
  30.3 1.3 %collective-permute-done.3.refs_3_ = f32[2,8,512]{2,1,0:T(8,128)S(1)} collective-permute-done((f32[2,8,512]{2,1,0:T(8,128)S(1)}, f32[2,8,512]{2,1,0:T(8,128)S(1)}, u32[]{:S(2)}, u32[]{:S(2)}) %collective-permute-start.3) | collective-permute-done | bytes 32800 | tf_op jit(solution)/shard_map/ppermute | solution.py:613
  31.6 2.9 %collective-permute-done.2.refs_2_ = f32[2,8,512]{2,1,0:T(8,128)S(1)} collective-permute-done((f32[2,8,512]{2,1,0:T(8,128)S(1)}, f32[2,8,512]{2,1,0:T(8,128)S(1)}, u32[]{:S(2)}, u32[]{:S(2)}) %collective-permute-start.2) | collective-permute-done | bytes 32800 | tf_op jit(solution)/shard_map/ppermute | solution.py:613
  34.5 6.9 %shard_map.45 = (f32[1,264,1024]{2,1,0:T(8,128)S(1)}, f32[1,264,1024]{2,1,0:T(8,128)S(1)}) custom-call(f32[2,8,512]{2,1,0:T(8,128)S(1)} %shard_map.44.refs_0_.refs_7_, f32[2,8,512]{2,1,0:T(8,128)S(1)} %collective-permute-done.1.refs_1_, f32[2,8,512]{2,1,0:T(8,128)S(1)} %collective-permute-done.2.refs_2_, f32[2,8,512]{2,1,0:T(8,128)S(1)} %collective-permute-done.3.refs_3_, ...), custom_call_target="tpu_custom_call" | custom-call | flops 4294967296 | bytes 16777216 | tf_op jit(solution)/shard_map/pallas_call | solution.py:429
  41.5 2.7 %collective-permute-done.4.theirs_ref = f32[1,264,1024]{2,1,0:T(8,128)S(1)} collective-permute-done((f32[1,264,1024]{2,1,0:T(8,128)S(1)}, f32[1,264,1024]{2,1,0:T(8,128)S(1)}, u32[]{:S(2)}, u32[]{:S(2)}) %collective-permute-start.4) | collective-permute-done | bytes 1081376 | tf_op jit(solution)/shard_map/ppermute | solution.py:596
  44.2 0.7 shard_map.46.refs_7_.refs_2_
  44.9 1.6 %collective-permute-start.9 = (bf16[272,1024]{1,0:T(8,128)(2,1)S(1)}, bf16[272,1024]{1,0:T(8,128)(2,1)S(1)}, u32[]{:S(2)}, u32[]{:S(2)}) collective-permute-start(bf16[272,1024]{1,0:T(8,128)(2,1)S(1)} %bitcast.10), channel_id=1, source_target_pairs={{0,16},{8,24},{16,0},{24,8},{1,17},{9,25},{17,1},{25,9},{2,18},{10... | collective-permute-start | bytes 1671176 | tf_op jit(solution)/shard_map/ppermute | solution.py:600
  46.5 4.4 %shard_map.47 = (f32[64,1024]{1,0:T(8,128)S(1)}, f32[64,1024]{1,0:T(8,128)S(1)}, f32[64,1024]{1,0:T(8,128)S(1)}, f32[72,1024]{1,0:T(8,128)S(1)}) custom-call(f32[2,8,512]{2,1,0:T(8,128)S(1)} %shard_map.44.refs_0_.refs_7_, f32[2,8,512]{2,1,0:T(8,128)S(1)} %collective-permute-done.1.refs_1_, f32[2,8,512]{2,1,0:T(8,128)S(1)} %collective-permute-done.2.refs_2_, ...), custom_call_target="tpu_custom_call" | custom-call | flops 2147483648 | bytes 12582912 | tf_op jit(solution)/shard_map/pallas_call | solution.py:429
  50.9 0.5 collective-permute-start.5
  51.5 0.4 collective-permute-start.7
  51.9 0.9 collective-permute-done.5.refs_8_
  52.9 0.4 collective-permute-done.6.refs_9_
  53.2 0.4 collective-permute-done.7.refs_10_
  53.6 4.4 %shard_map.48 = f32[1,264,1024]{2,1,0:T(8,128)S(1)} custom-call(f32[2,8,512]{2,1,0:T(8,128)S(1)} %shard_map.44.refs_0_.refs_7_, f32[2,8,512]{2,1,0:T(8,128)S(1)} %collective-permute-done.1.refs_1_, f32[2,8,512]{2,1,0:T(8,128)S(1)} %collective-permute-done.2.refs_2_, f32[2,8,512]{2,1,0:T(8,128)S(1)} %collective-permute-done.3.refs_3_, ...), custom_call_target="tpu_custom_call" | custom-call | tf_op jit(solution)/shard_map/pallas_call | solution.py:429
  58.0 1.6 %collective-permute-done.9.refs_1_ = bf16[272,1024]{1,0:T(8,128)(2,1)S(1)} collective-permute-done((bf16[272,1024]{1,0:T(8,128)(2,1)S(1)}, bf16[272,1024]{1,0:T(8,128)(2,1)S(1)}, u32[]{:S(2)}, u32[]{:S(2)}) %collective-permute-start.9) | collective-permute-done | bytes 557088 | tf_op jit(solution)/shard_map/ppermute | solution.py:600
  59.6 0.9 shard_map.49.refs_0_
  60.6 1.6 %collective-permute-start.11 = (bf16[256,1024]{1,0:T(8,128)(2,1)S(1)}, bf16[256,1024]{1,0:T(8,128)(2,1)S(1)}, u32[]{:S(2)}, u32[]{:S(2)}) collective-permute-start(bf16[256,1024]{1,0:T(8,128)(2,1)S(1)} %shard_map.49.refs_0_), channel_id=1, source_target_pairs={{0,16},{8,24},{16,0},{24,8},{1,17},{9,25},{17,1},{25,9},{2,18},{10... | collective-permute-start | bytes 1572872 | tf_op jit(solution)/shard_map/ppermute | solution.py:600
  62.2 0.3 collective-permute-done.10.refs_1_
  62.5 9.0 %shard_map.50 = (f32[1024,4096]{1,0:T(8,128)}, f32[2,8,512]{2,1,0:T(8,128)S(1)}) custom-call(bf16[256,1024]{1,0:T(8,128)(2,1)S(1)} %shard_map.49.refs_0_, bf16[256,1024]{1,0:T(8,128)(2,1)S(1)} %collective-permute-done.10.refs_1_, bf16[4096,1024]{1,0:T(8,128)(2,1)S(1)} %bitcast.9), custom_call_target="tpu_custom_call" | custom-call | flops 4294967296 | bytes 16777216 | tf_op jit(solution)/shard_map/pallas_call | solution.py:218
  71.5 3.4 %collective-permute-done.11.value_ref = bf16[256,1024]{1,0:T(8,128)(2,1)S(1)} collective-permute-done((bf16[256,1024]{1,0:T(8,128)(2,1)S(1)}, bf16[256,1024]{1,0:T(8,128)(2,1)S(1)}, u32[]{:S(2)}, u32[]{:S(2)}) %collective-permute-start.11) | collective-permute-done | bytes 524320 | tf_op jit(solution)/shard_map/ppermute | solution.py:600
  74.9 1.9 %collective-permute-done.12.refs_1_ = bf16[256,1024]{1,0:T(8,128)(2,1)S(1)} collective-permute-done((bf16[256,1024]{1,0:T(8,128)(2,1)S(1)}, bf16[256,1024]{1,0:T(8,128)(2,1)S(1)}, u32[]{:S(2)}, u32[]{:S(2)}) %collective-permute-start.12) | collective-permute-done | bytes 524320 | tf_op jit(solution)/shard_map/ppermute | solution.py:596
  76.8 8.8 %shard_map.52 = (f32[1024,4096]{1,0:T(8,128)}, f32[2,8,512]{2,1,0:T(8,128)S(1)}) custom-call(bf16[256,1024]{1,0:T(8,128)(2,1)S(1)} %shard_map.51.refs_0_, bf16[256,1024]{1,0:T(8,128)(2,1)S(1)} %collective-permute-done.12.refs_1_, bf16[4096,1024]{1,0:T(8,128)(2,1)S(1)} %bitcast.9, f32[1024,4096]{1,0:T(8,128)} %get-tuple-element.30.refs_3_), custom_call_target="tpu_custom_call", output_to_operand_aliasing={{0}: (3, {})} | custom-call | flops 4294967296 | bytes 16777216 | tf_op jit(solution)/shard_map/pallas_call | solution.py:218
  85.7 1.6 %collective-permute-start.13 = (f32[2,8,512]{2,1,0:T(8,128)S(1)}, f32[2,8,512]{2,1,0:T(8,128)S(1)}, u32[]{:S(2)}, u32[]{:S(2)}) collective-permute-start(f32[2,8,512]{2,1,0:T(8,128)S(1)} %shard_map.53.refs_0_), channel_id=1, source_target_pairs={{0,1},{1,0},{2,3},{3,2},{4,5},{5,4},{6,7},{7,6},{8,9},{9,8},{10,11... | collective-permute-start | bytes 98312 | tf_op jit(solution)/shard_map/ppermute | solution.py:613
  87.2 2.4 %collective-permute-done.13.refs_1_ = f32[2,8,512]{2,1,0:T(8,128)S(1)} collective-permute-done((f32[2,8,512]{2,1,0:T(8,128)S(1)}, f32[2,8,512]{2,1,0:T(8,128)S(1)}, u32[]{:S(2)}, u32[]{:S(2)}) %collective-permute-start.13) | collective-permute-done | bytes 32800 | tf_op jit(solution)/shard_map/ppermute | solution.py:613
  89.7 1.5 %collective-permute-start.16 = (f32[2,8,512]{2,1,0:T(8,128)S(1)}, f32[2,8,512]{2,1,0:T(8,128)S(1)}, u32[]{:S(2)}, u32[]{:S(2)}) collective-permute-start(f32[2,8,512]{2,1,0:T(8,128)S(1)} %shard_map.54.refs_0_.refs_8_), channel_id=1, source_target_pairs={{0,6},{1,7},{2,4},{3,5},{4,2},{5,3},{6,0},{7,1},{8,14},{9,15},{10,... | collective-permute-start | bytes 98312 | tf_op jit(solution)/shard_map/ppermute | solution.py:613
  91.2 0.6 collective-permute-start.15
  91.9 2.3 %collective-permute-start.14 = (f32[2,8,512]{2,1,0:T(8,128)S(1)}, f32[2,8,512]{2,1,0:T(8,128)S(1)}, u32[]{:S(2)}, u32[]{:S(2)}) collective-permute-start(f32[2,8,512]{2,1,0:T(8,128)S(1)} %shard_map.54.refs_0_.refs_8_), channel_id=1, source_target_pairs={{0,2},{1,3},{2,0},{3,1},{4,6},{5,7},{6,4},{7,5},{8,10},{9,11},{10,... | collective-permute-start | bytes 98312 | tf_op jit(solution)/shard_map/ppermute | solution.py:613
  94.1 1.3 %collective-permute-done.16.refs_3_ = f32[2,8,512]{2,1,0:T(8,128)S(1)} collective-permute-done((f32[2,8,512]{2,1,0:T(8,128)S(1)}, f32[2,8,512]{2,1,0:T(8,128)S(1)}, u32[]{:S(2)}, u32[]{:S(2)}) %collective-permute-start.16) | collective-permute-done | bytes 32800 | tf_op jit(solution)/shard_map/ppermute | solution.py:613
  95.5 0.6 collective-permute-done.15.refs_2_
  96.1 0.3 collective-permute-done.14.refs_1_
  96.4 8.5 %shard_map.55 = (f32[1,1032,256]{2,1,0:T(8,128)S(1)}, f32[1,1032,256]{2,1,0:T(8,128)S(1)}, bf16[1024,4096]{1,0:T(8,128)(2,1)S(1)}, f32[1,1024]{1,0:T(1,128)S(1)}) custom-call(f32[2,8,512]{2,1,0:T(8,128)S(1)} %shard_map.54.refs_0_.refs_8_, f32[2,8,512]{2,1,0:T(8,128)S(1)} %collective-permute-done.14.refs_1_, ...), custom_call_target="tpu_custom_call" | custom-call | flops 4294967296 | bytes 20971520 | tf_op jit(solution)/shard_map/pallas_call | solution.py:429
  105.0 2.4 %shard_map.56 = (f32[1,1032,256]{2,1,0:T(8,128)S(1)}, bf16[1024,4096]{1,0:T(8,128)(2,1)S(1)}) custom-call(bf16[1024,4096]{1,0:T(8,128)(2,1)S(1)} %get-tuple-element.33.kept_ref, f32[1,1024]{1,0:T(1,128)S(1)} %get-tuple-element.34.mass_ref, bf16[4096,1024]{1,0:T(8,128)(2,1)S(1)} %bitcast.9, ...), custom_call_target="tpu_custom_call", output_to_operand_aliasing={{1}: (0, {})} | custom-call | flops 2147483648 | bytes 10485760 | tf_op jit(solution)/shard_map/pallas_call | solution.py:385
  107.3 0.5 collective-permute-start.18
  107.9 0.8 shard_map.57._.refs_3_
  108.7 1.6 %collective-permute-start.19 = (bf16[1040,256]{1,0:T(8,128)(2,1)S(1)}, bf16[1040,256]{1,0:T(8,128)(2,1)S(1)}, u32[]{:S(2)}, u32[]{:S(2)}) collective-permute-start(bf16[1040,256]{1,0:T(8,128)(2,1)S(1)} %bitcast.11), channel_id=1, source_target_pairs={{0,16},{8,24},{16,0},{24,8},{1,17},{9,25},{17,1},{25,9},{2,18},{10... | collective-permute-start | bytes 1597448 | tf_op jit(solution)/shard_map/ppermute | solution.py:600
  110.3 0.6 copy.8
  110.9 2.4 %shard_map.58 = (f32[1,1032,256]{2,1,0:T(8,128)S(1)}, bf16[1024,4096]{1,0:T(8,128)(2,1)S(1)}) custom-call(bf16[1024,4096]{1,0:T(8,128)(2,1)S(1)} %get-tuple-element.36.kept_ref, f32[1,1024]{1,0:T(1,128)S(1)} %get-tuple-element.34.mass_ref, bf16[4096,1024]{1,0:T(8,128)(2,1)S(1)} %bitcast.9, ...), custom_call_target="tpu_custom_call", output_to_operand_aliasing={{1}: (0, {})} | custom-call | flops 2147483648 | bytes 10485760 | tf_op jit(solution)/shard_map/pallas_call | solution.py:385
  113.3 9.5 %collective-permute-done.19.refs_2_ = bf16[1040,256]{1,0:T(8,128)(2,1)S(1)} collective-permute-done((bf16[1040,256]{1,0:T(8,128)(2,1)S(1)}, bf16[1040,256]{1,0:T(8,128)(2,1)S(1)}, u32[]{:S(2)}, u32[]{:S(2)}) %collective-permute-start.19) | collective-permute-done | bytes 532512 | tf_op jit(solution)/shard_map/ppermute | solution.py:600
  122.8 2.0 %shard_map.59 = f32[1024,256]{1,0:T(8,128)} custom-call(f32[1032,256]{1,0:T(8,128)S(1)} %bitcast.14, f32[1032,256]{1,0:T(8,128)S(1)} %bitcast.13, bf16[1040,256]{1,0:T(8,128)(2,1)S(1)} %collective-permute-done.19.refs_2_, bf16[1,1040,256]{2,1,0:T(8,128)(2,1)S(1)} %shard_map.57._.refs_3_), custom_call_target="tpu_custom_call" | custom-call | flops 7864320 | bytes 3670016 | tf_op jit(solution)/shard_map/pallas_call | solution.py:542
  (21 shorter events, 0.7 us)
Async XLA Ops:
  0.6 2.2 %copy-start = (f32[1024,1024]{1,0:T(8,128)S(1)}, f32[1024,1024]{1,0:T(8,128)}, u32[]{:S(2)}) copy-start(f32[1024,1024]{1,0:T(8,128)} %in_ref.1) | copy-start | bytes 12582916
  2.8 2.2 %slice-start = ((s8[8388608]{0:T(1024)(128)(4,1)}), s8[4194304]{0:T(1024)(128)(4,1)S(1)}, s32[]{:S(2)}) async-start(s8[8388608]{0:T(1024)(128)(4,1)} %bitcast.8), calls=%async_computation | async-start | bytes 8388608
  3.1 3.3 %slice-start.1 = ((s8[8388608]{0:T(1024)(128)(4,1)}), s8[4194304]{0:T(1024)(128)(4,1)S(1)}, s32[]{:S(2)}) async-start(s8[8388608]{0:T(1024)(128)(4,1)} %bitcast.8), calls=%async_computation.1 | async-start | bytes 8388608
  20.6 4.9 %collective-permute-start = (f32[2,8,512]{2,1,0:T(8,128)S(1)}, f32[2,8,512]{2,1,0:T(8,128)S(1)}, u32[]{:S(2)}, u32[]{:S(2)}) collective-permute-start(f32[2,8,512]{2,1,0:T(8,128)S(1)} %get-tuple-element.21.refs_0_.refs_4_), channel_id=1, source_target_pairs={{0,1},{1,0},{2,3},{3,2},{4,5},{5,4},{6,7},{7,6},{8,9},{9,8},{10,11... | collective-permute-start | bytes 98312 | tf_op jit(solution)/shard_map/ppermute | solution.py:613
  25.5 6.1 %collective-permute-start.3 = (f32[2,8,512]{2,1,0:T(8,128)S(1)}, f32[2,8,512]{2,1,0:T(8,128)S(1)}, u32[]{:S(2)}, u32[]{:S(2)}) collective-permute-start(f32[2,8,512]{2,1,0:T(8,128)S(1)} %shard_map.44.refs_0_.refs_7_), channel_id=1, source_target_pairs={{0,6},{1,7},{2,4},{3,5},{4,2},{5,3},{6,0},{7,1},{8,14},{9,15},{10,... | collective-permute-start | bytes 98312 | tf_op jit(solution)/shard_map/ppermute | solution.py:613
  29.7 4.8 %collective-permute-start.2 = (f32[2,8,512]{2,1,0:T(8,128)S(1)}, f32[2,8,512]{2,1,0:T(8,128)S(1)}, u32[]{:S(2)}, u32[]{:S(2)}) collective-permute-start(f32[2,8,512]{2,1,0:T(8,128)S(1)} %shard_map.44.refs_0_.refs_7_), channel_id=1, source_target_pairs={{0,4},{1,5},{2,6},{3,7},{4,0},{5,1},{6,2},{7,3},{8,12},{9,13},{10,... | collective-permute-start | bytes 98312 | tf_op jit(solution)/shard_map/ppermute | solution.py:613
  29.7 4.8 %collective-permute-start.1 = (f32[2,8,512]{2,1,0:T(8,128)S(1)}, f32[2,8,512]{2,1,0:T(8,128)S(1)}, u32[]{:S(2)}, u32[]{:S(2)}) collective-permute-start(f32[2,8,512]{2,1,0:T(8,128)S(1)} %shard_map.44.refs_0_.refs_7_), channel_id=1, source_target_pairs={{0,2},{1,3},{2,0},{3,1},{4,6},{5,7},{6,4},{7,5},{8,10},{9,11},{10,... | collective-permute-start | bytes 98312 | tf_op jit(solution)/shard_map/ppermute | solution.py:613
  41.4 2.8 %collective-permute-start.4 = (f32[1,264,1024]{2,1,0:T(8,128)S(1)}, f32[1,264,1024]{2,1,0:T(8,128)S(1)}, u32[]{:S(2)}, u32[]{:S(2)}) collective-permute-start(f32[1,264,1024]{2,1,0:T(8,128)S(1)} %get-tuple-element.24.after_ref), channel_id=1, source_target_pairs={{0,8},{8,0},{16,24},{24,16},{1,9},{9,1},{17,25},{25,17},{2,10},{10... | collective-permute-start | bytes 3244040 | tf_op jit(solution)/shard_map/ppermute | solution.py:596
  44.9 14.7 %collective-permute-start.9 = (bf16[272,1024]{1,0:T(8,128)(2,1)S(1)}, bf16[272,1024]{1,0:T(8,128)(2,1)S(1)}, u32[]{:S(2)}, u32[]{:S(2)}) collective-permute-start(bf16[272,1024]{1,0:T(8,128)(2,1)S(1)} %bitcast.10), channel_id=1, source_target_pairs={{0,16},{8,24},{16,0},{24,8},{1,17},{9,25},{17,1},{25,9},{2,18},{10... | collective-permute-start | bytes 1671176 | tf_op jit(solution)/shard_map/ppermute | solution.py:600
  50.8 2.8 %collective-permute-start.8 = (f32[72,1024]{1,0:T(8,128)S(1)}, f32[72,1024]{1,0:T(8,128)S(1)}, u32[]{:S(2)}, u32[]{:S(2)}) collective-permute-start(f32[72,1024]{1,0:T(8,128)S(1)} %get-tuple-element.28), channel_id=1, source_target_pairs={{0,8},{8,0},{16,24},{24,16},{1,9},{9,1},{17,25},{25,17},{2,10},{10... | collective-permute-start | bytes 884744 | tf_op jit(solution)/shard_map/ppermute | solution.py:596
  50.9 1.9 %collective-permute-start.5 = (f32[64,1024]{1,0:T(8,128)S(1)}, f32[64,1024]{1,0:T(8,128)S(1)}, u32[]{:S(2)}, u32[]{:S(2)}) collective-permute-start(f32[64,1024]{1,0:T(8,128)S(1)} %get-tuple-element.25), channel_id=1, source_target_pairs={{0,8},{8,0},{16,24},{24,16},{1,9},{9,1},{17,25},{25,17},{2,10},{10... | collective-permute-start | bytes 786440 | tf_op jit(solution)/shard_map/ppermute | solution.py:596
  51.4 1.8 %collective-permute-start.6 = (f32[64,1024]{1,0:T(8,128)S(1)}, f32[64,1024]{1,0:T(8,128)S(1)}, u32[]{:S(2)}, u32[]{:S(2)}) collective-permute-start(f32[64,1024]{1,0:T(8,128)S(1)} %get-tuple-element.26), channel_id=1, source_target_pairs={{0,8},{8,0},{16,24},{24,16},{1,9},{9,1},{17,25},{25,17},{2,10},{10... | collective-permute-start | bytes 786440 | tf_op jit(solution)/shard_map/ppermute | solution.py:596
  51.5 2.1 %collective-permute-start.7 = (f32[64,1024]{1,0:T(8,128)S(1)}, f32[64,1024]{1,0:T(8,128)S(1)}, u32[]{:S(2)}, u32[]{:S(2)}) collective-permute-start(f32[64,1024]{1,0:T(8,128)S(1)} %get-tuple-element.27), channel_id=1, source_target_pairs={{0,8},{8,0},{16,24},{24,16},{1,9},{9,1},{17,25},{25,17},{2,10},{10... | collective-permute-start | bytes 786440 | tf_op jit(solution)/shard_map/ppermute | solution.py:596
  60.5 2.0 %collective-permute-start.10 = (bf16[256,1024]{1,0:T(8,128)(2,1)S(1)}, bf16[256,1024]{1,0:T(8,128)(2,1)S(1)}, u32[]{:S(2)}, u32[]{:S(2)}) collective-permute-start(bf16[256,1024]{1,0:T(8,128)(2,1)S(1)} %shard_map.49.refs_0_), channel_id=1, source_target_pairs={{0,8},{8,0},{16,24},{24,16},{1,9},{9,1},{17,25},{25,17},{2,10},{10... | collective-permute-start | bytes 1572872 | tf_op jit(solution)/shard_map/ppermute | solution.py:596
  60.6 14.3 %collective-permute-start.11 = (bf16[256,1024]{1,0:T(8,128)(2,1)S(1)}, bf16[256,1024]{1,0:T(8,128)(2,1)S(1)}, u32[]{:S(2)}, u32[]{:S(2)}) collective-permute-start(bf16[256,1024]{1,0:T(8,128)(2,1)S(1)} %shard_map.49.refs_0_), channel_id=1, source_target_pairs={{0,16},{8,24},{16,0},{24,8},{1,17},{9,25},{17,1},{25,9},{2,18},{10... | collective-permute-start | bytes 1572872 | tf_op jit(solution)/shard_map/ppermute | solution.py:600
  74.9 1.9 %collective-permute-start.12 = (bf16[256,1024]{1,0:T(8,128)(2,1)S(1)}, bf16[256,1024]{1,0:T(8,128)(2,1)S(1)}, u32[]{:S(2)}, u32[]{:S(2)}) collective-permute-start(bf16[256,1024]{1,0:T(8,128)(2,1)S(1)} %shard_map.51.refs_0_), channel_id=1, source_target_pairs={{0,8},{8,0},{16,24},{24,16},{1,9},{9,1},{17,25},{25,17},{2,10},{10... | collective-permute-start | bytes 1572872 | tf_op jit(solution)/shard_map/ppermute | solution.py:596
  85.7 4.0 %collective-permute-start.13 = (f32[2,8,512]{2,1,0:T(8,128)S(1)}, f32[2,8,512]{2,1,0:T(8,128)S(1)}, u32[]{:S(2)}, u32[]{:S(2)}) collective-permute-start(f32[2,8,512]{2,1,0:T(8,128)S(1)} %shard_map.53.refs_0_), channel_id=1, source_target_pairs={{0,1},{1,0},{2,3},{3,2},{4,5},{5,4},{6,7},{7,6},{8,9},{9,8},{10,11... | collective-permute-start | bytes 98312 | tf_op jit(solution)/shard_map/ppermute | solution.py:613
  89.7 5.8 %collective-permute-start.16 = (f32[2,8,512]{2,1,0:T(8,128)S(1)}, f32[2,8,512]{2,1,0:T(8,128)S(1)}, u32[]{:S(2)}, u32[]{:S(2)}) collective-permute-start(f32[2,8,512]{2,1,0:T(8,128)S(1)} %shard_map.54.refs_0_.refs_8_), channel_id=1, source_target_pairs={{0,6},{1,7},{2,4},{3,5},{4,2},{5,3},{6,0},{7,1},{8,14},{9,15},{10,... | collective-permute-start | bytes 98312 | tf_op jit(solution)/shard_map/ppermute | solution.py:613
  91.2 4.8 %collective-permute-start.15 = (f32[2,8,512]{2,1,0:T(8,128)S(1)}, f32[2,8,512]{2,1,0:T(8,128)S(1)}, u32[]{:S(2)}, u32[]{:S(2)}) collective-permute-start(f32[2,8,512]{2,1,0:T(8,128)S(1)} %shard_map.54.refs_0_.refs_8_), channel_id=1, source_target_pairs={{0,4},{1,5},{2,6},{3,7},{4,0},{5,1},{6,2},{7,3},{8,12},{9,13},{10,... | collective-permute-start | bytes 98312 | tf_op jit(solution)/shard_map/ppermute | solution.py:613
  91.9 4.5 %collective-permute-start.14 = (f32[2,8,512]{2,1,0:T(8,128)S(1)}, f32[2,8,512]{2,1,0:T(8,128)S(1)}, u32[]{:S(2)}, u32[]{:S(2)}) collective-permute-start(f32[2,8,512]{2,1,0:T(8,128)S(1)} %shard_map.54.refs_0_.refs_8_), channel_id=1, source_target_pairs={{0,2},{1,3},{2,0},{3,1},{4,6},{5,7},{6,4},{7,5},{8,10},{9,11},{10,... | collective-permute-start | bytes 98312 | tf_op jit(solution)/shard_map/ppermute | solution.py:613
  104.9 3.0 %collective-permute-start.17 = (f32[1,1032,256]{2,1,0:T(8,128)S(1)}, f32[1,1032,256]{2,1,0:T(8,128)S(1)}, u32[]{:S(2)}, u32[]{:S(2)}) collective-permute-start(f32[1,1032,256]{2,1,0:T(8,128)S(1)} %get-tuple-element.35._), channel_id=1, source_target_pairs={{0,8},{8,0},{16,24},{24,16},{1,9},{9,1},{17,25},{25,17},{2,10},{10... | collective-permute-start | bytes 3170312 | tf_op jit(solution)/shard_map/ppermute | solution.py:596
  107.3 5.9 %collective-permute-start.18 = (f32[1,1032,256]{2,1,0:T(8,128)S(1)}, f32[1,1032,256]{2,1,0:T(8,128)S(1)}, u32[]{:S(2)}, u32[]{:S(2)}) collective-permute-start(f32[1,1032,256]{2,1,0:T(8,128)S(1)} %get-tuple-element.38.after_ref), channel_id=1, source_target_pairs={{0,8},{8,0},{16,24},{24,16},{1,9},{9,1},{17,25},{25,17},{2,10},{10... | collective-permute-start | bytes 3170312 | tf_op jit(solution)/shard_map/ppermute | solution.py:596
  108.7 14.1 %collective-permute-start.19 = (bf16[1040,256]{1,0:T(8,128)(2,1)S(1)}, bf16[1040,256]{1,0:T(8,128)(2,1)S(1)}, u32[]{:S(2)}, u32[]{:S(2)}) collective-permute-start(bf16[1040,256]{1,0:T(8,128)(2,1)S(1)} %bitcast.11), channel_id=1, source_target_pairs={{0,16},{8,24},{16,0},{24,8},{1,17},{9,25},{17,1},{25,9},{2,18},{10... | collective-permute-start | bytes 1597448 | tf_op jit(solution)/shard_map/ppermute | solution.py:600
